TPU v7x, 256 devices: a whole 4x4x8 slice. The times are simulated.
256 devices in a mesh: depth: 4 (over y), seg: 32 (over x, z), tp: 2 (over core).
Axes of the slice: x: 4, y: 4, z: 8, core: 2. Of those that a mesh axis runs over, the one named last changes fastest.
Arguments:
- queries: bfloat16 [16384, 8192], P(('depth', 'seg'), 'tp'), may hold values from -64 to 64
- key_states: bfloat16 [16384, 1024], P(('depth', 'seg'), 'tp'), may hold values from -6 to 6
- value_states: bfloat16 [16384, 1024], P(('depth', 'seg'), 'tp'), may hold values from -6 to 6
- grad_output: bfloat16 [16384, 8192], P(('depth', 'seg'), 'tp'), may hold values from -6 to 6
- parents: int32 [3, 32], replicated, may hold values from 0 to 31
- lengths: int32 [4, 32], replicated, may hold values from 1 to 128, 3072 in all within a row
Outputs:
- grad_queries: bfloat16 [16384, 8192], P(('depth', 'seg'), 'tp')
- grad_keys: bfloat16 [16384, 1024], P(('depth', 'seg'), 'tp')
- grad_values: bfloat16 [16384, 1024], P(('depth', 'seg'), 'tp')
Inputs may be any that keep to these rules, and one draw needn't show every extreme that they name: parents[l, j] is the segment of level l that is the parent of segment j of level l + 1. lengths[l, s] is the number of live tokens of segment s of level l, the live ones first; in every level some segment has all 128.
All inputs are finite; a program needn't handle non-finite values.
Results may differ from a plain program's by a relative error of at most 0.011.
Values may be sent and summed in bfloat16 or wider, within the bound.
No kernel may reach another device: no remote copies, remote signals or barrier semaphores. Data moves between devices by JAX's collectives and lax.ppermute only.
A program may use at most 64 MiB of HBM per device.

v0:
```python
import jax
import jax.numpy as jnp
from jax import lax
from jax.sharding import PartitionSpec as P

HD = 128


def passed_along(block, axis, distance):
    devices = range(lax.axis_size(axis))
    route = [(i - distance, i) for i in devices if i - distance in devices]
    return lax.ppermute(block, axis, route)


def lookup(table_row, index):
    slots = jnp.arange(table_row.shape[0], dtype=jnp.int32)
    picked = jnp.where(index[:, None] == slots[None, :], table_row[None, :], 0)
    return jnp.sum(picked, axis=1)


def ancestor_table(parents, levels):
    segments = parents.shape[1]
    anchor = jnp.arange(segments, dtype=jnp.int32)
    layers = []
    for depth_level in range(levels):
        column = [jnp.zeros((segments,), jnp.int32) for other in range(levels)]
        current = anchor
        column[depth_level] = current
        for upper_level in range(depth_level - 1, -1, -1):
            current = lookup(parents[upper_level], current)
            column[upper_level] = current
        layers.append(jnp.stack(column))
    return jnp.stack(layers)


def attention_grad(queries, grad_output, key_states, value_states, allowed, live_rows):
    row_count = queries.shape[0]
    group_count = key_states.shape[1] // HD
    repeat_count = queries.shape[1] // key_states.shape[1]
    factor = HD ** (-0.5)
    grad_live = jnp.where(live_rows[:, None], grad_output, jnp.zeros_like(grad_output))
    query_parts, key_parts, value_parts = ([], [], [])
    for group_index in range(group_count):
        low = group_index * repeat_count * HD
        high = low + repeat_count * HD
        query_block = queries[:, low:high].reshape(row_count, repeat_count, HD)
        grad_block = grad_live[:, low:high].reshape(row_count, repeat_count, HD)
        key_block = key_states[:, group_index * HD : (group_index + 1) * HD]
        value_block = value_states[:, group_index * HD : (group_index + 1) * HD]
        scores = (
            jnp.einsum("reh,lh->erl", query_block, key_block, preferred_element_type=jnp.float32)
            * factor
        )
        scores = jnp.where(allowed[None], scores, -jnp.inf)
        highest = jnp.max(scores, axis=2, keepdims=True)
        weights = jnp.exp(scores - highest)
        softmax_weights = weights / jnp.sum(weights, axis=2, keepdims=True)
        probs_low = softmax_weights.astype(jnp.bfloat16)
        attended = jnp.einsum(
            "erl,lh->reh", probs_low, value_block, preferred_element_type=jnp.float32
        )
        correction = jnp.transpose(jnp.sum(grad_block.astype(jnp.float32) * attended, axis=2))
        grad_probs = jnp.einsum(
            "reh,lh->erl", grad_block, value_block, preferred_element_type=jnp.float32
        )
        grad_scores = (softmax_weights * (grad_probs - correction[:, :, None]) * factor).astype(
            jnp.bfloat16
        )
        query_parts.append(
            jnp.einsum(
                "erl,lh->reh", grad_scores, key_block, preferred_element_type=jnp.float32
            ).reshape(row_count, repeat_count * HD)
        )
        key_parts.append(
            jnp.einsum("erl,reh->lh", grad_scores, query_block, preferred_element_type=jnp.float32)
        )
        value_parts.append(
            jnp.einsum("erl,reh->lh", probs_low, grad_block, preferred_element_type=jnp.float32)
        )
    return (
        jnp.concatenate(query_parts, axis=1),
        jnp.concatenate(key_parts, axis=1),
        jnp.concatenate(value_parts, axis=1),
    )


def per_device(queries, key_states, value_states, grad_output, parents, lengths):
    levels = lax.axis_size("depth")
    segments = lax.axis_size("seg")
    level_here = lax.axis_index("depth")
    seg_here = lax.axis_index("seg")
    row_count = queries.shape[0]
    piece_rows = row_count // segments
    feature_width = key_states.shape[1]
    table = ancestor_table(parents, levels)
    level_ids = jnp.arange(levels, dtype=jnp.int32)
    segment_ids = jnp.arange(segments, dtype=jnp.int32)
    positions = jnp.arange(row_count, dtype=jnp.int32)
    chain_here = lax.dynamic_index_in_dim(table, level_here, 0, keepdims=False)
    ancestors_here = lax.dynamic_index_in_dim(chain_here, seg_here, 1, keepdims=False)
    block_lengths = jnp.sum(
        jnp.where(ancestors_here[:, None] == segment_ids[None, :], lengths, 0), axis=1
    )
    own_length = lax.dynamic_index_in_dim(block_lengths, level_here, 0, keepdims=False)
    source_column = lax.dynamic_index_in_dim(table, level_here, 1, keepdims=False)
    deeper = level_ids > level_here
    spread_keys, spread_values = (
        lax.all_to_all(
            key_states.reshape(segments, piece_rows, feature_width),
            "seg",
            split_axis=0,
            concat_axis=0,
            tiled=True,
        ),
        lax.all_to_all(
            value_states.reshape(segments, piece_rows, feature_width),
            "seg",
            split_axis=0,
            concat_axis=0,
            tiled=True,
        ),
    )
    selector = (
        (source_column[:, :, None] == segment_ids[None, None, :]) & deeper[:, None, None]
    ).astype(jnp.bfloat16)
    routed_keys = jnp.einsum(
        "dtj,jpf->dtpf", selector, spread_keys, preferred_element_type=jnp.float32
    ).astype(jnp.bfloat16)
    routed_values = jnp.einsum(
        "dtj,jpf->dtpf", selector, spread_values, preferred_element_type=jnp.float32
    ).astype(jnp.bfloat16)
    arrived_keys, arrived_values = (
        lax.all_to_all(
            lax.all_to_all(routed_keys, "depth", split_axis=0, concat_axis=0, tiled=True),
            "seg",
            split_axis=1,
            concat_axis=1,
            tiled=True,
        ),
        lax.all_to_all(
            lax.all_to_all(routed_values, "depth", split_axis=0, concat_axis=0, tiled=True),
            "seg",
            split_axis=1,
            concat_axis=1,
            tiled=True,
        ),
    )
    own_slot = (level_ids == level_here)[:, None, None]
    key_list = jnp.where(
        own_slot, key_states[None], arrived_keys.reshape(levels, row_count, feature_width)
    )
    value_list = jnp.where(
        own_slot, value_states[None], arrived_values.reshape(levels, row_count, feature_width)
    )
    key_list = key_list.reshape(levels * row_count, feature_width)
    value_list = value_list.reshape(levels * row_count, feature_width)
    below = (level_ids < level_here)[None, :, None] & (
        positions[None, None, :] < block_lengths[None, :, None]
    )
    own_part = (
        (level_ids == level_here)[None, :, None]
        & (positions[None, None, :] <= positions[:, None, None])
        & (positions[None, None, :] < own_length)
    )
    allowed = (below | own_part).reshape(row_count, levels * row_count)
    live_rows = positions < own_length
    grad_q, grad_k, grad_v = attention_grad(
        queries, grad_output, key_list, value_list, allowed, live_rows
    )
    grad_k = grad_k.reshape(levels, row_count, feature_width)
    grad_v = grad_v.reshape(levels, row_count, feature_width)
    own_keys = lax.dynamic_index_in_dim(grad_k, level_here, 0, keepdims=False)
    own_values = lax.dynamic_index_in_dim(grad_v, level_here, 0, keepdims=False)
    ancestor_slot = (level_ids < level_here)[:, None, None]
    sent_keys = jnp.where(ancestor_slot, grad_k, 0.0).astype(jnp.bfloat16)
    sent_values = jnp.where(ancestor_slot, grad_v, 0.0).astype(jnp.bfloat16)
    held_keys, held_values = lax.optimization_barrier((sent_keys, sent_values))
    carried_keys = held_keys.astype(jnp.float32)
    carried_values = held_values.astype(jnp.float32)
    for sender in range(levels - 1, 0, -1):
        active = (level_here == sender).astype(jnp.float32)
        outgoing_keys = (carried_keys[:sender] * active).reshape(
            sender, segments, piece_rows, feature_width
        )
        outgoing_values = (carried_values[:sender] * active).reshape(
            sender, segments, piece_rows, feature_width
        )
        mixed_keys, mixed_values = (
            lax.all_to_all(
                outgoing_keys.astype(jnp.bfloat16), "seg", split_axis=1, concat_axis=1, tiled=True
            ).astype(outgoing_keys.dtype),
            lax.all_to_all(
                outgoing_values.astype(jnp.bfloat16), "seg", split_axis=1, concat_axis=1, tiled=True
            ).astype(outgoing_values.dtype),
        )
        parent_map = (parents[sender - 1][None, :] == segment_ids[:, None]).astype(jnp.float32)
        summed_keys = jnp.einsum(
            "gj,ajpf->agpf", parent_map, mixed_keys, precision=lax.Precision.HIGHEST
        )
        summed_values = jnp.einsum(
            "gj,ajpf->agpf", parent_map, mixed_values, precision=lax.Precision.HIGHEST
        )
        back_keys, back_values = (
            lax.all_to_all(
                summed_keys.astype(jnp.bfloat16), "seg", split_axis=1, concat_axis=1, tiled=True
            ).astype(summed_keys.dtype),
            lax.all_to_all(
                summed_values.astype(jnp.bfloat16), "seg", split_axis=1, concat_axis=1, tiled=True
            ).astype(summed_values.dtype),
        )
        lifted_keys, lifted_values = (
            passed_along(
                back_keys.reshape(sender, row_count, feature_width).astype(jnp.bfloat16),
                "depth",
                -1,
            ).astype(jnp.float32),
            passed_along(
                back_values.reshape(sender, row_count, feature_width).astype(jnp.bfloat16),
                "depth",
                -1,
            ).astype(jnp.float32),
        )
        carried_keys = carried_keys.at[:sender].add(lifted_keys)
        carried_values = carried_values.at[:sender].add(lifted_values)
    extra_keys = lax.dynamic_index_in_dim(carried_keys, level_here, 0, keepdims=False)
    extra_values = lax.dynamic_index_in_dim(carried_values, level_here, 0, keepdims=False)
    return (
        grad_q.astype(jnp.bfloat16),
        (own_keys + extra_keys).astype(jnp.bfloat16),
        (own_values + extra_values).astype(jnp.bfloat16),
    )


def solution(mesh):
    placed = (
        P(("depth", "seg"), "tp"),
        P(("depth", "seg"), "tp"),
        P(("depth", "seg"), "tp"),
        P(("depth", "seg"), "tp"),
        P(),
        P(),
    )
    return jax.shard_map(
        per_device,
        mesh=mesh,
        in_specs=placed,
        out_specs=(P(("depth", "seg"), "tp"), P(("depth", "seg"), "tp"), P(("depth", "seg"), "tp")),
        check_vma=False,
    )
```

profile of v0, /device:TPU:32, one launch (start us, length us, event | category | flops | bytes accessed | tf_op | source)
XLA Modules:
  0.0 366.6 jit_solution(3445118930237621840)
XLA Ops:
  2.2 11.2 %all-to-all-start.3 = ((bf16[32,4,512]{2,1,0:T(4,128)(2,1)}), bf16[32,4,512]{2,1,0:T(4,128)(2,1)S(1)}, u32[]{:S(2)}, u32[]{:S(2)}) async-start(bf16[32,4,512]{2,1,0:T(4,128)(2,1)} %reshape.476), calls=%async_computation.3 | async-start | bytes 262144 | tf_op jit(solution)/shard_map/all_to_all | solution.py:115
  16.6 6.6 %all-to-all-done.3 = bf16[32,4,512]{2,1,0:T(4,128)(2,1)S(1)} async-done(((bf16[32,4,512]{2,1,0:T(4,128)(2,1)}), bf16[32,4,512]{2,1,0:T(4,128)(2,1)S(1)}, u32[]{:S(2)}, u32[]{:S(2)}) %all-to-all-start.3) | async-done | bytes 131104 | tf_op jit(solution)/shard_map/all_to_all | solution.py:115
  23.2 4.3 %all-to-all-start = ((bf16[32,4,512]{2,1,0:T(4,128)(2,1)}), bf16[32,4,512]{2,1,0:T(4,128)(2,1)S(1)}, u32[]{:S(2)}, u32[]{:S(2)}) async-start(bf16[32,4,512]{2,1,0:T(4,128)(2,1)} %reshape.473), calls=%async_computation | async-start | bytes 262144 | tf_op jit(solution)/shard_map/all_to_all | solution.py:108
  28.6 8.6 %all-to-all-done = bf16[32,4,512]{2,1,0:T(4,128)(2,1)S(1)} async-done(((bf16[32,4,512]{2,1,0:T(4,128)(2,1)}), bf16[32,4,512]{2,1,0:T(4,128)(2,1)S(1)}, u32[]{:S(2)}, u32[]{:S(2)}) %all-to-all-start) | async-done | bytes 131104 | tf_op jit(solution)/shard_map/all_to_all | solution.py:108
  37.2 4.5 %all-to-all-start.4 = ((bf16[4,32,4,512]{3,1,2,0:T(8,128)(2,1)}), bf16[4,32,4,512]{3,1,2,0:T(8,128)(2,1)S(1)}, u32[]{:S(2)}, u32[]{:S(2)}) async-start(bf16[4,32,4,512]{3,1,2,0:T(8,128)(2,1)} %convolution_convert_fusion), calls=%async_computation.4 | async-start | bytes 1048576 | tf_op jit(solution)/shard_map/all_to_all | solution.py:141
  42.8 6.9 %all-to-all-done.4 = bf16[4,32,4,512]{3,1,2,0:T(8,128)(2,1)S(1)} async-done(((bf16[4,32,4,512]{3,1,2,0:T(8,128)(2,1)}), bf16[4,32,4,512]{3,1,2,0:T(8,128)(2,1)S(1)}, u32[]{:S(2)}, u32[]{:S(2)}) %all-to-all-start.4) | async-done | bytes 524320 | tf_op jit(solution)/shard_map/all_to_all | solution.py:141
  49.8 3.5 all-to-all-start.1
  55.8 5.5 %all-to-all-done.1 = bf16[4,32,4,512]{3,1,2,0:T(8,128)(2,1)S(1)} async-done(((bf16[4,32,4,512]{3,1,2,0:T(8,128)(2,1)}), bf16[4,32,4,512]{3,1,2,0:T(8,128)(2,1)S(1)}, u32[]{:S(2)}, u32[]{:S(2)}) %all-to-all-start.1) | async-done | bytes 524320 | tf_op jit(solution)/shard_map/all_to_all | solution.py:134
  61.3 4.5 %all-to-all-start.5 = ((bf16[4,32,4,512]{3,2,0,1:T(4,128)(2,1)}), bf16[4,32,4,512]{3,2,0,1:T(4,128)(2,1)S(1)}, u32[]{:S(2)}, u32[]{:S(2)}) async-start(bf16[4,32,4,512]{3,2,0,1:T(4,128)(2,1)} %copy.125), calls=%async_computation.5 | async-start | bytes 1048576 | tf_op jit(solution)/shard_map/all_to_all | solution.py:140
  76.3 3.5 all-to-all-done.5
  79.8 6.4 %all-to-all-start.2 = ((bf16[4,32,4,512]{3,2,0,1:T(4,128)(2,1)}), bf16[4,32,4,512]{3,2,0,1:T(4,128)(2,1)S(1)}, u32[]{:S(2)}, u32[]{:S(2)}) async-start(bf16[4,32,4,512]{3,2,0,1:T(4,128)(2,1)} %copy.120), calls=%async_computation.2 | async-start | bytes 1048576 | tf_op jit(solution)/shard_map/all_to_all | solution.py:133
  86.7 13.3 %all-to-all-done.2 = bf16[4,32,4,512]{3,2,0,1:T(4,128)(2,1)S(1)} async-done(((bf16[4,32,4,512]{3,2,0,1:T(4,128)(2,1)}), bf16[4,32,4,512]{3,2,0,1:T(4,128)(2,1)S(1)}, u32[]{:S(2)}, u32[]{:S(2)}) %all-to-all-start.2) | async-done | bytes 524320 | tf_op jit(solution)/shard_map/all_to_all | solution.py:133
  101.5 3.0 fusion.113
  107.8 2.1 fusion.115
  113.3 2.1 fusion.114
  118.7 2.1 fusion.116
  131.0 2.2 fusion.15
  137.3 1.9 convert_element_type.263
  139.2 1.9 copy.169
  141.1 4.5 %all-to-all-start.6 = ((bf16[3,32,4,512]{3,2,0,1:T(4,128)(2,1)}), bf16[3,32,4,512]{3,2,0,1:T(4,128)(2,1)}, u32[]{:S(2)}, u32[]{:S(2)}) async-start(bf16[3,32,4,512]{3,2,0,1:T(4,128)(2,1)} %copy.169), calls=%async_computation.6 | async-start | bytes 786432 | tf_op jit(solution)/shard_map/all_to_all | solution.py:189
  146.4 1.9 copy.183
  148.4 9.8 %all-to-all-done.6 = bf16[3,32,4,512]{3,2,0,1:T(4,128)(2,1)} async-done(((bf16[3,32,4,512]{3,2,0,1:T(4,128)(2,1)}), bf16[3,32,4,512]{3,2,0,1:T(4,128)(2,1)}, u32[]{:S(2)}, u32[]{:S(2)}) %all-to-all-start.6) | async-done | bytes 393248 | tf_op jit(solution)/shard_map/all_to_all | solution.py:189
  158.2 4.4 %all-to-all-start.12 = ((bf16[3,32,4,512]{3,2,0,1:T(4,128)(2,1)}), bf16[3,32,4,512]{3,2,0,1:T(4,128)(2,1)S(1)}, u32[]{:S(2)}, u32[]{:S(2)}) async-start(bf16[3,32,4,512]{3,2,0,1:T(4,128)(2,1)} %copy.183), calls=%async_computation.12 | async-start | bytes 786432 | tf_op jit(solution)/shard_map/all_to_all | solution.py:192
  164.8 10.1 %all-to-all-done.12 = bf16[3,32,4,512]{3,2,0,1:T(4,128)(2,1)S(1)} async-done(((bf16[3,32,4,512]{3,2,0,1:T(4,128)(2,1)}), bf16[3,32,4,512]{3,2,0,1:T(4,128)(2,1)S(1)}, u32[]{:S(2)}, u32[]{:S(2)}) %all-to-all-start.12) | async-done | bytes 393248 | tf_op jit(solution)/shard_map/all_to_all | solution.py:192
  175.7 4.4 %all-to-all-start.7 = ((bf16[3,32,4,512]{3,2,0,1:T(4,128)(2,1)}), bf16[3,32,4,512]{3,2,0,1:T(4,128)(2,1)S(1)}, u32[]{:S(2)}, u32[]{:S(2)}) async-start(bf16[3,32,4,512]{3,2,0,1:T(4,128)(2,1)} %copy.171), calls=%async_computation.7 | async-start | bytes 786432 | tf_op jit(solution)/shard_map/all_to_all | solution.py:204
  182.5 10.0 %all-to-all-done.7 = bf16[3,32,4,512]{3,2,0,1:T(4,128)(2,1)S(1)} async-done(((bf16[3,32,4,512]{3,2,0,1:T(4,128)(2,1)}), bf16[3,32,4,512]{3,2,0,1:T(4,128)(2,1)S(1)}, u32[]{:S(2)}, u32[]{:S(2)}) %all-to-all-start.7) | async-done | bytes 393248 | tf_op jit(solution)/shard_map/all_to_all | solution.py:204
  193.2 4.6 %all-to-all-start.13 = ((bf16[3,32,4,512]{3,2,0,1:T(4,128)(2,1)}), bf16[3,32,4,512]{3,2,0,1:T(4,128)(2,1)S(1)}, u32[]{:S(2)}, u32[]{:S(2)}) async-start(bf16[3,32,4,512]{3,2,0,1:T(4,128)(2,1)} %copy.185), calls=%async_computation.13 | async-start | bytes 786432 | tf_op jit(solution)/shard_map/all_to_all | solution.py:207
  197.8 1.9 copy.172
  202.9 7.3 %all-to-all-done.13 = bf16[3,32,4,512]{3,2,0,1:T(4,128)(2,1)S(1)} async-done(((bf16[3,32,4,512]{3,2,0,1:T(4,128)(2,1)}), bf16[3,32,4,512]{3,2,0,1:T(4,128)(2,1)S(1)}, u32[]{:S(2)}, u32[]{:S(2)}) %all-to-all-start.13) | async-done | bytes 393248 | tf_op jit(solution)/shard_map/all_to_all | solution.py:207
  217.5 7.1 %all-to-all-start.8 = ((bf16[2,32,4,512]{3,2,0,1:T(4,128)(2,1)}), bf16[2,32,4,512]{3,2,0,1:T(4,128)(2,1)S(1)}, u32[]{:S(2)}, u32[]{:S(2)}) async-start(bf16[2,32,4,512]{3,2,0,1:T(4,128)(2,1)} %copy.174), calls=%async_computation.8 | async-start | bytes 524288 | tf_op jit(solution)/shard_map/all_to_all | solution.py:189
  228.0 9.9 %all-to-all-done.8 = bf16[2,32,4,512]{3,2,0,1:T(4,128)(2,1)S(1)} async-done(((bf16[2,32,4,512]{3,2,0,1:T(4,128)(2,1)}), bf16[2,32,4,512]{3,2,0,1:T(4,128)(2,1)S(1)}, u32[]{:S(2)}, u32[]{:S(2)}) %all-to-all-start.8) | async-done | bytes 262176 | tf_op jit(solution)/shard_map/all_to_all | solution.py:189
  238.0 4.9 %all-to-all-start.14 = ((bf16[2,32,4,512]{3,2,0,1:T(4,128)(2,1)}), bf16[2,32,4,512]{3,2,0,1:T(4,128)(2,1)}, u32[]{:S(2)}, u32[]{:S(2)}) async-start(bf16[2,32,4,512]{3,2,0,1:T(4,128)(2,1)} %copy.188), calls=%async_computation.14 | async-start | bytes 524288 | tf_op jit(solution)/shard_map/all_to_all | solution.py:192
  244.0 11.5 %all-to-all-done.14 = bf16[2,32,4,512]{3,2,0,1:T(4,128)(2,1)} async-done(((bf16[2,32,4,512]{3,2,0,1:T(4,128)(2,1)}), bf16[2,32,4,512]{3,2,0,1:T(4,128)(2,1)}, u32[]{:S(2)}, u32[]{:S(2)}) %all-to-all-start.14) | async-done | bytes 262176 | tf_op jit(solution)/shard_map/all_to_all | solution.py:192
  255.5 4.6 %all-to-all-start.9 = ((bf16[2,32,4,512]{3,2,0,1:T(4,128)(2,1)}), bf16[2,32,4,512]{3,2,0,1:T(4,128)(2,1)S(1)}, u32[]{:S(2)}, u32[]{:S(2)}) async-start(bf16[2,32,4,512]{3,2,0,1:T(4,128)(2,1)} %copy.176), calls=%async_computation.9 | async-start | bytes 524288 | tf_op jit(solution)/shard_map/all_to_all | solution.py:204
  262.2 10.2 %all-to-all-done.9 = bf16[2,32,4,512]{3,2,0,1:T(4,128)(2,1)S(1)} async-done(((bf16[2,32,4,512]{3,2,0,1:T(4,128)(2,1)}), bf16[2,32,4,512]{3,2,0,1:T(4,128)(2,1)S(1)}, u32[]{:S(2)}, u32[]{:S(2)}) %all-to-all-start.9) | async-done | bytes 262176 | tf_op jit(solution)/shard_map/all_to_all | solution.py:204
  273.1 4.6 %all-to-all-start.15 = ((bf16[2,32,4,512]{3,2,0,1:T(4,128)(2,1)}), bf16[2,32,4,512]{3,2,0,1:T(4,128)(2,1)S(1)}, u32[]{:S(2)}, u32[]{:S(2)}) async-start(bf16[2,32,4,512]{3,2,0,1:T(4,128)(2,1)} %copy.190), calls=%async_computation.15 | async-start | bytes 524288 | tf_op jit(solution)/shard_map/all_to_all | solution.py:207
  280.8 2.3 convolution_convert_fusion.6
  285.0 2.3 convolution_convert_fusion.8
  294.2 9.8 %all-to-all-start.10 = ((bf16[1,32,4,512]{3,2,0,1:T(4,128)(2,1)}), bf16[1,32,4,512]{3,2,0,1:T(4,128)(2,1)S(1)}, u32[]{:S(2)}, u32[]{:S(2)}) async-start(bf16[1,32,4,512]{3,2,0,1:T(4,128)(2,1)} %bitcast.92), calls=%async_computation.10 | async-start | bytes 262144 | tf_op jit(solution)/shard_map/all_to_all | solution.py:189
  306.7 6.9 %all-to-all-done.10 = bf16[1,32,4,512]{3,2,0,1:T(4,128)(2,1)S(1)} async-done(((bf16[1,32,4,512]{3,2,0,1:T(4,128)(2,1)}), bf16[1,32,4,512]{3,2,0,1:T(4,128)(2,1)S(1)}, u32[]{:S(2)}, u32[]{:S(2)}) %all-to-all-start.10) | async-done | bytes 131104 | tf_op jit(solution)/shard_map/all_to_all | solution.py:189
  313.6 5.0 %all-to-all-start.16 = ((bf16[1,32,4,512]{3,2,0,1:T(4,128)(2,1)}), bf16[1,32,4,512]{3,2,0,1:T(4,128)(2,1)}, u32[]{:S(2)}, u32[]{:S(2)}) async-start(bf16[1,32,4,512]{3,2,0,1:T(4,128)(2,1)} %bitcast.104), calls=%async_computation.16 | async-start | bytes 262144 | tf_op jit(solution)/shard_map/all_to_all | solution.py:192
  322.1 6.4 %all-to-all-done.16 = bf16[1,32,4,512]{3,2,0,1:T(4,128)(2,1)} async-done(((bf16[1,32,4,512]{3,2,0,1:T(4,128)(2,1)}), bf16[1,32,4,512]{3,2,0,1:T(4,128)(2,1)}, u32[]{:S(2)}, u32[]{:S(2)}) %all-to-all-start.16) | async-done | bytes 131104 | tf_op jit(solution)/shard_map/all_to_all | solution.py:192
  328.5 4.4 %all-to-all-start.11 = ((bf16[1,32,4,512]{3,2,0,1:T(4,128)(2,1)}), bf16[1,32,4,512]{3,2,0,1:T(4,128)(2,1)S(1)}, u32[]{:S(2)}, u32[]{:S(2)}) async-start(bf16[1,32,4,512]{3,2,0,1:T(4,128)(2,1)} %copy.181), calls=%async_computation.11 | async-start | bytes 262144 | tf_op jit(solution)/shard_map/all_to_all | solution.py:204
  337.2 5.4 %all-to-all-done.11 = bf16[1,32,4,512]{3,2,0,1:T(4,128)(2,1)S(1)} async-done(((bf16[1,32,4,512]{3,2,0,1:T(4,128)(2,1)}), bf16[1,32,4,512]{3,2,0,1:T(4,128)(2,1)S(1)}, u32[]{:S(2)}, u32[]{:S(2)}) %all-to-all-start.11) | async-done | bytes 131104 | tf_op jit(solution)/shard_map/all_to_all | solution.py:204
  342.6 4.5 %all-to-all-start.17 = ((bf16[1,32,4,512]{3,2,0,1:T(4,128)(2,1)}), bf16[1,32,4,512]{3,2,0,1:T(4,128)(2,1)S(1)}, u32[]{:S(2)}, u32[]{:S(2)}) async-start(bf16[1,32,4,512]{3,2,0,1:T(4,128)(2,1)} %copy.195), calls=%async_computation.17 | async-start | bytes 262144 | tf_op jit(solution)/shard_map/all_to_all | solution.py:207
  349.1 2.2 pad_maximum_fusion
  351.3 5.5 %all-to-all-done.17 = bf16[1,32,4,512]{3,2,0,1:T(4,128)(2,1)S(1)} async-done(((bf16[1,32,4,512]{3,2,0,1:T(4,128)(2,1)}), bf16[1,32,4,512]{3,2,0,1:T(4,128)(2,1)S(1)}, u32[]{:S(2)}, u32[]{:S(2)}) %all-to-all-start.17) | async-done | bytes 131104 | tf_op jit(solution)/shard_map/all_to_all | solution.py:207
  360.8 4.2 %collective-permute-done.5 = bf16[1,128,512]{2,1,0:T(8,128)(2,1)S(1)} collective-permute-done((bf16[1,128,512]{2,1,0:T(8,128)(2,1)S(1)}, bf16[1,128,512]{2,1,0:T(8,128)(2,1)S(1)}, u32[]{:S(2)}, u32[]{:S(2)}) %collective-permute-start.5) | collective-permute-done | bytes 131104 | tf_op jit(solution)/shard_map/ppermute | solution.py:12
  (200 shorter events, 100.4 us)
Async XLA Ops:
  2.2 21.0 %all-to-all-start.3 = ((bf16[32,4,512]{2,1,0:T(4,128)(2,1)}), bf16[32,4,512]{2,1,0:T(4,128)(2,1)S(1)}, u32[]{:S(2)}, u32[]{:S(2)}) async-start(bf16[32,4,512]{2,1,0:T(4,128)(2,1)} %reshape.476), calls=%async_computation.3 | async-start | bytes 262144 | tf_op jit(solution)/shard_map/all_to_all | solution.py:115
  13.4 40.0 %copy-start.31 = (s32[4,32]{1,0:T(4,128)S(1)}, s32[4,32]{1,0:T(4,128)}, u32[]{:S(2)}) copy-start(s32[4,32]{1,0:T(4,128)} %param.23) | copy-start | bytes 1540
  13.4 40.2 %copy-start.15 = (bf16[128,4096]{1,0:T(8,128)(2,1)S(1)}, bf16[128,4096]{1,0:T(8,128)(2,1)}, u32[]{:S(2)}) copy-start(bf16[128,4096]{1,0:T(8,128)(2,1)} %param.18) | copy-start | bytes 3145732
  23.2 14.0 %all-to-all-start = ((bf16[32,4,512]{2,1,0:T(4,128)(2,1)}), bf16[32,4,512]{2,1,0:T(4,128)(2,1)S(1)}, u32[]{:S(2)}, u32[]{:S(2)}) async-start(bf16[32,4,512]{2,1,0:T(4,128)(2,1)} %reshape.473), calls=%async_computation | async-start | bytes 262144 | tf_op jit(solution)/shard_map/all_to_all | solution.py:108
  37.2 12.5 %all-to-all-start.4 = ((bf16[4,32,4,512]{3,1,2,0:T(8,128)(2,1)}), bf16[4,32,4,512]{3,1,2,0:T(8,128)(2,1)S(1)}, u32[]{:S(2)}, u32[]{:S(2)}) async-start(bf16[4,32,4,512]{3,1,2,0:T(8,128)(2,1)} %convolution_convert_fusion), calls=%async_computation.4 | async-start | bytes 1048576 | tf_op jit(solution)/shard_map/all_to_all | solution.py:141
  49.8 11.5 %all-to-all-start.1 = ((bf16[4,32,4,512]{3,1,2,0:T(8,128)(2,1)}), bf16[4,32,4,512]{3,1,2,0:T(8,128)(2,1)S(1)}, u32[]{:S(2)}, u32[]{:S(2)}) async-start(bf16[4,32,4,512]{3,1,2,0:T(8,128)(2,1)} %convolution_convert_fusion.1), calls=%async_computation.1 | async-start | bytes 1048576 | tf_op jit(solution)/shard_map/all_to_all | solution.py:134
  54.6 11.9 %copy-start.16 = (bf16[128,4096]{1,0:T(8,128)(2,1)S(1)}, bf16[128,4096]{1,0:T(8,128)(2,1)}, u32[]{:S(2)}) copy-start(bf16[128,4096]{1,0:T(8,128)(2,1)} %param.21) | copy-start | bytes 3145732
  61.3 18.5 %all-to-all-start.5 = ((bf16[4,32,4,512]{3,2,0,1:T(4,128)(2,1)}), bf16[4,32,4,512]{3,2,0,1:T(4,128)(2,1)S(1)}, u32[]{:S(2)}, u32[]{:S(2)}) async-start(bf16[4,32,4,512]{3,2,0,1:T(4,128)(2,1)} %copy.125), calls=%async_computation.5 | async-start | bytes 1048576 | tf_op jit(solution)/shard_map/all_to_all | solution.py:140
  65.8 8.3 %copy-start.32 = (pred[4]{0:T(512)(128)(4,1)}, pred[4]{0:T(512)(128)(4,1)S(1)}, u32[]{:S(2)}) copy-start(pred[4]{0:T(512)(128)(4,1)S(1)} %iota_compare_fusion.11) | copy-start | bytes 16
  79.8 20.2 %all-to-all-start.2 = ((bf16[4,32,4,512]{3,2,0,1:T(4,128)(2,1)}), bf16[4,32,4,512]{3,2,0,1:T(4,128)(2,1)S(1)}, u32[]{:S(2)}, u32[]{:S(2)}) async-start(bf16[4,32,4,512]{3,2,0,1:T(4,128)(2,1)} %copy.120), calls=%async_computation.2 | async-start | bytes 1048576 | tf_op jit(solution)/shard_map/all_to_all | solution.py:133
  86.4 13.9 %copy-start.29 = (bf16[128,512]{1,0:T(8,128)(2,1)S(1)}, bf16[128,512]{1,0:T(8,128)(2,1)}, u32[]{:S(2)}) copy-start(bf16[128,512]{1,0:T(8,128)(2,1)} %param.20) | copy-start | bytes 393220
  86.7 14.7 %copy-start.22 = (bf16[128,1024]{0,1:T(8,128)(2,1)S(1)}, bf16[128,1024]{0,1:T(8,128)(2,1)}, u32[]{:S(2)}) copy-start(bf16[128,1024]{0,1:T(8,128)(2,1)} %copy.244) | copy-start | bytes 786436
  101.4 17.3 %copy-start.12 = (bf16[512,512]{1,0:T(8,128)(2,1)}, bf16[512,512]{1,0:T(8,128)(2,1)S(1)}, u32[]{:S(2)}) copy-start(bf16[512,512]{1,0:T(8,128)(2,1)S(1)} %get-tuple-element.106) | copy-start | bytes 1572868
  106.2 1.6 copy-start.21
  106.2 1.6 copy-start.30
  111.7 1.6 copy-start.20
  117.2 1.6 copy-start.18
  122.6 1.6 copy-start.9
  124.2 1.9 copy-start.10
  124.7 1.9 copy-start.5
  126.0 1.8 copy-start.11
  126.6 1.8 copy-start.6
  127.9 2.7 copy-start.23
  127.9 2.7 copy-start.24
  127.9 2.7 copy-start.25
  128.4 1.0 copy-start.4
  131.0 3.2 copy-start.19
  131.0 3.6 copy-start.26
  131.0 3.6 copy-start.27
  131.0 3.6 copy-start.28
  141.1 17.1 %all-to-all-start.6 = ((bf16[3,32,4,512]{3,2,0,1:T(4,128)(2,1)}), bf16[3,32,4,512]{3,2,0,1:T(4,128)(2,1)}, u32[]{:S(2)}, u32[]{:S(2)}) async-start(bf16[3,32,4,512]{3,2,0,1:T(4,128)(2,1)} %copy.169), calls=%async_computation.6 | async-start | bytes 786432 | tf_op jit(solution)/shard_map/all_to_all | solution.py:189
  158.2 16.8 %all-to-all-start.12 = ((bf16[3,32,4,512]{3,2,0,1:T(4,128)(2,1)}), bf16[3,32,4,512]{3,2,0,1:T(4,128)(2,1)S(1)}, u32[]{:S(2)}, u32[]{:S(2)}) async-start(bf16[3,32,4,512]{3,2,0,1:T(4,128)(2,1)} %copy.183), calls=%async_computation.12 | async-start | bytes 786432 | tf_op jit(solution)/shard_map/all_to_all | solution.py:192
  175.7 16.8 %all-to-all-start.7 = ((bf16[3,32,4,512]{3,2,0,1:T(4,128)(2,1)}), bf16[3,32,4,512]{3,2,0,1:T(4,128)(2,1)S(1)}, u32[]{:S(2)}, u32[]{:S(2)}) async-start(bf16[3,32,4,512]{3,2,0,1:T(4,128)(2,1)} %copy.171), calls=%async_computation.7 | async-start | bytes 786432 | tf_op jit(solution)/shard_map/all_to_all | solution.py:204
  193.2 16.9 %all-to-all-start.13 = ((bf16[3,32,4,512]{3,2,0,1:T(4,128)(2,1)}), bf16[3,32,4,512]{3,2,0,1:T(4,128)(2,1)S(1)}, u32[]{:S(2)}, u32[]{:S(2)}) async-start(bf16[3,32,4,512]{3,2,0,1:T(4,128)(2,1)} %copy.185), calls=%async_computation.13 | async-start | bytes 786432 | tf_op jit(solution)/shard_map/all_to_all | solution.py:207
  201.6 12.6 %collective-permute-start = (bf16[3,128,512]{2,1,0:T(8,128)(2,1)}, bf16[3,128,512]{2,1,0:T(8,128)(2,1)}, u32[]{:S(2)}, u32[]{:S(2)}) collective-permute-start(bf16[3,128,512]{2,1,0:T(8,128)(2,1)} %convert_element_type.266), channel_id=1, source_target_pairs={{64,0},{128,64},{192,128},{65,1},{129,65},{193,129},{66,2},{130,66... | collective-permute-start | bytes 1179656 | tf_op jit(solution)/shard_map/ppermute | solution.py:12
  212.9 11.8 %collective-permute-start.3 = (bf16[3,128,512]{2,1,0:T(8,128)(2,1)}, bf16[3,128,512]{2,1,0:T(8,128)(2,1)}, u32[]{:S(2)}, u32[]{:S(2)}) collective-permute-start(bf16[3,128,512]{2,1,0:T(8,128)(2,1)} %convert_element_type.290), channel_id=1, source_target_pairs={{64,0},{128,64},{192,128},{65,1},{129,65},{193,129},{66,2},{130,66... | collective-permute-start | bytes 1179656 | tf_op jit(solution)/shard_map/ppermute | solution.py:12
  217.5 20.4 %all-to-all-start.8 = ((bf16[2,32,4,512]{3,2,0,1:T(4,128)(2,1)}), bf16[2,32,4,512]{3,2,0,1:T(4,128)(2,1)S(1)}, u32[]{:S(2)}, u32[]{:S(2)}) async-start(bf16[2,32,4,512]{3,2,0,1:T(4,128)(2,1)} %copy.174), calls=%async_computation.8 | async-start | bytes 524288 | tf_op jit(solution)/shard_map/all_to_all | solution.py:189
  238.0 17.5 %all-to-all-start.14 = ((bf16[2,32,4,512]{3,2,0,1:T(4,128)(2,1)}), bf16[2,32,4,512]{3,2,0,1:T(4,128)(2,1)}, u32[]{:S(2)}, u32[]{:S(2)}) async-start(bf16[2,32,4,512]{3,2,0,1:T(4,128)(2,1)} %copy.188), calls=%async_computation.14 | async-start | bytes 524288 | tf_op jit(solution)/shard_map/all_to_all | solution.py:192
  255.5 16.9 %all-to-all-start.9 = ((bf16[2,32,4,512]{3,2,0,1:T(4,128)(2,1)}), bf16[2,32,4,512]{3,2,0,1:T(4,128)(2,1)S(1)}, u32[]{:S(2)}, u32[]{:S(2)}) async-start(bf16[2,32,4,512]{3,2,0,1:T(4,128)(2,1)} %copy.176), calls=%async_computation.9 | async-start | bytes 524288 | tf_op jit(solution)/shard_map/all_to_all | solution.py:204
  273.1 16.0 %all-to-all-start.15 = ((bf16[2,32,4,512]{3,2,0,1:T(4,128)(2,1)}), bf16[2,32,4,512]{3,2,0,1:T(4,128)(2,1)S(1)}, u32[]{:S(2)}, u32[]{:S(2)}) async-start(bf16[2,32,4,512]{3,2,0,1:T(4,128)(2,1)} %copy.190), calls=%async_computation.15 | async-start | bytes 524288 | tf_op jit(solution)/shard_map/all_to_all | solution.py:207
  279.6 11.8 %collective-permute-start.1 = (bf16[2,128,512]{2,1,0:T(8,128)(2,1)}, bf16[2,128,512]{2,1,0:T(8,128)(2,1)}, u32[]{:S(2)}, u32[]{:S(2)}) collective-permute-start(bf16[2,128,512]{2,1,0:T(8,128)(2,1)} %copy.178), channel_id=1, source_target_pairs={{64,0},{128,64},{192,128},{65,1},{129,65},{193,129},{66,2},{130,66... | collective-permute-start | bytes 786440 | tf_op jit(solution)/shard_map/ppermute | solution.py:12
  290.1 13.9 %collective-permute-start.4 = (bf16[2,128,512]{2,1,0:T(8,128)(2,1)}, bf16[2,128,512]{2,1,0:T(8,128)(2,1)}, u32[]{:S(2)}, u32[]{:S(2)}) collective-permute-start(bf16[2,128,512]{2,1,0:T(8,128)(2,1)} %copy.192), channel_id=1, source_target_pairs={{64,0},{128,64},{192,128},{65,1},{129,65},{193,129},{66,2},{130,66... | collective-permute-start | bytes 786440 | tf_op jit(solution)/shard_map/ppermute | solution.py:12
  294.2 19.5 %all-to-all-start.10 = ((bf16[1,32,4,512]{3,2,0,1:T(4,128)(2,1)}), bf16[1,32,4,512]{3,2,0,1:T(4,128)(2,1)S(1)}, u32[]{:S(2)}, u32[]{:S(2)}) async-start(bf16[1,32,4,512]{3,2,0,1:T(4,128)(2,1)} %bitcast.92), calls=%async_computation.10 | async-start | bytes 262144 | tf_op jit(solution)/shard_map/all_to_all | solution.py:189
  313.6 14.9 %all-to-all-start.16 = ((bf16[1,32,4,512]{3,2,0,1:T(4,128)(2,1)}), bf16[1,32,4,512]{3,2,0,1:T(4,128)(2,1)}, u32[]{:S(2)}, u32[]{:S(2)}) async-start(bf16[1,32,4,512]{3,2,0,1:T(4,128)(2,1)} %bitcast.104), calls=%async_computation.16 | async-start | bytes 262144 | tf_op jit(solution)/shard_map/all_to_all | solution.py:192
  328.5 14.2 %all-to-all-start.11 = ((bf16[1,32,4,512]{3,2,0,1:T(4,128)(2,1)}), bf16[1,32,4,512]{3,2,0,1:T(4,128)(2,1)S(1)}, u32[]{:S(2)}, u32[]{:S(2)}) async-start(bf16[1,32,4,512]{3,2,0,1:T(4,128)(2,1)} %copy.181), calls=%async_computation.11 | async-start | bytes 262144 | tf_op jit(solution)/shard_map/all_to_all | solution.py:204
  342.6 14.2 %all-to-all-start.17 = ((bf16[1,32,4,512]{3,2,0,1:T(4,128)(2,1)}), bf16[1,32,4,512]{3,2,0,1:T(4,128)(2,1)S(1)}, u32[]{:S(2)}, u32[]{:S(2)}) async-start(bf16[1,32,4,512]{3,2,0,1:T(4,128)(2,1)} %copy.195), calls=%async_computation.17 | async-start | bytes 262144 | tf_op jit(solution)/shard_map/all_to_all | solution.py:207
  347.8 10.3 %collective-permute-start.2 = (bf16[1,128,512]{2,1,0:T(8,128)(2,1)}, bf16[1,128,512]{2,1,0:T(8,128)(2,1)S(1)}, u32[]{:S(2)}, u32[]{:S(2)}) collective-permute-start(bf16[1,128,512]{2,1,0:T(8,128)(2,1)} %convert_element_type.281), channel_id=1, source_target_pairs={{64,0},{128,64},{192,128},{65,1},{129,65},{193,129},{66,2},{130,66... | collective-permute-start | bytes 393224 | tf_op jit(solution)/shard_map/ppermute | solution.py:12
  356.8 8.1 %collective-permute-start.5 = (bf16[1,128,512]{2,1,0:T(8,128)(2,1)S(1)}, bf16[1,128,512]{2,1,0:T(8,128)(2,1)S(1)}, u32[]{:S(2)}, u32[]{:S(2)}) collective-permute-start(bf16[1,128,512]{2,1,0:T(8,128)(2,1)S(1)} %convert_element_type.303), channel_id=1, source_target_pairs={{64,0},{128,64},{192,128},{65,1},{129,65},{193,129},{66,2},{130,66... | collective-permute-start | bytes 393224 | tf_op jit(solution)/shard_map/ppermute | solution.py:12
  (10 other events, 8.3 us)
where the time goes:
time: 371 us; the launch traced here: 367 us
  waiting for transfers between devices  142 us (38%)
  starting transfers between devices  105 us (28%)
  local copies, waits for them, and re-layouts  56.8 us (15%)
  matrix products  37.8 us (10%)
  other arithmetic  24 us (6%)
    all_to_all x3, waiting for transfers between devices, per_device(): lax.all_to_all(outgoing_values.astype(jnp.bfloat16), 'seg', split_axis=1,...  28 us
    all_to_all x3, waiting for transfers between devices, per_device(): lax.all_to_all(outgoing_keys.astype(jnp.bfloat16), 'seg', split_axis=1, c...  26.6 us
    all_to_all x3, waiting for transfers between devices, per_device(): lax.all_to_all(summed_keys.astype(jnp.bfloat16), 'seg', split_axis=1, con...  25.7 us
    all_to_all x3, starting transfers between devices, per_device(): lax.all_to_all(outgoing_keys.astype(jnp.bfloat16), 'seg', split_axis=1, c...  21.5 us
    unnamed x73, local copies, waits for them, and re-layouts  16.2 us
    all_to_all x3, starting transfers between devices, per_device(): lax.all_to_all(outgoing_values.astype(jnp.bfloat16), 'seg', split_axis=1,...  14.3 us
    all_to_all x3, starting transfers between devices, per_device(): lax.all_to_all(summed_values.astype(jnp.bfloat16), 'seg', split_axis=1, c...  13.6 us
    all_to_all x3, starting transfers between devices, per_device(): lax.all_to_all(summed_keys.astype(jnp.bfloat16), 'seg', split_axis=1, con...  13.4 us
  transfers between devices with their start and end apart: 24, of which 18 were waited for; matrix products, arithmetic and copies ran while one was open for 19% of the time, Pallas kernels for 0%

commit v1 on v0

v1 whole, which is shorter than its diff:
```python
import functools

import jax
import jax.numpy as jnp
from jax import lax
from jax.experimental import pallas as pl
from jax.experimental.pallas import tpu as pltpu
from jax.sharding import PartitionSpec as P

HD = 128
LEVELS = 4
SEGS = 32
ROWS = 128
HEADS = 4
REPEAT = 8
TILES = 2 * HEADS
UPPER = LEVELS - 1
DEVICES = LEVELS * SEGS
LOG2E = 1.4426950408889634
FACTOR = HD ** (-0.5)
VMEM = pl.BlockSpec(memory_space=pltpu.VMEM)
SMEM = pl.BlockSpec(memory_space=pltpu.SMEM)


def params():
    return pltpu.CompilerParams(vmem_limit_bytes=48 * 1024 * 1024)


def pack_kernel(key_ref, value_ref, out_ref, wide):
    for head in range(HEADS):
        lanes = slice(head * HD, (head + 1) * HD)
        wide[pl.ds(head, ROWS, stride=TILES), :] = key_ref[:, lanes].astype(jnp.float32)
        wide[pl.ds(HEADS + head, ROWS, stride=TILES), :] = value_ref[:, lanes].astype(jnp.float32)
    out_ref[...] = wide[...].reshape(ROWS, TILES, HD).astype(jnp.bfloat16)


def pack(keys, values):
    return pl.pallas_call(
        pack_kernel,
        out_shape=jax.ShapeDtypeStruct((ROWS, TILES, HD), jnp.bfloat16),
        in_specs=[VMEM, VMEM],
        out_specs=VMEM,
        scratch_shapes=[pltpu.VMEM((ROWS * TILES, HD), jnp.float32)],
        compiler_params=params(),
    )(keys, values)


def chains(parents_ref, seg):
    found = []
    for level in range(1, LEVELS):
        current = seg
        for upper in range(level - 1, -1, -1):
            current = parents_ref[upper, current]
            found.append((level, upper, current))
    return found


def select_kernel(parents_ref, held_ref, out_ref):
    out_ref[0:SEGS] = jnp.zeros((SEGS, UPPER, TILES, HD), jnp.bfloat16)
    blank = jnp.zeros((TILES, HD), jnp.bfloat16)

    def step(seg, carry):
        for level, upper, ancestor in chains(parents_ref, seg):
            out_ref[level * SEGS + seg, upper] = held_ref[upper * SEGS + ancestor]
        for level in range(1, UPPER):
            for upper in range(level, UPPER):
                out_ref[level * SEGS + seg, upper] = blank
        return carry

    lax.fori_loop(0, SEGS, step, 0, unroll=8)


def select(parents, held):
    return pl.pallas_call(
        select_kernel,
        out_shape=jax.ShapeDtypeStruct((DEVICES, UPPER, TILES, HD), jnp.bfloat16),
        in_specs=[SMEM, VMEM],
        out_specs=VMEM,
        compiler_params=params(),
    )(parents, held)


def sum_kernel(parents_ref, terms_ref, out_ref, total):
    total[...] = jnp.zeros_like(total)

    def step(seg, carry):
        for level, upper, ancestor in chains(parents_ref, seg):
            total[upper * SEGS + ancestor] += terms_ref[level * SEGS + seg, upper].astype(jnp.float32)
        return carry

    lax.fori_loop(0, SEGS, step, 0, unroll=8)
    out_ref[0 : UPPER * SEGS] = total[...].astype(jnp.bfloat16)
    out_ref[UPPER * SEGS :] = jnp.zeros((SEGS, TILES, HD), jnp.bfloat16)


def sum_terms(parents, terms):
    return pl.pallas_call(
        sum_kernel,
        out_shape=jax.ShapeDtypeStruct((DEVICES, TILES, HD), jnp.bfloat16),
        in_specs=[SMEM, VMEM],
        out_specs=VMEM,
        scratch_shapes=[pltpu.VMEM((UPPER * SEGS, TILES, HD), jnp.float32)],
        compiler_params=params(),
    )(parents, terms)


def dot_last(left, right):
    return lax.dot_general(left, right, (((1,), (1,)), ((), ())), preferred_element_type=jnp.float32)


def dot(left, right):
    return jnp.dot(left, right, preferred_element_type=jnp.float32)


def attention_kernel(
    place_ref, parents_ref, lengths_ref,
    query_ref, grad_ref, key_ref, value_ref, held_ref,
    gquery_ref, own_key_ref, own_value_ref, terms_ref,
    bias, wide, sums,
):
    head = pl.program_id(0)
    level = place_ref[0]
    seg = place_ref[1]
    own_length = lengths_ref[level, seg]

    @pl.when(head == 0)
    def _():
        slots = lax.broadcasted_iota(jnp.int32, (ROWS, ROWS), 0)
        rows = lax.broadcasted_iota(jnp.int32, (ROWS, ROWS), 1)
        never = jnp.full((ROWS, ROWS), -jnp.inf, jnp.float32)
        current = seg
        for upper in range(UPPER - 1, -1, -1):
            below = upper < level
            current = jnp.where(below, parents_ref[upper, current], current)
            live = jnp.where(below, lengths_ref[upper, current], 0)
            bias[upper * ROWS : (upper + 1) * ROWS, :] = jnp.where(slots < live, 0.0, never)
            wide[upper] = held_ref[:, upper].astype(jnp.float32).reshape(ROWS * TILES, HD)
        allowed = (slots <= rows) & (slots < own_length)
        bias[UPPER * ROWS :, :] = jnp.where(allowed, 0.0, never)

    keys = jnp.concatenate(
        [wide[u, pl.ds(head, ROWS, stride=TILES), :].astype(jnp.bfloat16) for u in range(UPPER)] + [key_ref[...]]
    )
    values = jnp.concatenate(
        [wide[u, pl.ds(HEADS + head, ROWS, stride=TILES), :].astype(jnp.bfloat16) for u in range(UPPER)]
        + [value_ref[...]]
    )
    keys_turned = keys.T
    live_rows = lax.broadcasted_iota(jnp.int32, (ROWS, HD), 0) < own_length
    blocked = bias[...]
    key_sum = jnp.zeros((LEVELS * ROWS, HD), jnp.float32)
    value_sum = jnp.zeros((LEVELS * ROWS, HD), jnp.float32)
    for pair in range(REPEAT // 2):
        heads = [slice((2 * pair + i) * HD, (2 * pair + i + 1) * HD) for i in range(2)]
        query = jnp.concatenate([query_ref[:, lanes] for lanes in heads])
        grad = jnp.concatenate(
            [jnp.where(live_rows, grad_ref[:, lanes], jnp.zeros((), jnp.bfloat16)) for lanes in heads]
        )
        scores = dot_last(keys, query) * (FACTOR * LOG2E) + jnp.concatenate([blocked, blocked], axis=1)
        weights = jnp.exp2(scores - jnp.max(scores, axis=0, keepdims=True))
        inverse = 1.0 / jnp.sum(weights, axis=0, keepdims=True)
        probs = weights * inverse
        grad_probs = dot_last(values, grad)
        correction = jnp.sum(probs * grad_probs, axis=0, keepdims=True)
        grad_scores = (probs * ((grad_probs - correction) * FACTOR)).astype(jnp.bfloat16)
        value_sum += dot(probs.astype(jnp.bfloat16), grad)
        key_sum += dot(grad_scores, query)
        turned = dot(keys_turned, grad_scores).astype(jnp.bfloat16)
        for i, lanes in enumerate(heads):
            gquery_ref[:, lanes] = turned[:, i * ROWS : (i + 1) * ROWS].T
    own_key_ref[...] = key_sum[UPPER * ROWS :]
    own_value_ref[...] = value_sum[UPPER * ROWS :]
    for upper in range(UPPER):
        block = slice(upper * ROWS, (upper + 1) * ROWS)
        sums[upper, pl.ds(head, ROWS, stride=TILES), :] = key_sum[block]
        sums[upper, pl.ds(HEADS + head, ROWS, stride=TILES), :] = value_sum[block]

    @pl.when(head == HEADS - 1)
    def _():
        for upper in range(UPPER):
            terms_ref[:, upper] = sums[upper].reshape(ROWS, TILES, HD).astype(jnp.bfloat16)


def attention(place, parents, lengths, queries, grad_output, keys, values, held):
    wide_block = pl.BlockSpec((ROWS, REPEAT * HD), lambda h: (0, h))
    head_block = pl.BlockSpec((ROWS, HD), lambda h: (0, h))
    held_block = pl.BlockSpec((ROWS, UPPER, TILES, HD), lambda h: (0, 0, 0, 0))
    width = HEADS * HD
    return pl.pallas_call(
        attention_kernel,
        grid=(HEADS,),
        out_shape=(
            jax.ShapeDtypeStruct((ROWS, REPEAT * width), jnp.bfloat16),
            jax.ShapeDtypeStruct((ROWS, width), jnp.float32),
            jax.ShapeDtypeStruct((ROWS, width), jnp.float32),
            jax.ShapeDtypeStruct((ROWS, UPPER, TILES, HD), jnp.bfloat16),
        ),
        in_specs=[SMEM, SMEM, SMEM, wide_block, wide_block, head_block, head_block, held_block],
        out_specs=(wide_block, head_block, head_block, held_block),
        scratch_shapes=[
            pltpu.VMEM((LEVELS * ROWS, ROWS), jnp.float32),
            pltpu.VMEM((UPPER, ROWS * TILES, HD), jnp.float32),
            pltpu.VMEM((UPPER, ROWS * TILES, HD), jnp.float32),
        ],
        compiler_params=params(),
    )(place, parents, lengths, queries, grad_output, keys, values, held)


def finish_kernel(extra_ref, own_key_ref, own_value_ref, key_ref, value_ref, wide):
    wide[...] = extra_ref[...].astype(jnp.float32).reshape(ROWS * TILES, HD)
    for head in range(HEADS):
        lanes = slice(head * HD, (head + 1) * HD)
        extra_key = wide[pl.ds(head, ROWS, stride=TILES), :]
        extra_value = wide[pl.ds(HEADS + head, ROWS, stride=TILES), :]
        key_ref[:, lanes] = (own_key_ref[:, lanes] + extra_key).astype(jnp.bfloat16)
        value_ref[:, lanes] = (own_value_ref[:, lanes] + extra_value).astype(jnp.bfloat16)


def finish(extra, own_keys, own_values):
    shape = jax.ShapeDtypeStruct((ROWS, HEADS * HD), jnp.bfloat16)
    return pl.pallas_call(
        finish_kernel,
        out_shape=(shape, shape),
        in_specs=[VMEM] * 3,
        out_specs=(VMEM, VMEM),
        scratch_shapes=[pltpu.VMEM((ROWS * TILES, HD), jnp.float32)],
        compiler_params=params(),
    )(extra, own_keys, own_values)


def exchange(pieces):
    return lax.all_to_all(pieces, ("depth", "seg"), 0, 0, tiled=True)


def per_device(queries, key_states, value_states, grad_output, parents, lengths):
    place = jnp.stack([lax.axis_index("depth"), lax.axis_index("seg")]).astype(jnp.int32)
    held = exchange(pack(key_states, value_states))
    arrived = exchange(select(parents, held))
    grad_q, own_keys, own_values, terms = attention(
        place, parents, lengths, queries, grad_output, key_states, value_states, arrived
    )
    extra = exchange(sum_terms(parents, exchange(terms)))
    grad_k, grad_v = finish(extra, own_keys, own_values)
    return grad_q, grad_k, grad_v


def solution(mesh):
    placed = P(("depth", "seg"), "tp")
    return jax.shard_map(
        per_device,
        mesh=mesh,
        in_specs=(placed, placed, placed, placed, P(), P()),
        out_specs=(placed, placed, placed),
        check_vma=False,
    )
```

time: 371 us -> 129 us (0.35); the launches traced: 367 us -> 129 us
  waiting for transfers between devices: 142 us -> 24.7 us
  starting transfers between devices: 105 us -> 6.77 us
  blocking collectives: 0 us -> 77.8 us
  local copies, waits for them, and re-layouts: 56.8 us -> 1.83 us
  matrix products: 37.8 us -> 0 us
  other arithmetic: 24 us -> 0.08 us
  Pallas kernels: 0 us -> 16.9 us
    all_to_all x18 -> x1, waiting for transfers between devices: 137 us -> 24.7 us  [exchange(): return lax.all_to_all(pieces, ('depth', 'seg'), 0, 0, tiled=True)]
    all_to_all x18 -> x1, starting transfers between devices: 97 us -> 6.77 us  [exchange(): return lax.all_to_all(pieces, ('depth', 'seg'), 0, 0, tiled=True)]
    all_to_all x0 -> x3, blocking collectives: none -> 77.8 us  [exchange(): return lax.all_to_all(pieces, ('depth', 'seg'), 0, 0, tiled=True)]
    dot_general x28 -> x0, matrix products: 28.5 us -> none  [the longest x4 7.95 us: attention_grad(): jnp.einsum('erl,lh->reh', grad_scores, key_block, preferred_element_type=...]
    convert_element_type x22 -> x0, local copies, waits for them, and re-layouts: 21.4 us -> none  [the longest x5 5.52 us: per_device(): outgoing_keys.astype(jnp.bfloat16)]
    pallas_call x0 -> x5, Pallas kernels: none -> 16.9 us  [the longest x1 12.8 us: attention(): pl.pallas_call(attention_kernel, grid=(HEADS,), out_shape=(jax.ShapeDtype...]
    unnamed x73 -> x16, local copies, waits for them, and re-layouts: 16.2 us -> 1.83 us
    convert_element_type x14 -> x0, other arithmetic: 11 us -> none  [the longest x4 7.07 us: attention_grad(): probs_low = softmax_weights.astype(jnp.bfloat16)]
  transfers between devices with their start and end apart: 24 -> 1, of which waited for: 18 -> 1; matrix products, arithmetic and copies ran while one was open for 19% -> 0% of each run, Pallas kernels for 0% -> 0%
where the time goes in v1:
time: 129 us
  blocking collectives  77.8 us (60%)
  waiting for transfers between devices  24.7 us (19%)
  Pallas kernels  16.9 us (13%)
  starting transfers between devices  6.77 us (5%)
  local copies, waits for them, and re-layouts  1.83 us (1%)
    all_to_all x3, blocking collectives, exchange(): return lax.all_to_all(pieces, ('depth', 'seg'), 0, 0, tiled=True)  77.8 us
    all_to_all x1, waiting for transfers between devices, exchange(): return lax.all_to_all(pieces, ('depth', 'seg'), 0, 0, tiled=True)  24.7 us
    pallas_call x1, Pallas kernels, attention(): pl.pallas_call(attention_kernel, grid=(HEADS,), out_shape=(jax.ShapeDtype...  12.8 us
    all_to_all x1, starting transfers between devices, exchange(): return lax.all_to_all(pieces, ('depth', 'seg'), 0, 0, tiled=True)  6.77 us
  transfers between devices with their start and end apart: 1, of which 1 were waited for; matrix products, arithmetic and copies ran while one was open for 0% of the time, Pallas kernels for 0%

profile of v1, /device:TPU:32, one launch (start us, length us, event | category | flops | bytes accessed | tf_op | source)
XLA Modules:
  0.0 128.8 jit_solution(18310165212411720466)
XLA Ops:
  0.6 0.0 copy-start.2
  0.6 0.9 copy-done.2
  1.5 0.0 copy-start.4
  1.5 0.9 copy-done.4
  2.4 0.1 shard_map.85
  2.6 0.0 copy-start.6
  2.6 29.3 %all_to_all.20.held_ref = bf16[128,8,128]{2,1,0:T(8,128)(2,1)S(1)} all-to-all(bf16[128,8,128]{2,1,0:T(8,128)(2,1)S(1)} %shard_map.85), channel_id=1, replica_groups=mesh['depth'=4,'seg'=32,'tp'=2] {'depth','seg'}, dimensions={0} | all-to-all | bytes 524288 | tf_op jit(solution)/shard_map/all_to_all | solution.py:232
  31.9 0.0 copy-done.6
  31.9 0.0 copy-start.1
  31.9 1.8 %shard_map.86 = bf16[128,3,8,128]{3,2,1,0:T(8,128)(2,1)} custom-call(s32[3,32]{1,0:T(4,128)S(1)} %copy-done.6, bf16[128,8,128]{2,1,0:T(8,128)(2,1)S(1)} %all_to_all.20.held_ref), custom_call_target="tpu_custom_call" | custom-call | tf_op jit(solution)/shard_map/pallas_call | solution.py:74
  33.7 0.0 copy-start
  33.7 0.0 copy-start.3
  33.7 0.0 copy-start.5
  33.7 6.8 %all-to-all-start.1 = ((bf16[128,3,8,128]{3,2,1,0:T(8,128)(2,1)}), bf16[128,3,8,128]{3,2,1,0:T(8,128)(2,1)S(1)}, u32[]{:S(2)}, u32[]{:S(2)}) async-start(bf16[128,3,8,128]{3,2,1,0:T(8,128)(2,1)} %shard_map.86), calls=%async_computation.1 | async-start | bytes 1572864 | tf_op jit(solution)/shard_map/all_to_all | solution.py:232
  40.5 0.0 copy-start.7
  40.5 0.1 pad_add_fusion.place_ref
  40.6 24.7 %all-to-all-done.1.held_ref = bf16[128,3,8,128]{3,2,1,0:T(8,128)(2,1)S(1)} async-done(((bf16[128,3,8,128]{3,2,1,0:T(8,128)(2,1)}), bf16[128,3,8,128]{3,2,1,0:T(8,128)(2,1)S(1)}, u32[]{:S(2)}, u32[]{:S(2)}) %all-to-all-start.1) | async-done | bytes 786464 | tf_op jit(solution)/shard_map/all_to_all | solution.py:232
  65.3 0.0 copy-done.1
  65.3 0.0 copy-done
  65.3 0.0 copy-done.3
  65.3 0.0 copy-done.5
  65.3 0.0 copy-done.7
  65.3 12.8 %shard_map.87 = (bf16[128,4096]{1,0:T(8,128)(2,1)}, f32[128,512]{1,0:T(8,128)S(1)}, f32[128,512]{1,0:T(8,128)S(1)}, bf16[128,3,8,128]{3,2,1,0:T(8,128)(2,1)S(1)}) custom-call(s32[2]{0:T(128)S(1)} %pad_add_fusion.place_ref, s32[3,32]{1,0:T(4,128)S(1)} %copy-done.6, s32[4,32]{1,0:T(4,128)S(1)} %copy-done.7, bf16[128,4096]{1,0:T(8,128)(2,1)S(1)} %copy-done, ...), custom_call_target="tpu_custom_call" | custom-call | tf_op jit(solution)/shard_map/pallas_call | solution.py:189
  78.1 29.3 %all_to_all.21.terms_ref = bf16[128,3,8,128]{3,2,1,0:T(8,128)(2,1)S(1)} all-to-all(bf16[128,3,8,128]{3,2,1,0:T(8,128)(2,1)S(1)} %get-tuple-element.10), channel_id=1, replica_groups=mesh['depth'=4,'seg'=32,'tp'=2] {'depth','seg'}, dimensions={0} | all-to-all | bytes 1572864 | tf_op jit(solution)/shard_map/all_to_all | solution.py:232
  107.4 1.3 %shard_map.88 = bf16[128,8,128]{2,1,0:T(8,128)(2,1)S(1)} custom-call(s32[3,32]{1,0:T(4,128)S(1)} %copy-done.6, bf16[128,3,8,128]{3,2,1,0:T(8,128)(2,1)S(1)} %all_to_all.21.terms_ref), custom_call_target="tpu_custom_call" | custom-call | tf_op jit(solution)/shard_map/pallas_call | solution.py:97
  108.7 19.2 %all_to_all.22.extra_ref = bf16[128,8,128]{2,1,0:T(8,128)(2,1)S(1)} all-to-all(bf16[128,8,128]{2,1,0:T(8,128)(2,1)S(1)} %shard_map.88), channel_id=1, replica_groups=mesh['depth'=4,'seg'=32,'tp'=2] {'depth','seg'}, dimensions={0} | all-to-all | bytes 524288 | tf_op jit(solution)/shard_map/all_to_all | solution.py:232
  127.9 0.9 shard_map.89
Async XLA Ops:
  0.6 0.9 copy-start.2
  1.5 0.9 copy-start.4
  2.6 29.3 %copy-start.6 = (s32[3,32]{1,0:T(4,128)S(1)}, s32[3,32]{1,0:T(4,128)}, u32[]{:S(2)}) copy-start(s32[3,32]{1,0:T(4,128)} %parents_ref.5) | copy-start | bytes 1156
  31.9 33.3 %copy-start.1 = (bf16[128,4096]{1,0:T(8,128)(2,1)S(1)}, bf16[128,4096]{1,0:T(8,128)(2,1)}, u32[]{:S(2)}) copy-start(bf16[128,4096]{1,0:T(8,128)(2,1)} %grad_ref.1) | copy-start | bytes 3145732
  33.7 31.6 %copy-start = (bf16[128,4096]{1,0:T(8,128)(2,1)S(1)}, bf16[128,4096]{1,0:T(8,128)(2,1)}, u32[]{:S(2)}) copy-start(bf16[128,4096]{1,0:T(8,128)(2,1)} %query_ref.1) | copy-start | bytes 3145732
  33.7 31.6 %copy-start.3 = (bf16[128,512]{1,0:T(8,128)(2,1)S(1)}, bf16[128,512]{1,0:T(8,128)(2,1)}, u32[]{:S(2)}) copy-start(bf16[128,512]{1,0:T(8,128)(2,1)} %key_ref.3) | copy-start | bytes 393220
  33.7 31.6 %copy-start.5 = (bf16[128,512]{1,0:T(8,128)(2,1)S(1)}, bf16[128,512]{1,0:T(8,128)(2,1)}, u32[]{:S(2)}) copy-start(bf16[128,512]{1,0:T(8,128)(2,1)} %value_ref.3) | copy-start | bytes 393220
  33.7 31.6 %all-to-all-start.1 = ((bf16[128,3,8,128]{3,2,1,0:T(8,128)(2,1)}), bf16[128,3,8,128]{3,2,1,0:T(8,128)(2,1)S(1)}, u32[]{:S(2)}, u32[]{:S(2)}) async-start(bf16[128,3,8,128]{3,2,1,0:T(8,128)(2,1)} %shard_map.86), calls=%async_computation.1 | async-start | bytes 1572864 | tf_op jit(solution)/shard_map/all_to_all | solution.py:232
  40.5 24.8 %copy-start.7 = (s32[4,32]{1,0:T(4,128)S(1)}, s32[4,32]{1,0:T(4,128)}, u32[]{:S(2)}) copy-start(s32[4,32]{1,0:T(4,128)} %lengths_ref.1) | copy-start | bytes 1540

commit v2 on v1

v2 whole, which is shorter than its diff:
```python
import jax
import jax.numpy as jnp
from jax import lax
from jax.experimental import pallas as pl
from jax.experimental.pallas import tpu as pltpu
from jax.sharding import PartitionSpec as P

HD = 128
LEVELS = 4
SEGS = 32
ROWS = 128
HEADS = 4
REPEAT = 8
GROUP = REPEAT * HD
WIDTH = HEADS * HD
TILE = 2 * HEADS
UPPER = LEVELS - 1
DEVICES = LEVELS * SEGS
SLOTS = 6
PIECE = 2 * SLOTS
HALF = HEADS // 2
GUEST_GRAD = HALF * GROUP
GUEST_KEY = 2 * HALF * GROUP
GUEST_VALUE = GUEST_KEY + HALF * HD
BACK_KEY = HALF * GROUP
BACK_VALUE = BACK_KEY + HALF * HD
LOG2E = 1.4426950408889634
FACTOR = HD ** (-0.5)
VMEM = pl.BlockSpec(memory_space=pltpu.VMEM)
SMEM = pl.BlockSpec(memory_space=pltpu.SMEM)

TASKS = {
    0: ((True, 2, (0, 2, 4)), (True, 3, (1, 3, 5))),
    1: ((False, 0, (0,)), (False, 1, (1,)), (False, 2, (2,)), (False, 3, (3,)), (True, 3, (4, 5))),
    2: ((False, 0, (0, 2)), (False, 1, (1, 3)), (False, 2, (4, 5))),
    3: ((False, 0, (0, 2, 4)), (False, 1, (1, 3, 5))),
}
HOST = {0: 3, 1: 2}


def call(kernel, out_shape, in_specs, out_specs, scratch=(), flops=0, moved=0, grid=None):
    extra = {} if grid is None else {"grid": grid}
    return pl.pallas_call(
        kernel,
        out_shape=out_shape,
        in_specs=in_specs,
        out_specs=out_specs,
        scratch_shapes=list(scratch),
        cost_estimate=pl.CostEstimate(flops=flops, bytes_accessed=moved, transcendentals=0),
        compiler_params=pltpu.CompilerParams(vmem_limit_bytes=48 * 1024 * 1024),
        **extra,
    )


def low(*shape):
    return jax.ShapeDtypeStruct(shape, jnp.bfloat16)


def full(*shape):
    return jax.ShapeDtypeStruct(shape, jnp.float32)


def wide_scratch(rows):
    return pltpu.VMEM((rows, HD), jnp.float32)


def pack_kernel(key_ref, value_ref, out_ref, wide):
    for head in range(HEADS):
        lanes = slice(head * HD, (head + 1) * HD)
        wide[pl.ds(2 * head, ROWS, stride=TILE), :] = key_ref[:, lanes].astype(jnp.float32)
        wide[pl.ds(2 * head + 1, ROWS, stride=TILE), :] = value_ref[:, lanes].astype(jnp.float32)
    out_ref[...] = wide[...].astype(jnp.bfloat16)


def pack(keys, values):
    return call(pack_kernel, low(ROWS * TILE, HD), [VMEM, VMEM], VMEM, [wide_scratch(ROWS * TILE)])(keys, values)


def chain(parents_ref, level, seg):
    found = []
    current = seg
    for upper in range(level - 1, -1, -1):
        current = parents_ref[upper, current]
        found.insert(0, current)
    return found


def tile_at(upper, ancestor):
    return pl.ds(pl.multiple_of((upper * SEGS + ancestor) * TILE, TILE), TILE)


def rows_of(level, seg, first, count):
    return pl.ds((level * SEGS + seg) * PIECE + first, count)


def select_kernel(parents_ref, held_ref, out_ref, wide, picked):
    wide[...] = held_ref[...].astype(jnp.float32)

    def step(seg, carry):
        for upper, ancestor in enumerate(chain(parents_ref, 3, seg)):
            tile = wide[tile_at(upper, ancestor), :]
            picked[rows_of(3, seg, 4 * upper, 4), :] = tile[0:4]
            picked[rows_of(0, seg, 4 * upper, 4), :] = tile[4:8]
        first, second = [wide[tile_at(u, a), :] for u, a in enumerate(chain(parents_ref, 2, seg))]
        picked[rows_of(2, seg, 0, 4), :] = first[0:4]
        picked[rows_of(2, seg, 4, 4), :] = second[0:4]
        picked[rows_of(2, seg, 8, 2), :] = first[4:6]
        picked[rows_of(2, seg, 10, 2), :] = second[4:6]
        picked[rows_of(1, seg, 8, 2), :] = first[6:8]
        picked[rows_of(1, seg, 10, 2), :] = second[6:8]
        (only,) = chain(parents_ref, 1, seg)
        picked[rows_of(1, seg, 0, 8), :] = wide[tile_at(0, only), :]
        return carry

    lax.fori_loop(0, SEGS, step, 0, unroll=8)
    out_ref[...] = picked[...].astype(jnp.bfloat16)


def select(parents, held):
    scratch = [wide_scratch(DEVICES * TILE), wide_scratch(DEVICES * PIECE)]
    return call(select_kernel, low(DEVICES * PIECE, HD), [SMEM, VMEM], VMEM, scratch)(parents, held)


def sum_kernel(parents_ref, terms_ref, out_ref, wide, total):
    wide[...] = terms_ref[...].astype(jnp.float32)
    total[...] = jnp.zeros_like(total)

    def rows(level, seg, first, count):
        return wide[rows_of(level, seg, first, count), :]

    def step(seg, carry):
        for upper, ancestor in enumerate(chain(parents_ref, 3, seg)):
            total[tile_at(upper, ancestor), :] += jnp.concatenate(
                [rows(3, seg, 4 * upper, 4), rows(0, seg, 4 * upper, 4)]
            )
        for upper, ancestor in enumerate(chain(parents_ref, 2, seg)):
            total[tile_at(upper, ancestor), :] += jnp.concatenate(
                [rows(2, seg, 4 * upper, 4), rows(2, seg, 8 + 2 * upper, 2), rows(1, seg, 8 + 2 * upper, 2)]
            )
        (only,) = chain(parents_ref, 1, seg)
        total[tile_at(0, only), :] += rows(1, seg, 0, 8)
        return carry

    lax.fori_loop(0, SEGS, step, 0, unroll=8)
    used = UPPER * SEGS * TILE
    out_ref[0:used] = total[...].astype(jnp.bfloat16)
    out_ref[used:] = jnp.zeros((SEGS * TILE, HD), jnp.bfloat16)


def sum_terms(parents, terms):
    scratch = [wide_scratch(DEVICES * PIECE), wide_scratch(UPPER * SEGS * TILE)]
    return call(sum_kernel, low(DEVICES * TILE, HD), [SMEM, VMEM], VMEM, scratch)(parents, terms)


def dot_last(left, right):
    return lax.dot_general(left, right, (((1,), (1,)), ((), ())), preferred_element_type=jnp.float32)


def dot(left, right):
    return jnp.dot(left, right, preferred_element_type=jnp.float32)


def block_mask(lengths):
    slots = lax.broadcasted_iota(jnp.int32, (ROWS, ROWS), 0)
    rows = lax.broadcasted_iota(jnp.int32, (ROWS, ROWS), 1)
    allowed = [slots < length for length in lengths]
    allowed[-1] = allowed[-1] & (slots <= rows)
    return jnp.concatenate([jnp.where(each, 0.0, -jnp.inf).astype(jnp.float32) for each in allowed])


def head_grad(keys, values, blocked, live_rows, query_at, grad_at, store):
    query = jnp.concatenate([query_at(i) for i in range(REPEAT)])
    grad = jnp.concatenate(
        [jnp.where(live_rows, grad_at(i), jnp.zeros((), jnp.bfloat16)) for i in range(REPEAT)]
    )
    scores = dot_last(keys, query) * (FACTOR * LOG2E) + jnp.concatenate([blocked] * REPEAT, axis=1)
    weights = jnp.exp2(scores - jnp.max(scores, axis=0, keepdims=True))
    probs = weights * (1.0 / jnp.sum(weights, axis=0, keepdims=True))
    grad_probs = dot_last(values, grad)
    correction = jnp.sum(probs * grad_probs, axis=0, keepdims=True)
    grad_scores = (probs * ((grad_probs - correction) * FACTOR)).astype(jnp.bfloat16)
    value_sum = dot(probs.astype(jnp.bfloat16), grad)
    key_sum = dot(grad_scores, query)
    turned = dot(keys.T, grad_scores).astype(jnp.bfloat16)
    for i in range(REPEAT):
        store(i, turned[:, i * ROWS : (i + 1) * ROWS].T)
    return key_sum, value_sum


def live(length):
    return lax.broadcasted_iota(jnp.int32, (ROWS, HD), 0) < length


def lanes_at(ref, start, width=HD):
    return ref.at[:, start : start + width]


def root_kernel(place_ref, lengths_ref, query_ref, grad_ref, key_ref, value_ref, gquery_ref, gkey_ref, gvalue_ref):
    @pl.when(place_ref[0] == 0)
    def _():
        length = lengths_ref[0, place_ref[1]]
        blocked = block_mask([length])
        for head in range(HEADS):
            lanes = slice(head * HD, (head + 1) * HD)

            def store(i, block):
                lanes_at(gquery_ref, head * GROUP + i * HD)[...] = block

            gkey_ref[:, lanes], gvalue_ref[:, lanes] = head_grad(
                key_ref[:, lanes],
                value_ref[:, lanes],
                blocked,
                live(length),
                lambda i: lanes_at(query_ref, head * GROUP + i * HD)[...],
                lambda i: lanes_at(grad_ref, head * GROUP + i * HD)[...],
                store,
            )


def root_grad(place, lengths, queries, grad_output, keys, values):
    shapes = (low(ROWS, HEADS * GROUP), full(ROWS, WIDTH), full(ROWS, WIDTH))
    specs = [SMEM, SMEM] + [VMEM] * 4
    return call(root_kernel, shapes, specs, (VMEM,) * 3, flops=10**9, moved=6 * 2**20)(
        place, lengths, queries, grad_output, keys, values
    )


def attention_kernel(
    place_ref, parents_ref, lengths_ref,
    query_ref, grad_ref, key_ref, value_ref, guest_ref, held_ref,
    gquery_ref, gkey_ref, gvalue_ref, back_ref, terms_ref,
    wide, sums,
):
    seg = place_ref[1]
    wide[...] = held_ref[...].astype(jnp.float32)

    def slot_rows(slot, part):
        return pl.ds(2 * slot + part, ROWS, stride=PIECE)

    def run(level_here):
        def setting(level):
            lengths = [lengths_ref[u, a] for u, a in enumerate(chain(parents_ref, level, seg))]
            lengths.append(lengths_ref[level, seg])
            return block_mask(lengths), live(lengths[-1])

        own = setting(level_here) if level_here else None
        hosted = setting(HOST[level_here]) if level_here in HOST else None
        for guest, head, slots in TASKS[level_here]:
            if guest:
                place = head - HALF
                sources = (guest_ref, place * GROUP, guest_ref, GUEST_GRAD + place * GROUP)
                own_key = lanes_at(guest_ref, GUEST_KEY + place * HD)
                own_value = lanes_at(guest_ref, GUEST_VALUE + place * HD)
                target, first = back_ref, place * GROUP
                key_target = lanes_at(back_ref, BACK_KEY + place * HD)
                value_target = lanes_at(back_ref, BACK_VALUE + place * HD)
            else:
                sources = (query_ref, head * GROUP, grad_ref, head * GROUP)
                own_key, own_value = lanes_at(key_ref, head * HD), lanes_at(value_ref, head * HD)
                target, first = gquery_ref, head * GROUP
                key_target, value_target = lanes_at(gkey_ref, head * HD), lanes_at(gvalue_ref, head * HD)
            blocked, live_rows = hosted if guest else own
            keys, values = [
                jnp.concatenate(
                    [wide[slot_rows(slot, part), :].astype(jnp.bfloat16) for slot in slots] + [mine[...]]
                )
                for part, mine in enumerate((own_key, own_value))
            ]

            def store(i, block):
                lanes_at(target, first + i * HD)[...] = block

            key_sum, value_sum = head_grad(
                keys,
                values,
                blocked,
                live_rows,
                lambda i: lanes_at(sources[0], sources[1] + i * HD)[...],
                lambda i: lanes_at(sources[2], sources[3] + i * HD)[...],
                store,
            )
            for index, slot in enumerate(slots):
                block = slice(index * ROWS, (index + 1) * ROWS)
                sums[slot_rows(slot, 0), :] = key_sum[block]
                sums[slot_rows(slot, 1), :] = value_sum[block]
            key_target[...] = key_sum[len(slots) * ROWS :].astype(key_target.dtype)
            value_target[...] = value_sum[len(slots) * ROWS :].astype(value_target.dtype)

    for level in range(LEVELS):
        pl.when(place_ref[0] == level)(lambda level=level: run(level))
    terms_ref[...] = sums[...].astype(jnp.bfloat16)


def attention(place, parents, lengths, queries, grad_output, keys, values, guest, held):
    shapes = (
        low(ROWS, HEADS * GROUP), full(ROWS, WIDTH), full(ROWS, WIDTH),
        low(ROWS, BACK_VALUE + HALF * HD), low(ROWS * PIECE, HD),
    )
    specs = [SMEM] * 3 + [VMEM] * 6
    scratch = [wide_scratch(ROWS * PIECE), wide_scratch(ROWS * PIECE)]
    return call(attention_kernel, shapes, specs, (VMEM,) * 5, scratch, flops=3 * 10**9, moved=10 * 2**20)(
        place, parents, lengths, queries, grad_output, keys, values, guest, held
    )


def join_kernel(place_ref, root_ref, here_ref, back_ref, out_ref):
    level = place_ref[0]
    head = pl.program_id(0)
    away = ((level == 3) & (head >= HALF)) | ((level == 2) & (head == HEADS - 1))

    @pl.when(away)
    def _():
        out_ref[...] = back_ref[...]

    @pl.when(level == 0)
    def _():
        out_ref[...] = root_ref[...]

    @pl.when((level != 0) & jnp.logical_not(away))
    def _():
        out_ref[...] = here_ref[...]


def join(place, root, here, back):
    block = pl.BlockSpec((ROWS, GROUP), lambda h: (0, h))
    late = pl.BlockSpec((ROWS, GROUP), lambda h: (0, jnp.maximum(h - HALF, 0)))
    return call(
        join_kernel, low(ROWS, HEADS * GROUP), [SMEM, block, block, late], block, grid=(HEADS,), moved=4 * 2**20
    )(place, root, here, back)


def finish_kernel(
    place_ref, extra_ref, root_key_ref, root_value_ref, here_key_ref, here_value_ref, back_ref, key_ref, value_ref, wide
):
    level = place_ref[0]
    wide[...] = extra_ref[...].astype(jnp.float32)
    for head in range(HEADS):
        lanes = slice(head * HD, (head + 1) * HD)
        away = ((level == 3) & (head >= HALF)) | ((level == 2) & (head == HEADS - 1))
        parts = (
            (root_key_ref, here_key_ref, BACK_KEY, key_ref),
            (root_value_ref, here_value_ref, BACK_VALUE, value_ref),
        )
        for part, (root_ref, here_ref, start, out_ref) in enumerate(parts):
            own = jnp.where(level == 0, root_ref[:, lanes], here_ref[:, lanes])
            if head >= HALF:
                back = back_ref[:, start + (head - HALF) * HD : start + (head - HALF + 1) * HD]
                own = jnp.where(away, back.astype(jnp.float32), own)
            out_ref[:, lanes] = (own + wide[pl.ds(2 * head + part, ROWS, stride=TILE), :]).astype(jnp.bfloat16)


def finish(place, extra, root_key, root_value, here_key, here_value, back):
    shapes = (low(ROWS, WIDTH), low(ROWS, WIDTH))
    specs = [SMEM] + [VMEM] * 6
    return call(finish_kernel, shapes, specs, (VMEM, VMEM), [wide_scratch(ROWS * TILE)])(
        place, extra, root_key, root_value, here_key, here_value, back
    )


def exchange(pieces, *tile):
    rows = pieces.shape[0]
    swapped = lax.all_to_all(pieces.reshape(DEVICES, *tile, HD), ("depth", "seg"), 0, 0, tiled=True)
    return swapped.reshape(rows, HD)


def per_device(queries, key_states, value_states, grad_output, parents, lengths):
    place = jnp.stack([lax.axis_index("depth"), lax.axis_index("seg")]).astype(jnp.int32)
    held = exchange(pack(key_states, value_states), TILE)
    lent = jnp.concatenate(
        [queries[:, HALF * GROUP :], grad_output[:, HALF * GROUP :], key_states[:, HALF * HD :], value_states[:, HALF * HD :]],
        axis=1,
    )
    guest = lax.ppermute(lent, "depth", [(host, here) for here, host in HOST.items()])
    root_q, root_k, root_v = root_grad(place, lengths, queries, grad_output, key_states, value_states)
    arrived = exchange(select(parents, held), SLOTS // 2, 4)
    here_q, here_k, here_v, back, terms = attention(
        place, parents, lengths, queries, grad_output, key_states, value_states, guest, arrived
    )
    back = lax.ppermute(back, "depth", list(HOST.items()))
    grad_q = join(place, root_q, here_q, back)
    extra = exchange(sum_terms(parents, exchange(terms, SLOTS // 2, 4)), TILE)
    grad_k, grad_v = finish(place, extra, root_k, root_v, here_k, here_v, back)
    return grad_q, grad_k, grad_v


def solution(mesh):
    placed = P(("depth", "seg"), "tp")
    return jax.shard_map(
        per_device,
        mesh=mesh,
        in_specs=(placed, placed, placed, placed, P(), P()),
        out_specs=(placed, placed, placed),
        check_vma=False,
    )
```

time: 129 us -> 118 us (0.915)
  blocking collectives: 77.8 us -> 0 us
  starting transfers between devices: 6.77 us -> 45.7 us
  waiting for transfers between devices: 24.7 us -> 43.5 us
  local copies, waits for them, and re-layouts: 1.83 us -> 8.79 us
    all_to_all x3 -> x0, blocking collectives: 77.8 us -> none  [exchange(): return lax.all_to_all(pieces, ('depth', 'seg'), 0, 0, tiled=True)]
    all_to_all x1 -> x4, starting transfers between devices: 6.77 us -> 39.1 us  [exchange(): lax.all_to_all(pieces.reshape(DEVICES, *tile, HD), ('depth', 'seg'), 0, 0...]
    ppermute x0 -> x2, waiting for transfers between devices: none -> 15.8 us  [the longest x1 15.8 us: per_device(): lax.ppermute(lent, 'depth', [(host, here) for here, host in HOST.items()])]
    ppermute x0 -> x2, starting transfers between devices: none -> 6.57 us  [the longest x1 5.16 us: per_device(): back = lax.ppermute(back, 'depth', list(HOST.items()))]
    unnamed x16 -> x22, local copies, waits for them, and re-layouts: 1.83 us -> 7.54 us
    all_to_all x1 -> x4, waiting for transfers between devices: 24.7 us -> 27.7 us  [exchange(): lax.all_to_all(pieces.reshape(DEVICES, *tile, HD), ('depth', 'seg'), 0, 0...]
    pallas_call x5 -> x7, Pallas kernels: 16.9 us -> 17.9 us  [the longest x1 6.67 us: attention(): call(attention_kernel, shapes, specs, (VMEM,) * 5, scratch, flops=3 * 10...]
  transfers between devices with their start and end apart: 1 -> 6, of which waited for: 1 -> 5; matrix products, arithmetic and copies ran while one was open for 0% -> 1% of each run, Pallas kernels for 0% -> 8%
where the time goes in v2:
time: 118 us
  starting transfers between devices  45.7 us (39%)
  waiting for transfers between devices  43.5 us (37%)
  Pallas kernels  17.9 us (15%)
  local copies, waits for them, and re-layouts  8.79 us (7%)
  other arithmetic  1.18 us (1%)
    all_to_all x4, starting transfers between devices, exchange(): lax.all_to_all(pieces.reshape(DEVICES, *tile, HD), ('depth', 'seg'), 0, 0...  39.1 us
    all_to_all x4, waiting for transfers between devices, exchange(): lax.all_to_all(pieces.reshape(DEVICES, *tile, HD), ('depth', 'seg'), 0, 0...  27.7 us
    ppermute x1, waiting for transfers between devices, per_device(): lax.ppermute(lent, 'depth', [(host, here) for here, host in HOST.items()])  15.8 us
    unnamed x22, local copies, waits for them, and re-layouts  7.54 us
    pallas_call x1, Pallas kernels, attention(): call(attention_kernel, shapes, specs, (VMEM,) * 5, scratch, flops=3 * 10...  6.67 us
    ppermute x1, starting transfers between devices, per_device(): back = lax.ppermute(back, 'depth', list(HOST.items()))  5.16 us
    pallas_call x1, Pallas kernels, root_grad(): call(root_kernel, shapes, specs, (VMEM,) * 3, flops=10 ** 9, moved=6 * 2...  2.83 us
  transfers between devices with their start and end apart: 6, of which 5 were waited for; matrix products, arithmetic and copies ran while one was open for 1% of the time, Pallas kernels for 8%

profile of v2, /device:TPU:32, one launch (start us, length us, event | category | flops | bytes accessed | tf_op | source)
XLA Modules:
  0.0 117.9 jit_solution(18251942694720230037)
XLA Ops:
  0.6 0.0 copy-start
  0.6 0.9 copy-done
  1.5 0.0 copy-start.2
  1.5 0.9 copy-done.2
  2.4 0.8 shard_map.86
  3.3 15.0 %all-to-all-start = ((bf16[128,8,128]{2,1,0:T(8,128)(2,1)}), bf16[128,8,128]{2,1,0:T(8,128)(2,1)S(1)}, u32[]{:S(2)}, u32[]{:S(2)}) async-start(bf16[128,8,128]{2,1,0:T(8,128)(2,1)} %bitcast.2), calls=%async_computation | async-start | bytes 524288 | tf_op jit(solution)/shard_map/all_to_all | solution.py:362
  18.3 0.0 slice-start
  18.3 0.0 slice-start.1
  18.3 0.0 slice-start.2
  18.3 0.0 slice-start.3
  18.4 0.8 slice-done
  19.1 0.0 slice-done.1
  19.2 0.2 slice-done.2
  19.4 0.2 slice-done.3
  19.6 0.0 copy-start.8
  19.6 1.1 pad_maximum_fusion
  20.7 0.0 copy-start.1
  20.7 0.0 copy-start.3
  20.7 0.0 copy-start.10
  20.7 1.4 %collective-permute-start = (bf16[128,4608]{1,0:T(8,128)(2,1)}, bf16[128,4608]{1,0:T(8,128)(2,1)}, u32[]{:S(2)}, u32[]{:S(2)}) collective-permute-start(bf16[128,4608]{1,0:T(8,128)(2,1)} %pad_maximum_fusion), channel_id=1, source_target_pairs={{192,0},{128,64},{193,1},{129,65},{194,2},{130,66},{195,3},{131,67... | collective-permute-start | bytes 3538952 | tf_op jit(solution)/shard_map/ppermute | solution.py:373
  22.1 10.7 %all-to-all-done = bf16[128,8,128]{2,1,0:T(8,128)(2,1)S(1)} async-done(((bf16[128,8,128]{2,1,0:T(8,128)(2,1)}), bf16[128,8,128]{2,1,0:T(8,128)(2,1)S(1)}, u32[]{:S(2)}, u32[]{:S(2)}) %all-to-all-start) | async-done | bytes 262176 | tf_op jit(solution)/shard_map/all_to_all | solution.py:362
  32.8 0.0 copy-done.8
  32.8 1.7 %shard_map.87 = bf16[1536,128]{1,0:T(8,128)(2,1)} custom-call(s32[3,32]{1,0:T(4,128)S(1)} %copy-done.8, bf16[1024,128]{1,0:T(8,128)(2,1)S(1)} %bitcast.12), custom_call_target="tpu_custom_call" | custom-call | tf_op jit(solution)/shard_map/pallas_call | solution.py:121
  34.5 6.6 %all-to-all-start.1 = ((bf16[128,3,4,128]{3,2,1,0:T(4,128)(2,1)}), bf16[128,3,4,128]{3,2,1,0:T(4,128)(2,1)S(1)}, u32[]{:S(2)}, u32[]{:S(2)}) async-start(bf16[128,3,4,128]{3,2,1,0:T(4,128)(2,1)} %bitcast.4), calls=%async_computation.1 | async-start | bytes 786432 | tf_op jit(solution)/shard_map/all_to_all | solution.py:362
  41.1 0.1 pad_add_fusion.place_ref
  41.2 15.8 %collective-permute-done.guest_ref = bf16[128,4608]{1,0:T(8,128)(2,1)} collective-permute-done((bf16[128,4608]{1,0:T(8,128)(2,1)}, bf16[128,4608]{1,0:T(8,128)(2,1)}, u32[]{:S(2)}, u32[]{:S(2)}) %collective-permute-start) | collective-permute-done | bytes 1179680 | tf_op jit(solution)/shard_map/ppermute | solution.py:373
  57.0 0.5 all-to-all-done.1
  57.5 0.0 copy-done.1
  57.5 0.0 copy-done.3
  57.5 0.0 copy-done.10
  57.5 0.0 copy-start.4
  57.5 1.2 %copy-done.4 = bf16[128,4096]{1,0:T(8,128)(2,1)S(1)} copy-done((bf16[128,4096]{1,0:T(8,128)(2,1)S(1)}, bf16[128,4096]{1,0:T(8,128)(2,1)}, u32[]{:S(2)}) %copy-start.4) | copy-done | bytes 1048600
  58.7 1.2 %copy-done.6 = bf16[128,4096]{1,0:T(8,128)(2,1)S(1)} copy-done((bf16[128,4096]{1,0:T(8,128)(2,1)S(1)}, bf16[128,4096]{1,0:T(8,128)(2,1)}, u32[]{:S(2)}) %copy-start.6) | copy-done | bytes 1048600
  60.0 6.7 %shard_map.88 = (bf16[128,4096]{1,0:T(8,128)(2,1)S(1)}, f32[128,512]{1,0:T(8,128)S(1)}, f32[128,512]{1,0:T(8,128)S(1)}, bf16[128,2560]{1,0:T(8,128)(2,1)S(1)}, bf16[1536,128]{1,0:T(8,128)(2,1)}) custom-call(s32[2]{0:T(128)S(1)} %pad_add_fusion.place_ref, s32[3,32]{1,0:T(4,128)S(1)} %copy-done.8, s32[4,32]{1,0:T(4,128)S(1)} %copy-done.10, ...), custom_call_target="tpu_custom_call" | custom-call | flops 3000000000 | bytes 10485760 | tf_op jit(solution)/shard_map/pallas_call | solution.py:301
  66.6 0.8 copy-done.9
  67.5 10.8 %all-to-all-start.2 = ((bf16[128,3,4,128]{3,2,1,0:T(4,128)(2,1)}), bf16[128,3,4,128]{3,2,1,0:T(4,128)(2,1)S(1)}, u32[]{:S(2)}, u32[]{:S(2)}) async-start(bf16[128,3,4,128]{3,2,1,0:T(4,128)(2,1)} %bitcast.6), calls=%async_computation.2 | async-start | bytes 786432 | tf_op jit(solution)/shard_map/all_to_all | solution.py:362
  78.3 5.2 %collective-permute-start.1 = (bf16[128,2560]{1,0:T(8,128)(2,1)}, bf16[128,2560]{1,0:T(8,128)(2,1)S(1)}, u32[]{:S(2)}, u32[]{:S(2)}) collective-permute-start(bf16[128,2560]{1,0:T(8,128)(2,1)} %copy-done.9), channel_id=1, source_target_pairs={{0,192},{64,128},{1,193},{65,129},{2,194},{66,130},{3,195},{67,131... | collective-permute-start | bytes 1966088 | tf_op jit(solution)/shard_map/ppermute | solution.py:379
  83.5 10.9 %all-to-all-done.2 = bf16[128,3,4,128]{3,2,1,0:T(4,128)(2,1)S(1)} async-done(((bf16[128,3,4,128]{3,2,1,0:T(4,128)(2,1)}), bf16[128,3,4,128]{3,2,1,0:T(4,128)(2,1)S(1)}, u32[]{:S(2)}, u32[]{:S(2)}) %all-to-all-start.2) | async-done | bytes 393248 | tf_op jit(solution)/shard_map/all_to_all | solution.py:362
  94.4 2.1 %shard_map.90 = bf16[1024,128]{1,0:T(8,128)(2,1)} custom-call(s32[3,32]{1,0:T(4,128)S(1)} %copy-done.8, bf16[1536,128]{1,0:T(8,128)(2,1)S(1)} %bitcast.10), custom_call_target="tpu_custom_call" | custom-call | tf_op jit(solution)/shard_map/pallas_call | solution.py:152
  96.5 6.6 %all-to-all-start.3 = ((bf16[128,8,128]{2,1,0:T(8,128)(2,1)}), bf16[128,8,128]{2,1,0:T(8,128)(2,1)S(1)}, u32[]{:S(2)}, u32[]{:S(2)}) async-start(bf16[128,8,128]{2,1,0:T(8,128)(2,1)} %bitcast.8), calls=%async_computation.3 | async-start | bytes 524288 | tf_op jit(solution)/shard_map/all_to_all | solution.py:362
  103.1 0.0 copy-start.5
  103.2 1.2 %copy-done.5 = bf16[128,4096]{1,0:T(8,128)(2,1)S(1)} copy-done((bf16[128,4096]{1,0:T(8,128)(2,1)S(1)}, bf16[128,4096]{1,0:T(8,128)(2,1)}, u32[]{:S(2)}) %copy-start.5) | copy-done | bytes 1048600
  104.4 1.2 %copy-done.7 = bf16[128,4096]{1,0:T(8,128)(2,1)S(1)} copy-done((bf16[128,4096]{1,0:T(8,128)(2,1)S(1)}, bf16[128,4096]{1,0:T(8,128)(2,1)}, u32[]{:S(2)}) %copy-start.7) | copy-done | bytes 1048600
  105.6 2.8 %shard_map.85 = (bf16[128,4096]{1,0:T(8,128)(2,1)S(1)}, f32[128,512]{1,0:T(8,128)S(1)}, f32[128,512]{1,0:T(8,128)S(1)}) custom-call(s32[2]{0:T(128)S(1)} %pad_add_fusion.place_ref, s32[4,32]{1,0:T(4,128)S(1)} %copy-done.10, bf16[128,4096]{1,0:T(8,128)(2,1)S(1)} %copy-done.5, bf16[128,4096]{1,0:T(8,128)(2,1)S(1)} %copy-done.7, ...), custom_call_target="tpu_custom_call" | custom-call | flops 1000000000 | bytes 6291456 | tf_op jit(solution)/shard_map/pallas_call | solution.py:223
  108.4 0.0 collective-permute-done.1.back_ref
  108.4 2.3 %shard_map.89 = bf16[128,4096]{1,0:T(8,128)(2,1)} custom-call(s32[2]{0:T(128)S(1)} %pad_add_fusion.place_ref, bf16[128,4096]{1,0:T(8,128)(2,1)S(1)} %get-tuple-element.13.root_ref, bf16[128,4096]{1,0:T(8,128)(2,1)S(1)} %get-tuple-element.14.here_ref, bf16[128,2560]{1,0:T(8,128)(2,1)S(1)} %collective-permute-done.1.back_ref), custom_call_target="tpu_custom_call" | custom-call | bytes 4194304 | tf_op jit(solution)/shard_map/pallas_call | solution.py:327
  110.8 5.6 %all-to-all-done.3 = bf16[128,8,128]{2,1,0:T(8,128)(2,1)S(1)} async-done(((bf16[128,8,128]{2,1,0:T(8,128)(2,1)}), bf16[128,8,128]{2,1,0:T(8,128)(2,1)S(1)}, u32[]{:S(2)}, u32[]{:S(2)}) %all-to-all-start.3) | async-done | bytes 262176 | tf_op jit(solution)/shard_map/all_to_all | solution.py:362
  116.4 1.5 %shard_map.91 = (bf16[128,512]{1,0:T(8,128)(2,1)}, bf16[128,512]{1,0:T(8,128)(2,1)}) custom-call(s32[2]{0:T(128)S(1)} %pad_add_fusion.place_ref, bf16[1024,128]{1,0:T(8,128)(2,1)S(1)} %bitcast.11, f32[128,512]{1,0:T(8,128)S(1)} %get-tuple-element.17.root_key_ref, f32[128,512]{1,0:T(8,128)S(1)} %get-tuple-element.18.root_value_ref, ...), custom_call_target="tpu_custom_call" | custom-call | tf_op jit(solution)/shard_map/pallas_call | solution.py:355
  (3 shorter events, 0.0 us)
Async XLA Ops:
  0.6 0.9 copy-start
  1.5 0.9 copy-start.2
  3.3 29.5 %all-to-all-start = ((bf16[128,8,128]{2,1,0:T(8,128)(2,1)}), bf16[128,8,128]{2,1,0:T(8,128)(2,1)S(1)}, u32[]{:S(2)}, u32[]{:S(2)}) async-start(bf16[128,8,128]{2,1,0:T(8,128)(2,1)} %bitcast.2), calls=%async_computation | async-start | bytes 524288 | tf_op jit(solution)/shard_map/all_to_all | solution.py:362
  18.3 0.8 slice-start
  18.3 0.9 slice-start.1
  18.3 1.1 slice-start.2
  18.3 1.2 %slice-start.3 = ((bf16[128,4096]{1,0:T(8,128)(2,1)}), bf16[128,2048]{1,0:T(8,128)(2,1)S(1)}, s32[]{:S(2)}) async-start(bf16[128,4096]{1,0:T(8,128)(2,1)} %grad_ref.3), calls=%async_computation.7 | async-start | bytes 1048576 | tf_op jit(solution)/shard_map/slice | solution.py:370
  19.6 13.2 %copy-start.8 = (s32[3,32]{1,0:T(4,128)S(1)}, s32[3,32]{1,0:T(4,128)}, u32[]{:S(2)}) copy-start(s32[3,32]{1,0:T(4,128)} %parents_ref.5) | copy-start | bytes 1156
  20.7 36.8 %copy-start.1 = (bf16[128,512]{1,0:T(8,128)(2,1)S(1)}, bf16[128,512]{1,0:T(8,128)(2,1)}, u32[]{:S(2)}) copy-start(bf16[128,512]{1,0:T(8,128)(2,1)} %key_ref.5) | copy-start | bytes 393220
  20.7 36.8 %copy-start.3 = (bf16[128,512]{1,0:T(8,128)(2,1)S(1)}, bf16[128,512]{1,0:T(8,128)(2,1)}, u32[]{:S(2)}) copy-start(bf16[128,512]{1,0:T(8,128)(2,1)} %value_ref.5) | copy-start | bytes 393220
  20.7 36.8 %copy-start.10 = (s32[4,32]{1,0:T(4,128)S(1)}, s32[4,32]{1,0:T(4,128)}, u32[]{:S(2)}) copy-start(s32[4,32]{1,0:T(4,128)} %lengths_ref.3) | copy-start | bytes 1540
  20.7 36.3 %collective-permute-start = (bf16[128,4608]{1,0:T(8,128)(2,1)}, bf16[128,4608]{1,0:T(8,128)(2,1)}, u32[]{:S(2)}, u32[]{:S(2)}) collective-permute-start(bf16[128,4608]{1,0:T(8,128)(2,1)} %pad_maximum_fusion), channel_id=1, source_target_pairs={{192,0},{128,64},{193,1},{129,65},{194,2},{130,66},{195,3},{131,67... | collective-permute-start | bytes 3538952 | tf_op jit(solution)/shard_map/ppermute | solution.py:373
  34.5 23.0 %all-to-all-start.1 = ((bf16[128,3,4,128]{3,2,1,0:T(4,128)(2,1)}), bf16[128,3,4,128]{3,2,1,0:T(4,128)(2,1)S(1)}, u32[]{:S(2)}, u32[]{:S(2)}) async-start(bf16[128,3,4,128]{3,2,1,0:T(4,128)(2,1)} %bitcast.4), calls=%async_computation.1 | async-start | bytes 786432 | tf_op jit(solution)/shard_map/all_to_all | solution.py:362
  57.5 1.2 %copy-start.4 = (bf16[128,4096]{1,0:T(8,128)(2,1)S(1)}, bf16[128,4096]{1,0:T(8,128)(2,1)}, u32[]{:S(2)}) copy-start(bf16[128,4096]{1,0:T(8,128)(2,1)} %query_ref.3) | copy-start | bytes 3145732
  58.7 1.2 %copy-start.6 = (bf16[128,4096]{1,0:T(8,128)(2,1)S(1)}, bf16[128,4096]{1,0:T(8,128)(2,1)}, u32[]{:S(2)}) copy-start(bf16[128,4096]{1,0:T(8,128)(2,1)} %grad_ref.3) | copy-start | bytes 3145732
  66.6 0.8 copy-start.9
  67.5 27.0 %all-to-all-start.2 = ((bf16[128,3,4,128]{3,2,1,0:T(4,128)(2,1)}), bf16[128,3,4,128]{3,2,1,0:T(4,128)(2,1)S(1)}, u32[]{:S(2)}, u32[]{:S(2)}) async-start(bf16[128,3,4,128]{3,2,1,0:T(4,128)(2,1)} %bitcast.6), calls=%async_computation.2 | async-start | bytes 786432 | tf_op jit(solution)/shard_map/all_to_all | solution.py:362
  78.3 30.1 %collective-permute-start.1 = (bf16[128,2560]{1,0:T(8,128)(2,1)}, bf16[128,2560]{1,0:T(8,128)(2,1)S(1)}, u32[]{:S(2)}, u32[]{:S(2)}) collective-permute-start(bf16[128,2560]{1,0:T(8,128)(2,1)} %copy-done.9), channel_id=1, source_target_pairs={{0,192},{64,128},{1,193},{65,129},{2,194},{66,130},{3,195},{67,131... | collective-permute-start | bytes 1966088 | tf_op jit(solution)/shard_map/ppermute | solution.py:379
  96.5 19.9 %all-to-all-start.3 = ((bf16[128,8,128]{2,1,0:T(8,128)(2,1)}), bf16[128,8,128]{2,1,0:T(8,128)(2,1)S(1)}, u32[]{:S(2)}, u32[]{:S(2)}) async-start(bf16[128,8,128]{2,1,0:T(8,128)(2,1)} %bitcast.8), calls=%async_computation.3 | async-start | bytes 524288 | tf_op jit(solution)/shard_map/all_to_all | solution.py:362
  103.1 1.2 %copy-start.5 = (bf16[128,4096]{1,0:T(8,128)(2,1)S(1)}, bf16[128,4096]{1,0:T(8,128)(2,1)}, u32[]{:S(2)}) copy-start(bf16[128,4096]{1,0:T(8,128)(2,1)} %query_ref.3) | copy-start | bytes 3145732
  104.4 1.2 %copy-start.7 = (bf16[128,4096]{1,0:T(8,128)(2,1)S(1)}, bf16[128,4096]{1,0:T(8,128)(2,1)}, u32[]{:S(2)}) copy-start(bf16[128,4096]{1,0:T(8,128)(2,1)} %grad_ref.3) | copy-start | bytes 3145732

commit v3 on v2

v3 whole, which is shorter than its diff:
```python
import jax
import jax.numpy as jnp
from jax import lax
from jax.experimental import pallas as pl
from jax.experimental.pallas import tpu as pltpu
from jax.sharding import PartitionSpec as P

HD = 128
LEVELS = 4
SEGS = 32
ROWS = 128
HEADS = 4
REPEAT = 8
GROUP = REPEAT * HD
WIDTH = HEADS * HD
TILE = 2 * HEADS
UPPER = LEVELS - 1
DEVICES = LEVELS * SEGS
SLOTS = 6
PIECE = 2 * SLOTS
HALF = HEADS // 2
LENT = HALF * (GROUP + HD)
BACK_KEY = HALF * GROUP
BACK_VALUE = BACK_KEY + HALF * HD
VMEM_LIMIT = 40 * 1024 * 1024
BESIDE = 10**12
LOG2E = 1.4426950408889634
FACTOR = HD ** (-0.5)
VMEM = pl.BlockSpec(memory_space=pltpu.VMEM)
SMEM = pl.BlockSpec(memory_space=pltpu.SMEM)
ANY = pl.BlockSpec(memory_space=pl.ANY)

TASKS = {
    0: ((True, 2, (0, 2, 4)), (True, 3, (1, 3, 5))),
    1: ((False, 0, (0,)), (False, 1, (1,)), (False, 2, (2,)), (False, 3, (3,)), (True, 3, (4, 5))),
    2: ((False, 0, (0, 2)), (False, 1, (1, 3)), (False, 2, (4, 5))),
    3: ((False, 0, (0, 2, 4)), (False, 1, (1, 3, 5))),
}
HOST = {0: 3, 1: 2}
MOST = max(len(tasks) for tasks in TASKS.values())


def call(kernel, out_shape, in_specs, out_specs, scratch=(), flops=0, moved=0, grid=None):
    extra = {} if grid is None else {"grid": grid}
    return pl.pallas_call(
        kernel,
        out_shape=out_shape,
        in_specs=in_specs,
        out_specs=out_specs,
        scratch_shapes=list(scratch),
        cost_estimate=pl.CostEstimate(flops=flops, bytes_accessed=moved, transcendentals=0),
        compiler_params=pltpu.CompilerParams(vmem_limit_bytes=VMEM_LIMIT),
        **extra,
    )


def low(*shape):
    return jax.ShapeDtypeStruct(shape, jnp.bfloat16)


def full(*shape):
    return jax.ShapeDtypeStruct(shape, jnp.float32)


def near(*shape, dtype=jnp.bfloat16):
    return pltpu.VMEM(shape, dtype)


def far(*shape, dtype=jnp.bfloat16):
    return pltpu.HBM(shape, dtype)


def in_far(*arrays):
    return [pltpu.with_memory_space_constraint(array, pltpu.HBM) for array in arrays]


def wide_scratch(rows):
    return pltpu.VMEM((rows, HD), jnp.float32)


def pack_kernel(query_ref, grad_ref, key_ref, value_ref, out_ref, first_ref, second_ref, keys, values, wide, sems):
    half = HALF * GROUP
    copies = [
        pltpu.make_async_copy(key_ref, keys, sems.at[0]),
        pltpu.make_async_copy(value_ref, values, sems.at[1]),
        pltpu.make_async_copy(query_ref.at[:, half:], first_ref.at[:, :half], sems.at[2]),
        pltpu.make_async_copy(grad_ref.at[:, half:], second_ref.at[:, :half], sems.at[3]),
    ]
    for copy in copies:
        copy.start()
    for copy in copies[:2]:
        copy.wait()
    first_ref[:, half:] = keys[:, HALF * HD :]
    second_ref[:, half:] = values[:, HALF * HD :]
    for head in range(HEADS):
        lanes = slice(head * HD, (head + 1) * HD)
        wide[pl.ds(2 * head, ROWS, stride=TILE), :] = keys[:, lanes].astype(jnp.float32)
        wide[pl.ds(2 * head + 1, ROWS, stride=TILE), :] = values[:, lanes].astype(jnp.float32)
    out_ref[...] = wide[...].astype(jnp.bfloat16)
    for copy in copies[2:]:
        copy.wait()


def pack(queries, grad_output, keys, values):
    shapes = (near(ROWS * TILE, HD), near(ROWS, LENT), near(ROWS, LENT))
    scratch = [near(ROWS, WIDTH), near(ROWS, WIDTH), wide_scratch(ROWS * TILE), pltpu.SemaphoreType.DMA((4,))]
    return call(pack_kernel, shapes, [ANY] * 4, (VMEM,) * 3, scratch)(*in_far(queries, grad_output, keys, values))


def chain(parents_ref, level, seg):
    found = []
    current = seg
    for upper in range(level - 1, -1, -1):
        current = parents_ref[upper, current]
        found.insert(0, current)
    return found


def tile_at(upper, ancestor):
    return pl.ds(pl.multiple_of((upper * SEGS + ancestor) * TILE, TILE), TILE)


def rows_of(level, seg, first, count):
    return pl.ds((level * SEGS + seg) * PIECE + first, count)


def select_kernel(parents_ref, held_ref, out_ref, wide, picked):
    wide[...] = held_ref[...].astype(jnp.float32)

    def step(seg, carry):
        for upper, ancestor in enumerate(chain(parents_ref, 3, seg)):
            tile = wide[tile_at(upper, ancestor), :]
            picked[rows_of(3, seg, 4 * upper, 4), :] = tile[0:4]
            picked[rows_of(0, seg, 4 * upper, 4), :] = tile[4:8]
        first, second = [wide[tile_at(u, a), :] for u, a in enumerate(chain(parents_ref, 2, seg))]
        picked[rows_of(2, seg, 0, 4), :] = first[0:4]
        picked[rows_of(2, seg, 4, 4), :] = second[0:4]
        picked[rows_of(2, seg, 8, 2), :] = first[4:6]
        picked[rows_of(2, seg, 10, 2), :] = second[4:6]
        picked[rows_of(1, seg, 8, 2), :] = first[6:8]
        picked[rows_of(1, seg, 10, 2), :] = second[6:8]
        (only,) = chain(parents_ref, 1, seg)
        picked[rows_of(1, seg, 0, 8), :] = wide[tile_at(0, only), :]
        return carry

    lax.fori_loop(0, SEGS, step, 0, unroll=8)
    out_ref[...] = picked[...].astype(jnp.bfloat16)


def select(parents, held):
    scratch = [wide_scratch(DEVICES * TILE), wide_scratch(DEVICES * PIECE)]
    return call(select_kernel, near(DEVICES * PIECE, HD), [SMEM, VMEM], VMEM, scratch)(parents, held)


def sum_kernel(parents_ref, terms_ref, after_ref, out_ref, wide, *totals):
    wide[...] = terms_ref[...].astype(jnp.float32)
    for total in totals:
        total[...] = jnp.zeros_like(total)
    from_three, from_two, from_one = totals[:3], totals[3:5], totals[5]

    def rows(level, seg, first, count):
        return wide[rows_of(level, seg, first, count), :]

    def step(seg, carry):
        for upper, ancestor in enumerate(chain(parents_ref, 3, seg)):
            from_three[upper][tile_at(0, ancestor), :] += jnp.concatenate(
                [rows(3, seg, 4 * upper, 4), rows(0, seg, 4 * upper, 4)]
            )
        for upper, ancestor in enumerate(chain(parents_ref, 2, seg)):
            from_two[upper][tile_at(0, ancestor), :] += jnp.concatenate(
                [rows(2, seg, 4 * upper, 4), rows(2, seg, 8 + 2 * upper, 2), rows(1, seg, 8 + 2 * upper, 2)]
            )
        (only,) = chain(parents_ref, 1, seg)
        from_one[tile_at(0, only), :] += rows(1, seg, 0, 8)
        return carry

    lax.fori_loop(0, SEGS, step, 0, unroll=8)
    size = SEGS * TILE
    out_ref[0:size] = (from_three[0][...] + from_two[0][...] + from_one[...]).astype(jnp.bfloat16)
    out_ref[size : 2 * size] = (from_three[1][...] + from_two[1][...]).astype(jnp.bfloat16)
    out_ref[2 * size : 3 * size] = from_three[2][...].astype(jnp.bfloat16)
    out_ref[3 * size :] = jnp.zeros((size, HD), jnp.bfloat16)


def sum_terms(parents, terms, after):
    scratch = [wide_scratch(DEVICES * PIECE)] + [wide_scratch(SEGS * TILE)] * 6
    return call(sum_kernel, near(DEVICES * TILE, HD), [SMEM, VMEM, ANY], VMEM, scratch)(parents, terms, after)


def dot_last(left, right):
    return lax.dot_general(left, right, (((1,), (1,)), ((), ())), preferred_element_type=jnp.float32)


def dot(left, right):
    return jnp.dot(left, right, preferred_element_type=jnp.float32)


def block_mask(lengths):
    slots = lax.broadcasted_iota(jnp.int32, (ROWS, ROWS), 0)
    rows = lax.broadcasted_iota(jnp.int32, (ROWS, ROWS), 1)
    allowed = [slots < length for length in lengths]
    allowed[-1] = allowed[-1] & (slots <= rows)
    return jnp.concatenate([jnp.where(each, 0.0, -jnp.inf).astype(jnp.float32) for each in allowed])


def head_grad(keys, values, blocked, live_rows, query_at, grad_at, store):
    query = jnp.concatenate([query_at(i) for i in range(REPEAT)])
    grad = jnp.concatenate(
        [jnp.where(live_rows, grad_at(i), jnp.zeros((), jnp.bfloat16)) for i in range(REPEAT)]
    )
    scores = dot_last(keys, query) * (FACTOR * LOG2E) + jnp.concatenate([blocked] * REPEAT, axis=1)
    weights = jnp.exp2(scores - jnp.max(scores, axis=0, keepdims=True))
    probs = weights * (1.0 / jnp.sum(weights, axis=0, keepdims=True))
    grad_probs = dot_last(values, grad)
    correction = jnp.sum(probs * grad_probs, axis=0, keepdims=True)
    grad_scores = (probs * ((grad_probs - correction) * FACTOR)).astype(jnp.bfloat16)
    value_sum = dot(probs.astype(jnp.bfloat16), grad)
    key_sum = dot(grad_scores, query)
    turned = dot(keys.T, grad_scores).astype(jnp.bfloat16)
    for i in range(REPEAT):
        store(i, turned[:, i * ROWS : (i + 1) * ROWS].T)
    return key_sum, value_sum


def live(length):
    return lax.broadcasted_iota(jnp.int32, (ROWS, HD), 0) < length


def lanes_at(ref, start, width=HD):
    return ref.at[:, start : start + width]


def root_kernel(
    place_ref, lengths_ref, query_ref, grad_ref, key_ref, value_ref, guest_ref, after_ref,
    gquery_ref, gkey_ref, gvalue_ref,
    query, grad, keys, values, gquery, sems,
):
    @pl.when(place_ref[0] == 0)
    def _():
        pairs = ((query_ref, query), (grad_ref, grad), (key_ref, keys), (value_ref, values))
        copies = [pltpu.make_async_copy(*pair, sems.at[i]) for i, pair in enumerate(pairs)]
        for copy in copies:
            copy.start()
        for copy in copies:
            copy.wait()
        length = lengths_ref[0, place_ref[1]]
        blocked = block_mask([length])
        for head in range(HEADS):
            lanes = slice(head * HD, (head + 1) * HD)

            def store(i, block):
                lanes_at(gquery, head * GROUP + i * HD)[...] = block

            gkey_ref[:, lanes], gvalue_ref[:, lanes] = head_grad(
                keys[:, lanes],
                values[:, lanes],
                blocked,
                live(length),
                lambda i: lanes_at(query, head * GROUP + i * HD)[...],
                lambda i: lanes_at(grad, head * GROUP + i * HD)[...],
                store,
            )
        out = pltpu.make_async_copy(gquery, gquery_ref, sems.at[0])
        out.start()
        out.wait()


def root_grad(place, lengths, queries, grad_output, keys, values, guest, after):
    shapes = (
        far(ROWS, HEADS * GROUP), near(ROWS, WIDTH, dtype=jnp.float32), near(ROWS, WIDTH, dtype=jnp.float32)
    )
    specs = [SMEM, SMEM] + [ANY] * 6
    outs = (ANY, VMEM, VMEM)
    scratch = [
        near(ROWS, HEADS * GROUP), near(ROWS, HEADS * GROUP), near(ROWS, WIDTH), near(ROWS, WIDTH),
        near(ROWS, HEADS * GROUP), pltpu.SemaphoreType.DMA((4,)),
    ]
    return call(root_kernel, shapes, specs, outs, scratch, flops=BESIDE)(
        place, lengths, *in_far(queries, grad_output, keys, values), guest, after
    )


def attention_kernel(
    place_ref, parents_ref, lengths_ref,
    query_ref, grad_ref, key_ref, value_ref, first_ref, second_ref, held_ref, after_ref,
    gquery_ref, gkey_ref, gvalue_ref, back_ref, terms_ref,
    query, grad, keys, values, held, gquery, gkey, gvalue, back_own, wide, sums, in_sems, out_sems, held_sem,
):
    level_here = place_ref[0]
    seg = place_ref[1]

    def fetches(level, index):
        guest, head, _ = TASKS[level][index]
        if guest:
            wide_at, narrow_at = (head - HALF) * GROUP, HALF * GROUP + (head - HALF) * HD
            many = (first_ref, second_ref, first_ref, second_ref)
        else:
            wide_at, narrow_at = head * GROUP, head * HD
            many = (query_ref, grad_ref, key_ref, value_ref)
        sources = [lanes_at(ref, wide_at, GROUP) for ref in many[:2]] + [lanes_at(ref, narrow_at) for ref in many[2:]]
        return [
            pltpu.make_async_copy(source, target.at[index], in_sems.at[index, i])
            for i, (source, target) in enumerate(zip(sources, (query, grad, keys, values)))
        ]

    def result(level, index):
        guest, head, _ = TASKS[level][index]
        target = lanes_at(back_ref, (head - HALF) * GROUP, GROUP) if guest else lanes_at(gquery_ref, head * GROUP, GROUP)
        return pltpu.make_async_copy(gquery.at[index], target, out_sems.at[index])

    def at_level(level, body):
        pl.when(level_here == level)(body)

    def fetch_all(level):
        for index in range(len(TASKS[level])):
            for copy in fetches(level, index):
                copy.start()

    fetch_held = pltpu.make_async_copy(held_ref, held, held_sem)
    fetch_held.start()
    for level in range(LEVELS):
        at_level(level, lambda level=level: fetch_all(level))
    fetch_held.wait()
    wide[...] = held[...].astype(jnp.float32)

    def slot_rows(slot, part):
        return pl.ds(2 * slot + part, ROWS, stride=PIECE)

    def setting(level):
        lengths = [lengths_ref[u, a] for u, a in enumerate(chain(parents_ref, level, seg))]
        lengths.append(lengths_ref[level, seg])
        return block_mask(lengths), live(lengths[-1])

    def work(level, index, blocked, live_rows):
        slots = TASKS[level][index][2]
        key_list, value_list = [
            jnp.concatenate([wide[slot_rows(slot, part), :].astype(jnp.bfloat16) for slot in slots] + [mine[index]])
            for part, mine in enumerate((keys, values))
        ]

        def store(i, block):
            gquery[index, :, i * HD : (i + 1) * HD] = block

        key_sum, value_sum = head_grad(
            key_list,
            value_list,
            blocked,
            live_rows,
            lambda i: query[index, :, i * HD : (i + 1) * HD],
            lambda i: grad[index, :, i * HD : (i + 1) * HD],
            store,
        )
        for position, slot in enumerate(slots):
            block = slice(position * ROWS, (position + 1) * ROWS)
            sums[slot_rows(slot, 0), :] = key_sum[block]
            sums[slot_rows(slot, 1), :] = value_sum[block]
        gkey[index] = key_sum[len(slots) * ROWS :]
        gvalue[index] = value_sum[len(slots) * ROWS :]

    def work_on(level, indices, *settings):
        for index in indices:
            for copy in fetches(level, index):
                copy.wait()
        for index, (blocked, live_rows) in zip(indices, settings):
            work(level, index, blocked, live_rows)

    def send(level, indices):
        for index in indices:
            result(level, index).start()

    @pl.when((level_here == 3) | (level_here == 0))
    def _():
        work_on(3, (0, 1), *[setting(3)] * 2)
        at_level(3, lambda: send(3, (0, 1)))
        at_level(0, lambda: send(0, (0, 1)))

    @pl.when(level_here == 2)
    def _():
        both = setting(2)
        work_on(2, (0, 1), both, both)
        send(2, (0, 1))
        work_on(2, (2,), both)
        send(2, (2,))

    @pl.when(level_here == 1)
    def _():
        own, other = setting(1), setting(2)
        work_on(1, (4, 0), other, own)
        send(1, (4, 0))
        work_on(1, (1, 2, 3), own, own, own)
        send(1, (1, 2, 3))

    def hand_out(level):
        for index, (guest, head, _) in enumerate(TASKS[level]):
            if guest:
                place = head - HALF
                back_own[:, place * HD : (place + 1) * HD] = gkey[index].astype(jnp.bfloat16)
                back_own[:, (HALF + place) * HD : (HALF + place + 1) * HD] = gvalue[index].astype(jnp.bfloat16)
            else:
                gkey_ref[:, head * HD : (head + 1) * HD] = gkey[index]
                gvalue_ref[:, head * HD : (head + 1) * HD] = gvalue[index]
        own = pltpu.make_async_copy(back_own, lanes_at(back_ref, BACK_KEY, 2 * HALF * HD), in_sems.at[0, 0])
        if level in HOST:
            own.start()
            own.wait()
        for index in range(len(TASKS[level])):
            result(level, index).wait()

    terms_ref[...] = sums[...].astype(jnp.bfloat16)
    for level in range(LEVELS):
        at_level(level, lambda level=level: hand_out(level))


def attention(place, parents, lengths, queries, grad_output, keys, values, first, second, held, after):
    shapes = (
        far(ROWS, HEADS * GROUP), near(ROWS, WIDTH, dtype=jnp.float32), near(ROWS, WIDTH, dtype=jnp.float32),
        far(ROWS, BACK_VALUE + HALF * HD), near(ROWS * PIECE, HD),
    )
    specs = [SMEM] * 3 + [ANY] * 8
    outs = (ANY, VMEM, VMEM, ANY, VMEM)
    scratch = [
        near(MOST, ROWS, GROUP),
        near(MOST, ROWS, GROUP),
        near(MOST, ROWS, HD),
        near(MOST, ROWS, HD),
        near(ROWS * PIECE, HD),
        near(MOST, ROWS, GROUP),
        near(MOST, ROWS, HD, dtype=jnp.float32),
        near(MOST, ROWS, HD, dtype=jnp.float32),
        near(ROWS, 2 * HALF * HD),
        wide_scratch(ROWS * PIECE),
        wide_scratch(ROWS * PIECE),
        pltpu.SemaphoreType.DMA((MOST, 4)),
        pltpu.SemaphoreType.DMA((MOST,)),
        pltpu.SemaphoreType.DMA(()),
    ]
    return call(attention_kernel, shapes, specs, outs, scratch, flops=3 * 10**9, moved=10 * 2**20)(
        place, parents, lengths, *in_far(queries, grad_output, keys, values), first, second, held, after
    )


def token_kernel(after_ref, out_ref):
    out_ref[...] = jnp.zeros_like(out_ref)


def token(after):
    return call(token_kernel, full(8, HD), [ANY], VMEM, flops=BESIDE)(after)


def join_kernel(
    place_ref, root_ref, here_ref, back_ref, root_key_ref, here_key_ref, back_key_ref,
    root_value_ref, here_value_ref, back_value_ref, out_ref, key_ref, value_ref,
):
    level = place_ref[0]
    head = pl.program_id(0)
    away = ((level == 3) & (head >= HALF)) | ((level == 2) & (head == HEADS - 1))

    def take(source, key_source, value_source):
        out_ref[...] = source[...]
        key_ref[...] = key_source[...].astype(jnp.float32)
        value_ref[...] = value_source[...].astype(jnp.float32)

    pl.when(away)(lambda: take(back_ref, back_key_ref, back_value_ref))
    pl.when(level == 0)(lambda: take(root_ref, root_key_ref, root_value_ref))
    pl.when((level != 0) & jnp.logical_not(away))(lambda: take(here_ref, here_key_ref, here_value_ref))


def join(place, root, here, back):
    def spec(width, skipped, first):
        return pl.BlockSpec((ROWS, width), lambda h: (0, first // width + jnp.maximum(h - skipped, 0)))

    operands, specs = [place], [SMEM]
    for index, (width, first) in enumerate(((GROUP, 0), (HD, BACK_KEY), (HD, BACK_VALUE))):
        operands += [root[index], here[index], back]
        specs += [spec(width, 0, 0), spec(width, 0, 0), spec(width, HALF, first)]
    shapes = (low(ROWS, HEADS * GROUP), full(ROWS, WIDTH), full(ROWS, WIDTH))
    outs = (spec(GROUP, 0, 0), spec(HD, 0, 0), spec(HD, 0, 0))
    return call(join_kernel, shapes, specs, outs, grid=(HEADS,), moved=6 * 2**20)(*operands)


def finish_kernel(extra_ref, own_key_ref, own_value_ref, key_ref, value_ref, wide):
    wide[...] = extra_ref[...].astype(jnp.float32)
    for head in range(HEADS):
        lanes = slice(head * HD, (head + 1) * HD)
        for part, (own_ref, out_ref) in enumerate(((own_key_ref, key_ref), (own_value_ref, value_ref))):
            extra = wide[pl.ds(2 * head + part, ROWS, stride=TILE), :]
            out_ref[:, lanes] = (own_ref[:, lanes] + extra).astype(jnp.bfloat16)


def finish(extra, own_key, own_value):
    shapes = (low(ROWS, WIDTH), low(ROWS, WIDTH))
    return call(finish_kernel, shapes, [VMEM] * 3, (VMEM, VMEM), [wide_scratch(ROWS * TILE)])(
        extra, own_key, own_value
    )


def exchange(pieces, *tile):
    rows = pieces.shape[0]
    swapped = lax.all_to_all(pieces.reshape(DEVICES, *tile, HD), ("depth", "seg"), 0, 0, tiled=True)
    return swapped.reshape(rows, HD)


def per_device(queries, key_states, value_states, grad_output, parents, lengths):
    place = jnp.stack([lax.axis_index("depth"), lax.axis_index("seg")]).astype(jnp.int32)
    place, parents, lengths = in_far(place, parents, lengths)
    packed, *lent = pack(queries, grad_output, key_states, value_states)
    first, second = [lax.ppermute(each, "depth", [(host, here) for here, host in HOST.items()]) for each in lent]
    picked = select(parents, exchange(packed, TILE))
    arrived = exchange(picked, SLOTS // 2, 4)
    root = root_grad(place, lengths, queries, grad_output, key_states, value_states, first, picked)
    *here, back, terms = attention(
        place, parents, lengths, queries, grad_output, key_states, value_states, first, second, arrived, root[1]
    )
    back = lax.ppermute(back, "depth", list(HOST.items()))
    grad_q, own_k, own_v = join(place, root, here, back)
    extra = exchange(sum_terms(parents, exchange(terms, SLOTS // 2, 4), token(back)), TILE)
    grad_k, grad_v = finish(extra, own_k, own_v)
    return grad_q, grad_k, grad_v


def solution(mesh):
    placed = P(("depth", "seg"), "tp")
    return jax.shard_map(
        per_device,
        mesh=mesh,
        in_specs=(placed, placed, placed, placed, P(), P()),
        out_specs=(placed, placed, placed),
        check_vma=False,
    )
```

time: 118 us -> 116 us (0.983)
  local copies, waits for them, and re-layouts: 8.79 us -> 2.18 us
  Pallas kernels: 17.9 us -> 23.2 us
  starting transfers between devices: 45.7 us -> 43.5 us
  waiting for transfers between devices: 43.5 us -> 44.8 us
    ppermute x1 -> x2, waiting for transfers between devices: 15.8 us -> 0.01 us  [per_device(): lax.ppermute(each, 'depth', [(host, here) for here, host in HOST.items()])]
    all_to_all x4, waiting for transfers between devices: 27.7 us -> 38 us  [exchange(): lax.all_to_all(pieces.reshape(DEVICES, *tile, HD), ('depth', 'seg'), 0, 0...]
    ppermute x1, waiting for transfers between devices: 0.01 us -> 6.86 us  [per_device(): back = lax.ppermute(back, 'depth', list(HOST.items()))]
    unnamed x22 -> x8, local copies, waits for them, and re-layouts: 7.54 us -> 2.18 us
    pallas_call x7 -> x8, Pallas kernels: 17.9 us -> 23.2 us  [the longest x1 7.93 us: attention(): call(attention_kernel, shapes, specs, outs, scratch, flops=3 * 10 ** 9, m...]
    ppermute x1, starting transfers between devices: 5.16 us -> 2.66 us  [per_device(): back = lax.ppermute(back, 'depth', list(HOST.items()))]
    slice x8 -> x0, local copies, waits for them, and re-layouts: 1.25 us -> none  [the longest x2 0.8 us: per_device(): key_states[:, HALF * HD:]]
    ppermute x1 -> x2, starting transfers between devices: 1.41 us -> 2.58 us  [per_device(): lax.ppermute(each, 'depth', [(host, here) for here, host in HOST.items()])]
  transfers between devices with their start and end apart: 6 -> 7, of which waited for: 5 -> 5; matrix products, arithmetic and copies ran while one was open for 1% -> 1% of each run, Pallas kernels for 8% -> 9%
where the time goes in v3:
time: 116 us; the launch traced here: 115 us
  waiting for transfers between devices  44.8 us (39%)
  starting transfers between devices  43.5 us (38%)
  Pallas kernels  23.2 us (20%)
  local copies, waits for them, and re-layouts  2.18 us (2%)
    all_to_all x4, starting transfers between devices, exchange(): lax.all_to_all(pieces.reshape(DEVICES, *tile, HD), ('depth', 'seg'), 0, 0...  38.3 us
    all_to_all x4, waiting for transfers between devices, exchange(): lax.all_to_all(pieces.reshape(DEVICES, *tile, HD), ('depth', 'seg'), 0, 0...  38 us
    pallas_call x1, Pallas kernels, attention(): call(attention_kernel, shapes, specs, outs, scratch, flops=3 * 10 ** 9, m...  7.93 us
    ppermute x1, waiting for transfers between devices, per_device(): back = lax.ppermute(back, 'depth', list(HOST.items()))  6.86 us
    pallas_call x1, Pallas kernels, root_grad(): call(root_kernel, shapes, specs, outs, scratch, flops=BESIDE)  5.55 us
    ppermute x1, starting transfers between devices, per_device(): back = lax.ppermute(back, 'depth', list(HOST.items()))  2.66 us
    pallas_call x1, Pallas kernels, join(): call(join_kernel, shapes, specs, outs, grid=(HEADS,), moved=6 * 2 ** 20)  2.64 us
    ppermute x2, starting transfers between devices, per_device(): lax.ppermute(each, 'depth', [(host, here) for here, host in HOST.items()])  2.58 us
  transfers between devices with their start and end apart: 7, of which 5 were waited for; matrix products, arithmetic and copies ran while one was open for 1% of the time, Pallas kernels for 9%

profile of v3, /device:TPU:32, one launch (start us, length us, event | category | flops | bytes accessed | tf_op | source)
XLA Modules:
  0.0 115.1 jit_solution(10793513821051853988)
XLA Ops:
  0.6 2.3 %shard_map.85 = (bf16[1024,128]{1,0:T(8,128)(2,1)}, bf16[128,2304]{1,0:T(8,128)(2,1)S(1)}, bf16[128,2304]{1,0:T(8,128)(2,1)}) custom-call(bf16[128,4096]{1,0:T(8,128)(2,1)} %query_ref.5, bf16[128,4096]{1,0:T(8,128)(2,1)} %grad_ref.5, bf16[128,512]{1,0:T(8,128)(2,1)} %key_ref.5, bf16[128,512]{1,0:T(8,128)(2,1)} %value_ref.5), custom_call_target="tpu_custom_call" | custom-call | tf_op jit(solution)/shard_map/pallas_call | solution.py:107
  2.9 1.3 %collective-permute-start = (bf16[128,2304]{1,0:T(8,128)(2,1)S(1)}, bf16[128,2304]{1,0:T(8,128)(2,1)S(1)}, u32[]{:S(2)}, u32[]{:S(2)}) collective-permute-start(bf16[128,2304]{1,0:T(8,128)(2,1)S(1)} %get-tuple-element.19), channel_id=1, source_target_pairs={{192,0},{128,64},{193,1},{129,65},{194,2},{130,66},{195,3},{131,67... | collective-permute-start | bytes 1769480 | tf_op jit(solution)/shard_map/ppermute | solution.py:507
  4.2 16.1 %all-to-all-start = ((bf16[128,8,128]{2,1,0:T(8,128)(2,1)}), bf16[128,8,128]{2,1,0:T(8,128)(2,1)S(1)}, u32[]{:S(2)}, u32[]{:S(2)}) async-start(bf16[128,8,128]{2,1,0:T(8,128)(2,1)} %bitcast.2), calls=%async_computation | async-start | bytes 524288 | tf_op jit(solution)/shard_map/all_to_all | solution.py:499
  20.3 1.3 %collective-permute-start.1 = (bf16[128,2304]{1,0:T(8,128)(2,1)}, bf16[128,2304]{1,0:T(8,128)(2,1)}, u32[]{:S(2)}, u32[]{:S(2)}) collective-permute-start(bf16[128,2304]{1,0:T(8,128)(2,1)} %get-tuple-element.22), channel_id=1, source_target_pairs={{192,0},{128,64},{193,1},{129,65},{194,2},{130,66},{195,3},{131,67... | collective-permute-start | bytes 1769480 | tf_op jit(solution)/shard_map/ppermute | solution.py:507
  21.6 0.6 pad_add_fusion.place_ref
  22.2 12.3 %all-to-all-done = bf16[128,8,128]{2,1,0:T(8,128)(2,1)S(1)} async-done(((bf16[128,8,128]{2,1,0:T(8,128)(2,1)}), bf16[128,8,128]{2,1,0:T(8,128)(2,1)S(1)}, u32[]{:S(2)}, u32[]{:S(2)}) %all-to-all-start) | async-done | bytes 262176 | tf_op jit(solution)/shard_map/all_to_all | solution.py:499
  34.6 1.8 %shard_map.86.after_ref = bf16[1536,128]{1,0:T(8,128)(2,1)} custom-call(s32[3,32]{1,0:T(4,128)} %parents_ref.5, bf16[1024,128]{1,0:T(8,128)(2,1)S(1)} %bitcast.11), custom_call_target="tpu_custom_call" | custom-call | tf_op jit(solution)/shard_map/pallas_call | solution.py:152
  36.4 7.6 %all-to-all-start.1 = ((bf16[128,3,4,128]{3,2,1,0:T(4,128)(2,1)}), bf16[128,3,4,128]{3,2,1,0:T(4,128)(2,1)}, u32[]{:S(2)}, u32[]{:S(2)}) async-start(bf16[128,3,4,128]{3,2,1,0:T(4,128)(2,1)} %bitcast.4), calls=%async_computation.1 | async-start | bytes 786432 | tf_op jit(solution)/shard_map/all_to_all | solution.py:499
  44.0 0.0 collective-permute-done.guest_ref.first_ref
  44.0 5.5 %shard_map.87 = (bf16[128,4096]{1,0:T(8,128)(2,1)}, f32[128,512]{1,0:T(8,128)S(1)}, f32[128,512]{1,0:T(8,128)S(1)}) custom-call(s32[2]{0:T(128)} %pad_add_fusion.place_ref, s32[4,32]{1,0:T(4,128)} %lengths_ref.3, bf16[128,4096]{1,0:T(8,128)(2,1)} %query_ref.5, bf16[128,4096]{1,0:T(8,128)(2,1)} %grad_ref.5, bf16[128,512]{1,0:T(8,128)(2,1)} %key_ref.5, ...), custom_call_target="tpu_custom_call" | custom-call | flops 999999995904 | tf_op jit(solution)/shard_map/pallas_call | solution.py:278
  49.6 0.0 copy-start.2
  49.6 0.0 collective-permute-done.1.second_ref
  49.6 9.9 %all-to-all-done.1 = bf16[128,3,4,128]{3,2,1,0:T(4,128)(2,1)} async-done(((bf16[128,3,4,128]{3,2,1,0:T(4,128)(2,1)}), bf16[128,3,4,128]{3,2,1,0:T(4,128)(2,1)}, u32[]{:S(2)}, u32[]{:S(2)}) %all-to-all-start.1) | async-done | bytes 393248 | tf_op jit(solution)/shard_map/all_to_all | solution.py:499
  59.5 7.9 %shard_map.88 = (bf16[128,4096]{1,0:T(8,128)(2,1)}, f32[128,512]{1,0:T(8,128)S(1)}, f32[128,512]{1,0:T(8,128)S(1)}, bf16[128,2560]{1,0:T(8,128)(2,1)}, bf16[1536,128]{1,0:T(8,128)(2,1)}) custom-call(s32[2]{0:T(128)} %pad_add_fusion.place_ref, s32[3,32]{1,0:T(4,128)} %parents_ref.5, s32[4,32]{1,0:T(4,128)} %lengths_ref.3, bf16[128,4096]{1,0:T(8,128)(2,1)} %query_ref.5, ...), custom_call_target="tpu_custom_call" | custom-call | flops 3000000000 | bytes 10485760 | tf_op jit(solution)/shard_map/pallas_call | solution.py:437
  67.4 0.0 copy-done.2
  67.4 2.7 %collective-permute-start.2 = (bf16[128,2560]{1,0:T(8,128)(2,1)}, bf16[128,2560]{1,0:T(8,128)(2,1)S(1)}, u32[]{:S(2)}, u32[]{:S(2)}) collective-permute-start(bf16[128,2560]{1,0:T(8,128)(2,1)} %get-tuple-element.25), channel_id=1, source_target_pairs={{0,192},{64,128},{1,193},{65,129},{2,194},{66,130},{3,195},{67,131... | collective-permute-start | bytes 1966088 | tf_op jit(solution)/shard_map/ppermute | solution.py:514
  70.1 7.8 %all-to-all-start.2 = ((bf16[128,3,4,128]{3,2,1,0:T(4,128)(2,1)}), bf16[128,3,4,128]{3,2,1,0:T(4,128)(2,1)}, u32[]{:S(2)}, u32[]{:S(2)}) async-start(bf16[128,3,4,128]{3,2,1,0:T(4,128)(2,1)} %bitcast.6), calls=%async_computation.2 | async-start | bytes 786432 | tf_op jit(solution)/shard_map/all_to_all | solution.py:499
  77.9 6.9 %collective-permute-done.2.back_ref.back_key_ref.back_value_ref.after_ref = bf16[128,2560]{1,0:T(8,128)(2,1)S(1)} collective-permute-done((bf16[128,2560]{1,0:T(8,128)(2,1)}, bf16[128,2560]{1,0:T(8,128)(2,1)S(1)}, u32[]{:S(2)}, u32[]{:S(2)}) %collective-permute-start.2) | collective-permute-done | bytes 655392 | tf_op jit(solution)/shard_map/ppermute | solution.py:514
  84.8 0.0 copy-start
  84.8 7.3 %all-to-all-done.2 = bf16[128,3,4,128]{3,2,1,0:T(4,128)(2,1)} async-done(((bf16[128,3,4,128]{3,2,1,0:T(4,128)(2,1)}), bf16[128,3,4,128]{3,2,1,0:T(4,128)(2,1)}, u32[]{:S(2)}, u32[]{:S(2)}) %all-to-all-start.2) | async-done | bytes 393248 | tf_op jit(solution)/shard_map/all_to_all | solution.py:499
  92.1 2.2 %shard_map.91 = bf16[1024,128]{1,0:T(8,128)(2,1)} custom-call(s32[3,32]{1,0:T(4,128)} %parents_ref.5, bf16[1536,128]{1,0:T(8,128)(2,1)} %bitcast.7.terms_ref, f32[8,128]{1,0:T(8,128)S(1)} %shard_map.90.after_ref), custom_call_target="tpu_custom_call" | custom-call | tf_op jit(solution)/shard_map/pallas_call | solution.py:187
  94.3 6.7 %all-to-all-start.3 = ((bf16[128,8,128]{2,1,0:T(8,128)(2,1)}), bf16[128,8,128]{2,1,0:T(8,128)(2,1)S(1)}, u32[]{:S(2)}, u32[]{:S(2)}) async-start(bf16[128,8,128]{2,1,0:T(8,128)(2,1)} %bitcast.8), calls=%async_computation.3 | async-start | bytes 524288 | tf_op jit(solution)/shard_map/all_to_all | solution.py:499
  101.0 0.0 copy-done
  101.0 0.0 copy-start.1
  101.0 1.2 %copy-done.1 = bf16[128,4096]{1,0:T(8,128)(2,1)S(1)} copy-done((bf16[128,4096]{1,0:T(8,128)(2,1)S(1)}, bf16[128,4096]{1,0:T(8,128)(2,1)}, u32[]{:S(2)}) %copy-start.1) | copy-done | bytes 1048600
  102.3 0.0 copy-start.3
  102.3 0.9 copy-done.3
  103.2 2.6 %shard_map.89 = (bf16[128,4096]{1,0:T(8,128)(2,1)}, f32[128,512]{1,0:T(8,128)S(1)}, f32[128,512]{1,0:T(8,128)S(1)}) custom-call(s32[2]{0:T(128)} %pad_add_fusion.place_ref, bf16[128,4096]{1,0:T(8,128)(2,1)S(1)} %copy-done, bf16[128,4096]{1,0:T(8,128)(2,1)S(1)} %copy-done.1, ...), custom_call_target="tpu_custom_call" | custom-call | bytes 6291456 | tf_op jit(solution)/shard_map/pallas_call | solution.py:478
  105.8 8.4 %all-to-all-done.3 = bf16[128,8,128]{2,1,0:T(8,128)(2,1)S(1)} async-done(((bf16[128,8,128]{2,1,0:T(8,128)(2,1)}), bf16[128,8,128]{2,1,0:T(8,128)(2,1)S(1)}, u32[]{:S(2)}, u32[]{:S(2)}) %all-to-all-start.3) | async-done | bytes 262176 | tf_op jit(solution)/shard_map/all_to_all | solution.py:499
  114.2 0.9 shard_map.92
  (1 shorter events, 0.0 us)
Async XLA Ops:
  2.9 41.1 %collective-permute-start = (bf16[128,2304]{1,0:T(8,128)(2,1)S(1)}, bf16[128,2304]{1,0:T(8,128)(2,1)S(1)}, u32[]{:S(2)}, u32[]{:S(2)}) collective-permute-start(bf16[128,2304]{1,0:T(8,128)(2,1)S(1)} %get-tuple-element.19), channel_id=1, source_target_pairs={{192,0},{128,64},{193,1},{129,65},{194,2},{130,66},{195,3},{131,67... | collective-permute-start | bytes 1769480 | tf_op jit(solution)/shard_map/ppermute | solution.py:507
  4.2 30.4 %all-to-all-start = ((bf16[128,8,128]{2,1,0:T(8,128)(2,1)}), bf16[128,8,128]{2,1,0:T(8,128)(2,1)S(1)}, u32[]{:S(2)}, u32[]{:S(2)}) async-start(bf16[128,8,128]{2,1,0:T(8,128)(2,1)} %bitcast.2), calls=%async_computation | async-start | bytes 524288 | tf_op jit(solution)/shard_map/all_to_all | solution.py:499
  20.3 29.2 %collective-permute-start.1 = (bf16[128,2304]{1,0:T(8,128)(2,1)}, bf16[128,2304]{1,0:T(8,128)(2,1)}, u32[]{:S(2)}, u32[]{:S(2)}) collective-permute-start(bf16[128,2304]{1,0:T(8,128)(2,1)} %get-tuple-element.22), channel_id=1, source_target_pairs={{192,0},{128,64},{193,1},{129,65},{194,2},{130,66},{195,3},{131,67... | collective-permute-start | bytes 1769480 | tf_op jit(solution)/shard_map/ppermute | solution.py:507
  36.4 23.1 %all-to-all-start.1 = ((bf16[128,3,4,128]{3,2,1,0:T(4,128)(2,1)}), bf16[128,3,4,128]{3,2,1,0:T(4,128)(2,1)}, u32[]{:S(2)}, u32[]{:S(2)}) async-start(bf16[128,3,4,128]{3,2,1,0:T(4,128)(2,1)} %bitcast.4), calls=%async_computation.1 | async-start | bytes 786432 | tf_op jit(solution)/shard_map/all_to_all | solution.py:499
  49.6 17.9 %copy-start.2 = (f32[128,512]{1,0:T(8,128)}, f32[128,512]{1,0:T(8,128)S(1)}, u32[]{:S(2)}) copy-start(f32[128,512]{1,0:T(8,128)S(1)} %get-tuple-element.23.after_ref.root_key_ref) | copy-start | bytes 786436
  67.4 17.4 %collective-permute-start.2 = (bf16[128,2560]{1,0:T(8,128)(2,1)}, bf16[128,2560]{1,0:T(8,128)(2,1)S(1)}, u32[]{:S(2)}, u32[]{:S(2)}) collective-permute-start(bf16[128,2560]{1,0:T(8,128)(2,1)} %get-tuple-element.25), channel_id=1, source_target_pairs={{0,192},{64,128},{1,193},{65,129},{2,194},{66,130},{3,195},{67,131... | collective-permute-start | bytes 1966088 | tf_op jit(solution)/shard_map/ppermute | solution.py:514
  70.1 22.0 %all-to-all-start.2 = ((bf16[128,3,4,128]{3,2,1,0:T(4,128)(2,1)}), bf16[128,3,4,128]{3,2,1,0:T(4,128)(2,1)}, u32[]{:S(2)}, u32[]{:S(2)}) async-start(bf16[128,3,4,128]{3,2,1,0:T(4,128)(2,1)} %bitcast.6), calls=%async_computation.2 | async-start | bytes 786432 | tf_op jit(solution)/shard_map/all_to_all | solution.py:499
  84.8 16.2 %copy-start = (bf16[128,4096]{1,0:T(8,128)(2,1)S(1)}, bf16[128,4096]{1,0:T(8,128)(2,1)}, u32[]{:S(2)}) copy-start(bf16[128,4096]{1,0:T(8,128)(2,1)} %get-tuple-element.21.root_ref) | copy-start | bytes 3145732
  94.3 20.0 %all-to-all-start.3 = ((bf16[128,8,128]{2,1,0:T(8,128)(2,1)}), bf16[128,8,128]{2,1,0:T(8,128)(2,1)S(1)}, u32[]{:S(2)}, u32[]{:S(2)}) async-start(bf16[128,8,128]{2,1,0:T(8,128)(2,1)} %bitcast.8), calls=%async_computation.3 | async-start | bytes 524288 | tf_op jit(solution)/shard_map/all_to_all | solution.py:499
  101.0 1.2 %copy-start.1 = (bf16[128,4096]{1,0:T(8,128)(2,1)S(1)}, bf16[128,4096]{1,0:T(8,128)(2,1)}, u32[]{:S(2)}) copy-start(bf16[128,4096]{1,0:T(8,128)(2,1)} %get-tuple-element.24.here_ref) | copy-start | bytes 3145732
  102.3 0.9 copy-start.3

commit v4 on v3

--- a/solution.py
+++ b/solution.py
@@ -22,8 +22,8 @@
 LENT = HALF * (GROUP + HD)
 BACK_KEY = HALF * GROUP
 BACK_VALUE = BACK_KEY + HALF * HD
-VMEM_LIMIT = 40 * 1024 * 1024
-BESIDE = 10**12
+VMEM_LIMIT = 32 * 1024 * 1024
+BESIDE = 4 * 10**10
 LOG2E = 1.4426950408889634
 FACTOR = HD ** (-0.5)
 VMEM = pl.BlockSpec(memory_space=pltpu.VMEM)
@@ -37,6 +37,8 @@
     3: ((False, 0, (0, 2, 4)), (False, 1, (1, 3, 5))),
 }
 HOST = {0: 3, 1: 2}
+EARLY = {0: (0, 1), 1: (4, 0), 2: (0, 1), 3: (0, 1)}
+LATE = {0: (), 1: (1, 2, 3), 2: (2,), 3: ()}
 MOST = max(len(tasks) for tasks in TASKS.values())
 
 
@@ -72,6 +74,10 @@
 
 def in_far(*arrays):
     return [pltpu.with_memory_space_constraint(array, pltpu.HBM) for array in arrays]
+
+
+def in_near(*arrays):
+    return [pltpu.with_memory_space_constraint(array, pltpu.VMEM) for array in arrays]
 
 
 def wide_scratch(rows):
@@ -184,7 +190,9 @@
 
 def sum_terms(parents, terms, after):
     scratch = [wide_scratch(DEVICES * PIECE)] + [wide_scratch(SEGS * TILE)] * 6
-    return call(sum_kernel, near(DEVICES * TILE, HD), [SMEM, VMEM, ANY], VMEM, scratch)(parents, terms, after)
+    return call(sum_kernel, near(DEVICES * TILE, HD), [SMEM, VMEM, ANY], VMEM, scratch)(
+        parents, *in_near(terms), after
+    )
 
 
 def dot_last(left, right):
@@ -231,10 +239,40 @@
 
 
 def root_kernel(
-    place_ref, lengths_ref, query_ref, grad_ref, key_ref, value_ref, guest_ref, after_ref,
-    gquery_ref, gkey_ref, gvalue_ref,
-    query, grad, keys, values, gquery, sems,
+    place_ref, lengths_ref, query_ref, grad_ref, key_ref, value_ref, first_ref, second_ref, after_ref, picked_ref,
+    gquery_ref, gkey_ref, gvalue_ref, query_tasks, grad_tasks, key_tasks, value_tasks,
+    query, grad, keys, values, gquery, sems, task_sems,
 ):
+    def fetches(level, index):
+        guest, head, _ = TASKS[level][index]
+        if guest:
+            wide_at, narrow_at = (head - HALF) * GROUP, HALF * GROUP + (head - HALF) * HD
+            many = (first_ref, second_ref, first_ref, second_ref)
+        else:
+            wide_at, narrow_at = head * GROUP, head * HD
+            many = (query_ref, grad_ref, key_ref, value_ref)
+        copies = [
+            pltpu.make_async_copy(lanes_at(ref, narrow_at), target.at[index], task_sems.at[index, i])
+            for i, (ref, target) in enumerate(zip(many[2:], (key_tasks, value_tasks)))
+        ]
+        if index in EARLY[level]:
+            position = EARLY[level].index(index)
+            copies += [
+                pltpu.make_async_copy(lanes_at(ref, wide_at, GROUP), target.at[position], task_sems.at[index, 2 + i])
+                for i, (ref, target) in enumerate(zip(many[:2], (query_tasks, grad_tasks)))
+            ]
+        return copies
+
+    def gather(level):
+        copies = [copy for index in range(len(TASKS[level])) for copy in fetches(level, index)]
+        for copy in copies:
+            copy.start()
+        for copy in copies:
+            copy.wait()
+
+    for level in range(LEVELS):
+        pl.when(place_ref[0] == level)(lambda level=level: gather(level))
+
     @pl.when(place_ref[0] == 0)
     def _():
         pairs = ((query_ref, query), (grad_ref, grad), (key_ref, keys), (value_ref, values))
@@ -265,43 +303,32 @@
         out.wait()
 
 
-def root_grad(place, lengths, queries, grad_output, keys, values, guest, after):
+def task_shapes():
+    return near(2, ROWS, GROUP), near(2, ROWS, GROUP), near(MOST, ROWS, HD), near(MOST, ROWS, HD)
+
+
+def root_grad(place, lengths, queries, grad_output, keys, values, first, second, *after):
     shapes = (
-        far(ROWS, HEADS * GROUP), near(ROWS, WIDTH, dtype=jnp.float32), near(ROWS, WIDTH, dtype=jnp.float32)
-    )
-    specs = [SMEM, SMEM] + [ANY] * 6
-    outs = (ANY, VMEM, VMEM)
+        far(ROWS, HEADS * GROUP), far(ROWS, WIDTH, dtype=jnp.float32), far(ROWS, WIDTH, dtype=jnp.float32),
+    ) + task_shapes()
+    specs = [SMEM, SMEM] + [ANY] * 8
+    outs = (ANY,) + (VMEM,) * 6
     scratch = [
         near(ROWS, HEADS * GROUP), near(ROWS, HEADS * GROUP), near(ROWS, WIDTH), near(ROWS, WIDTH),
-        near(ROWS, HEADS * GROUP), pltpu.SemaphoreType.DMA((4,)),
+        near(ROWS, HEADS * GROUP), pltpu.SemaphoreType.DMA((4,)), pltpu.SemaphoreType.DMA((MOST, 4)),
     ]
-    return call(root_kernel, shapes, specs, outs, scratch, flops=BESIDE)(
-        place, lengths, *in_far(queries, grad_output, keys, values), guest, after
+    return call(root_kernel, shapes, specs, outs, scratch, flops=10**9, moved=6 * 2**20)(
+        place, lengths, *in_far(queries, grad_output, keys, values), first, second, *after
     )
 
 
 def attention_kernel(
-    place_ref, parents_ref, lengths_ref,
-    query_ref, grad_ref, key_ref, value_ref, first_ref, second_ref, held_ref, after_ref,
+    place_ref, parents_ref, lengths_ref, query_ref, grad_ref, query, grad, keys, values, held,
     gquery_ref, gkey_ref, gvalue_ref, back_ref, terms_ref,
-    query, grad, keys, values, held, gquery, gkey, gvalue, back_own, wide, sums, in_sems, out_sems, held_sem,
+    late_query, late_grad, gquery, gkey, gvalue, back_own, wide, sums, in_sems, out_sems, own_sem,
 ):
     level_here = place_ref[0]
     seg = place_ref[1]
-
-    def fetches(level, index):
-        guest, head, _ = TASKS[level][index]
-        if guest:
-            wide_at, narrow_at = (head - HALF) * GROUP, HALF * GROUP + (head - HALF) * HD
-            many = (first_ref, second_ref, first_ref, second_ref)
-        else:
-            wide_at, narrow_at = head * GROUP, head * HD
-            many = (query_ref, grad_ref, key_ref, value_ref)
-        sources = [lanes_at(ref, wide_at, GROUP) for ref in many[:2]] + [lanes_at(ref, narrow_at) for ref in many[2:]]
-        return [
-            pltpu.make_async_copy(source, target.at[index], in_sems.at[index, i])
-            for i, (source, target) in enumerate(zip(sources, (query, grad, keys, values)))
-        ]
 
     def result(level, index):
         guest, head, _ = TASKS[level][index]
@@ -311,16 +338,20 @@
     def at_level(level, body):
         pl.when(level_here == level)(body)
 
-    def fetch_all(level):
-        for index in range(len(TASKS[level])):
-            for copy in fetches(level, index):
+    def late(level, index):
+        place, start = LATE[level].index(index), TASKS[level][index][1] * GROUP
+        return [
+            pltpu.make_async_copy(lanes_at(ref, start, GROUP), target.at[place], in_sems.at[place, i])
+            for i, (ref, target) in enumerate(((query_ref, late_query), (grad_ref, late_grad)))
+        ]
+
+    def fetch_late(level):
+        for index in LATE[level]:
+            for copy in late(level, index):
                 copy.start()
 
-    fetch_held = pltpu.make_async_copy(held_ref, held, held_sem)
-    fetch_held.start()
-    for level in range(LEVELS):
-        at_level(level, lambda level=level: fetch_all(level))
-    fetch_held.wait()
+    for level in (1, 2):
+        at_level(level, lambda level=level: fetch_late(level))
     wide[...] = held[...].astype(jnp.float32)
 
     def slot_rows(slot, part):
@@ -338,6 +369,11 @@
             for part, mine in enumerate((keys, values))
         ]
 
+        if index in EARLY[level]:
+            place, query_from, grad_from = EARLY[level].index(index), query, grad
+        else:
+            place, query_from, grad_from = LATE[level].index(index), late_query, late_grad
+
         def store(i, block):
             gquery[index, :, i * HD : (i + 1) * HD] = block
 
@@ -346,8 +382,8 @@
             value_list,
             blocked,
             live_rows,
-            lambda i: query[index, :, i * HD : (i + 1) * HD],
-            lambda i: grad[index, :, i * HD : (i + 1) * HD],
+            lambda i: query_from[place, :, i * HD : (i + 1) * HD],
+            lambda i: grad_from[place, :, i * HD : (i + 1) * HD],
             store,
         )
         for position, slot in enumerate(slots):
@@ -359,8 +395,9 @@
 
     def work_on(level, indices, *settings):
         for index in indices:
-            for copy in fetches(level, index):
-                copy.wait()
+            if index in LATE[level]:
+                for copy in late(level, index):
+                    copy.wait()
         for index, (blocked, live_rows) in zip(indices, settings):
             work(level, index, blocked, live_rows)
 
@@ -399,7 +436,7 @@
             else:
                 gkey_ref[:, head * HD : (head + 1) * HD] = gkey[index]
                 gvalue_ref[:, head * HD : (head + 1) * HD] = gvalue[index]
-        own = pltpu.make_async_copy(back_own, lanes_at(back_ref, BACK_KEY, 2 * HALF * HD), in_sems.at[0, 0])
+        own = pltpu.make_async_copy(back_own, lanes_at(back_ref, BACK_KEY, 2 * HALF * HD), own_sem)
         if level in HOST:
             own.start()
             own.wait()
@@ -411,31 +448,28 @@
         at_level(level, lambda level=level: hand_out(level))
 
 
-def attention(place, parents, lengths, queries, grad_output, keys, values, first, second, held, after):
+def attention(place, parents, lengths, queries, grad_output, tasks, held):
     shapes = (
-        far(ROWS, HEADS * GROUP), near(ROWS, WIDTH, dtype=jnp.float32), near(ROWS, WIDTH, dtype=jnp.float32),
+        far(ROWS, HEADS * GROUP), far(ROWS, WIDTH, dtype=jnp.float32), far(ROWS, WIDTH, dtype=jnp.float32),
         far(ROWS, BACK_VALUE + HALF * HD), near(ROWS * PIECE, HD),
     )
-    specs = [SMEM] * 3 + [ANY] * 8
+    specs = [SMEM] * 3 + [ANY] * 2 + [VMEM] * 5
     outs = (ANY, VMEM, VMEM, ANY, VMEM)
     scratch = [
         near(MOST, ROWS, GROUP),
         near(MOST, ROWS, GROUP),
-        near(MOST, ROWS, HD),
-        near(MOST, ROWS, HD),
-        near(ROWS * PIECE, HD),
         near(MOST, ROWS, GROUP),
         near(MOST, ROWS, HD, dtype=jnp.float32),
         near(MOST, ROWS, HD, dtype=jnp.float32),
         near(ROWS, 2 * HALF * HD),
         wide_scratch(ROWS * PIECE),
         wide_scratch(ROWS * PIECE),
-        pltpu.SemaphoreType.DMA((MOST, 4)),
+        pltpu.SemaphoreType.DMA((MOST, 2)),
         pltpu.SemaphoreType.DMA((MOST,)),
         pltpu.SemaphoreType.DMA(()),
     ]
     return call(attention_kernel, shapes, specs, outs, scratch, flops=3 * 10**9, moved=10 * 2**20)(
-        place, parents, lengths, *in_far(queries, grad_output, keys, values), first, second, held, after
+        place, parents, lengths, *in_far(queries, grad_output), *in_near(*tasks, held)
     )
 
 
@@ -469,7 +503,7 @@
     def spec(width, skipped, first):
         return pl.BlockSpec((ROWS, width), lambda h: (0, first // width + jnp.maximum(h - skipped, 0)))
 
-    operands, specs = [place], [SMEM]
+    root, here, operands, specs = in_far(*root), in_far(*here), [place], [SMEM]
     for index, (width, first) in enumerate(((GROUP, 0), (HD, BACK_KEY), (HD, BACK_VALUE))):
         operands += [root[index], here[index], back]
         specs += [spec(width, 0, 0), spec(width, 0, 0), spec(width, HALF, first)]
@@ -507,10 +541,11 @@
     first, second = [lax.ppermute(each, "depth", [(host, here) for here, host in HOST.items()]) for each in lent]
     picked = select(parents, exchange(packed, TILE))
     arrived = exchange(picked, SLOTS // 2, 4)
-    root = root_grad(place, lengths, queries, grad_output, key_states, value_states, first, picked)
-    *here, back, terms = attention(
-        place, parents, lengths, queries, grad_output, key_states, value_states, first, second, arrived, root[1]
-    )
+    *root, query_tasks, grad_tasks, key_tasks, value_tasks = root_grad(
+        place, lengths, queries, grad_output, key_states, value_states, first, second, token(first), picked
+    )
+    tasks = (query_tasks, grad_tasks, key_tasks, value_tasks)
+    *here, back, terms = attention(place, parents, lengths, queries, grad_output, tasks, arrived)
     back = lax.ppermute(back, "depth", list(HOST.items()))
     grad_q, own_k, own_v = join(place, root, here, back)
     extra = exchange(sum_terms(parents, exchange(terms, SLOTS // 2, 4), token(back)), TILE)

time: 116 us -> 114 us (0.983)
  starting transfers between devices: 43.5 us -> 41.3 us
  local copies, waits for them, and re-layouts: 2.18 us -> 0 us
  waiting for transfers between devices: 44.8 us -> 46.4 us
    unnamed x8 -> x0, local copies, waits for them, and re-layouts: 2.18 us -> none
    all_to_all x4, starting transfers between devices: 38.3 us -> 36.2 us  [exchange(): lax.all_to_all(pieces.reshape(DEVICES, *tile, HD), ('depth', 'seg'), 0, 0...]
    ppermute x1, waiting for transfers between devices: 6.86 us -> 8.49 us  [per_device(): back = lax.ppermute(back, 'depth', list(HOST.items()))]
  transfers between devices with their start and end apart: 7 -> 7, of which waited for: 5 -> 5; matrix products, arithmetic and copies ran while one was open for 1% -> 1% of each run, Pallas kernels for 9% -> 11%
where the time goes in v4:
time: 114 us; the launch traced here: 113 us
  waiting for transfers between devices  46.4 us (41%)
  starting transfers between devices  41.3 us (36%)
  Pallas kernels  23.9 us (21%)
    all_to_all x4, waiting for transfers between devices, exchange(): lax.all_to_all(pieces.reshape(DEVICES, *tile, HD), ('depth', 'seg'), 0, 0...  37.9 us
    all_to_all x4, starting transfers between devices, exchange(): lax.all_to_all(pieces.reshape(DEVICES, *tile, HD), ('depth', 'seg'), 0, 0...  36.2 us
    ppermute x1, waiting for transfers between devices, per_device(): back = lax.ppermute(back, 'depth', list(HOST.items()))  8.49 us
    pallas_call x1, Pallas kernels, attention(): call(attention_kernel, shapes, specs, outs, scratch, flops=3 * 10 ** 9, m...  6.89 us
    pallas_call x1, Pallas kernels, root_grad(): call(root_kernel, shapes, specs, outs, scratch, flops=10 ** 9, moved=6 *...  6.71 us
    pallas_call x1, Pallas kernels, join(): call(join_kernel, shapes, specs, outs, grid=(HEADS,), moved=6 * 2 ** 20)  3.74 us
    ppermute x2, starting transfers between devices, per_device(): lax.ppermute(each, 'depth', [(host, here) for here, host in HOST.items()])  2.58 us
    ppermute x1, starting transfers between devices, per_device(): back = lax.ppermute(back, 'depth', list(HOST.items()))  2.48 us
  transfers between devices with their start and end apart: 7, of which 5 were waited for; matrix products, arithmetic and copies ran while one was open for 1% of the time, Pallas kernels for 11%

profile of v4, /device:TPU:32, one launch (start us, length us, event | category | flops | bytes accessed | tf_op | source)
XLA Modules:
  0.0 113.0 jit_solution(7027571144971270920)
XLA Ops:
  0.6 2.1 %shard_map.85 = (bf16[1024,128]{1,0:T(8,128)(2,1)}, bf16[128,2304]{1,0:T(8,128)(2,1)S(1)}, bf16[128,2304]{1,0:T(8,128)(2,1)S(1)}) custom-call(bf16[128,4096]{1,0:T(8,128)(2,1)} %query_ref.5, bf16[128,4096]{1,0:T(8,128)(2,1)} %grad_ref.5, bf16[128,512]{1,0:T(8,128)(2,1)} %key_ref.3, bf16[128,512]{1,0:T(8,128)(2,1)} %value_ref.3), custom_call_target="tpu_custom_call" | custom-call | tf_op jit(solution)/shard_map/pallas_call | solution.py:113
  2.7 1.3 %collective-permute-start = (bf16[128,2304]{1,0:T(8,128)(2,1)S(1)}, bf16[128,2304]{1,0:T(8,128)(2,1)S(1)}, u32[]{:S(2)}, u32[]{:S(2)}) collective-permute-start(bf16[128,2304]{1,0:T(8,128)(2,1)S(1)} %get-tuple-element.23), channel_id=1, source_target_pairs={{192,0},{128,64},{193,1},{129,65},{194,2},{130,66},{195,3},{131,67... | collective-permute-start | bytes 1769480 | tf_op jit(solution)/shard_map/ppermute | solution.py:541
  4.0 16.1 %all-to-all-start = ((bf16[128,8,128]{2,1,0:T(8,128)(2,1)}), bf16[128,8,128]{2,1,0:T(8,128)(2,1)S(1)}, u32[]{:S(2)}, u32[]{:S(2)}) async-start(bf16[128,8,128]{2,1,0:T(8,128)(2,1)} %bitcast.2), calls=%async_computation | async-start | bytes 524288 | tf_op jit(solution)/shard_map/all_to_all | solution.py:533
  20.1 1.3 %collective-permute-start.1 = (bf16[128,2304]{1,0:T(8,128)(2,1)S(1)}, bf16[128,2304]{1,0:T(8,128)(2,1)S(1)}, u32[]{:S(2)}, u32[]{:S(2)}) collective-permute-start(bf16[128,2304]{1,0:T(8,128)(2,1)S(1)} %get-tuple-element.24), channel_id=1, source_target_pairs={{192,0},{128,64},{193,1},{129,65},{194,2},{130,66},{195,3},{131,67... | collective-permute-start | bytes 1769480 | tf_op jit(solution)/shard_map/ppermute | solution.py:541
  21.4 0.6 pad_add_fusion.place_ref
  22.1 12.3 %all-to-all-done = bf16[128,8,128]{2,1,0:T(8,128)(2,1)S(1)} async-done(((bf16[128,8,128]{2,1,0:T(8,128)(2,1)}), bf16[128,8,128]{2,1,0:T(8,128)(2,1)S(1)}, u32[]{:S(2)}, u32[]{:S(2)}) %all-to-all-start) | async-done | bytes 262176 | tf_op jit(solution)/shard_map/all_to_all | solution.py:533
  34.4 1.8 %shard_map.87.picked_ref = bf16[1536,128]{1,0:T(8,128)(2,1)} custom-call(s32[3,32]{1,0:T(4,128)} %parents_ref.5, bf16[1024,128]{1,0:T(8,128)(2,1)S(1)} %bitcast.12), custom_call_target="tpu_custom_call" | custom-call | tf_op jit(solution)/shard_map/pallas_call | solution.py:158
  36.2 6.6 %all-to-all-start.1 = ((bf16[128,3,4,128]{3,2,1,0:T(4,128)(2,1)}), bf16[128,3,4,128]{3,2,1,0:T(4,128)(2,1)S(1)}, u32[]{:S(2)}, u32[]{:S(2)}) async-start(bf16[128,3,4,128]{3,2,1,0:T(4,128)(2,1)} %bitcast.4), calls=%async_computation.1 | async-start | bytes 786432 | tf_op jit(solution)/shard_map/all_to_all | solution.py:533
  42.8 0.0 collective-permute-done.after_ref.first_ref
  42.8 0.0 collective-permute-done.1.second_ref
  42.8 6.7 %shard_map.88 = (bf16[128,4096]{1,0:T(8,128)(2,1)}, f32[128,512]{1,0:T(8,128)}, f32[128,512]{1,0:T(8,128)}, bf16[2,128,1024]{2,1,0:T(8,128)(2,1)S(1)}, bf16[2,12...) custom-call(s32[2]{0:T(128)} %pad_add_fusion.place_ref, ...), custom_call_target="tpu_custom_call" | custom-call | flops 1000000000 | bytes 6291456 | tf_op jit(solution)/shard_map/pallas_call | solution.py:320
  49.6 9.6 %all-to-all-done.1 = bf16[128,3,4,128]{3,2,1,0:T(4,128)(2,1)S(1)} async-done(((bf16[128,3,4,128]{3,2,1,0:T(4,128)(2,1)}), bf16[128,3,4,128]{3,2,1,0:T(4,128)(2,1)S(1)}, u32[]{:S(2)}, u32[]{:S(2)}) %all-to-all-start.1) | async-done | bytes 393248 | tf_op jit(solution)/shard_map/all_to_all | solution.py:533
  59.1 6.9 %shard_map.89 = (bf16[128,4096]{1,0:T(8,128)(2,1)}, f32[128,512]{1,0:T(8,128)}, f32[128,512]{1,0:T(8,128)}, bf16[128,2560]{1,0:T(8,128)(2,1)}, bf16[1536,128]{1,0:T(8,128)(2,1)}) custom-call(s32[2]{0:T(128)} %pad_add_fusion.place_ref, s32[3,32]{1,0:T(4,128)} %parents_ref.5, s32[4,32]{1,0:T(4,128)} %lengths_ref.3, bf16[128,4096]{1,0:T(8,128)(2,1)} %query_ref.5, ...), custom_call_target="tpu_custom_call" | custom-call | flops 3000000000 | bytes 10485760 | tf_op jit(solution)/shard_map/pallas_call | solution.py:471
  66.0 2.5 %collective-permute-start.2 = (bf16[128,2560]{1,0:T(8,128)(2,1)}, bf16[128,2560]{1,0:T(8,128)(2,1)S(1)}, u32[]{:S(2)}, u32[]{:S(2)}) collective-permute-start(bf16[128,2560]{1,0:T(8,128)(2,1)} %get-tuple-element.32), channel_id=1, source_target_pairs={{0,192},{64,128},{1,193},{65,129},{2,194},{66,130},{3,195},{67,131... | collective-permute-start | bytes 1966088 | tf_op jit(solution)/shard_map/ppermute | solution.py:549
  68.5 6.9 %all-to-all-start.2 = ((bf16[128,3,4,128]{3,2,1,0:T(4,128)(2,1)}), bf16[128,3,4,128]{3,2,1,0:T(4,128)(2,1)S(1)}, u32[]{:S(2)}, u32[]{:S(2)}) async-start(bf16[128,3,4,128]{3,2,1,0:T(4,128)(2,1)} %bitcast.6), calls=%async_computation.2 | async-start | bytes 786432 | tf_op jit(solution)/shard_map/all_to_all | solution.py:533
  75.4 8.5 %collective-permute-done.2.back_ref.back_key_ref.back_value_ref.after_ref = bf16[128,2560]{1,0:T(8,128)(2,1)S(1)} collective-permute-done((bf16[128,2560]{1,0:T(8,128)(2,1)}, bf16[128,2560]{1,0:T(8,128)(2,1)S(1)}, u32[]{:S(2)}, u32[]{:S(2)}) %collective-permute-start.2) | collective-permute-done | bytes 655392 | tf_op jit(solution)/shard_map/ppermute | solution.py:549
  83.9 6.6 %all-to-all-done.2 = bf16[128,3,4,128]{3,2,1,0:T(4,128)(2,1)S(1)} async-done(((bf16[128,3,4,128]{3,2,1,0:T(4,128)(2,1)}), bf16[128,3,4,128]{3,2,1,0:T(4,128)(2,1)S(1)}, u32[]{:S(2)}, u32[]{:S(2)}) %all-to-all-start.2) | async-done | bytes 393248 | tf_op jit(solution)/shard_map/all_to_all | solution.py:533
  90.5 1.8 %shard_map.92 = bf16[1024,128]{1,0:T(8,128)(2,1)} custom-call(s32[3,32]{1,0:T(4,128)} %parents_ref.5, bf16[1536,128]{1,0:T(8,128)(2,1)S(1)} %bitcast.10, f32[8,128]{1,0:T(8,128)S(1)} %shard_map.91.after_ref), custom_call_target="tpu_custom_call" | custom-call | tf_op jit(solution)/shard_map/pallas_call | solution.py:193
  92.3 6.6 %all-to-all-start.3 = ((bf16[128,8,128]{2,1,0:T(8,128)(2,1)}), bf16[128,8,128]{2,1,0:T(8,128)(2,1)S(1)}, u32[]{:S(2)}, u32[]{:S(2)}) async-start(bf16[128,8,128]{2,1,0:T(8,128)(2,1)} %bitcast.8), calls=%async_computation.3 | async-start | bytes 524288 | tf_op jit(solution)/shard_map/all_to_all | solution.py:533
  98.9 3.7 %shard_map.90 = (bf16[128,4096]{1,0:T(8,128)(2,1)}, f32[128,512]{1,0:T(8,128)S(1)}, f32[128,512]{1,0:T(8,128)S(1)}) custom-call(s32[2]{0:T(128)} %pad_add_fusion.place_ref, bf16[128,4096]{1,0:T(8,128)(2,1)} %get-tuple-element.26.root_ref, bf16[128,4096]{1,0:T(8,128)(2,1)} %get-tuple-element.31.here_ref, ...), custom_call_target="tpu_custom_call" | custom-call | bytes 6291456 | tf_op jit(solution)/shard_map/pallas_call | solution.py:512
  102.7 9.5 %all-to-all-done.3 = bf16[128,8,128]{2,1,0:T(8,128)(2,1)S(1)} async-done(((bf16[128,8,128]{2,1,0:T(8,128)(2,1)}), bf16[128,8,128]{2,1,0:T(8,128)(2,1)S(1)}, u32[]{:S(2)}, u32[]{:S(2)}) %all-to-all-start.3) | async-done | bytes 262176 | tf_op jit(solution)/shard_map/all_to_all | solution.py:533
  112.1 0.9 shard_map.93
  (2 shorter events, 0.0 us)
Async XLA Ops:
  2.7 40.1 %collective-permute-start = (bf16[128,2304]{1,0:T(8,128)(2,1)S(1)}, bf16[128,2304]{1,0:T(8,128)(2,1)S(1)}, u32[]{:S(2)}, u32[]{:S(2)}) collective-permute-start(bf16[128,2304]{1,0:T(8,128)(2,1)S(1)} %get-tuple-element.23), channel_id=1, source_target_pairs={{192,0},{128,64},{193,1},{129,65},{194,2},{130,66},{195,3},{131,67... | collective-permute-start | bytes 1769480 | tf_op jit(solution)/shard_map/ppermute | solution.py:541
  4.0 30.3 %all-to-all-start = ((bf16[128,8,128]{2,1,0:T(8,128)(2,1)}), bf16[128,8,128]{2,1,0:T(8,128)(2,1)S(1)}, u32[]{:S(2)}, u32[]{:S(2)}) async-start(bf16[128,8,128]{2,1,0:T(8,128)(2,1)} %bitcast.2), calls=%async_computation | async-start | bytes 524288 | tf_op jit(solution)/shard_map/all_to_all | solution.py:533
  20.1 22.7 %collective-permute-start.1 = (bf16[128,2304]{1,0:T(8,128)(2,1)S(1)}, bf16[128,2304]{1,0:T(8,128)(2,1)S(1)}, u32[]{:S(2)}, u32[]{:S(2)}) collective-permute-start(bf16[128,2304]{1,0:T(8,128)(2,1)S(1)} %get-tuple-element.24), channel_id=1, source_target_pairs={{192,0},{128,64},{193,1},{129,65},{194,2},{130,66},{195,3},{131,67... | collective-permute-start | bytes 1769480 | tf_op jit(solution)/shard_map/ppermute | solution.py:541
  36.2 23.0 %all-to-all-start.1 = ((bf16[128,3,4,128]{3,2,1,0:T(4,128)(2,1)}), bf16[128,3,4,128]{3,2,1,0:T(4,128)(2,1)S(1)}, u32[]{:S(2)}, u32[]{:S(2)}) async-start(bf16[128,3,4,128]{3,2,1,0:T(4,128)(2,1)} %bitcast.4), calls=%async_computation.1 | async-start | bytes 786432 | tf_op jit(solution)/shard_map/all_to_all | solution.py:533
  66.0 17.8 %collective-permute-start.2 = (bf16[128,2560]{1,0:T(8,128)(2,1)}, bf16[128,2560]{1,0:T(8,128)(2,1)S(1)}, u32[]{:S(2)}, u32[]{:S(2)}) collective-permute-start(bf16[128,2560]{1,0:T(8,128)(2,1)} %get-tuple-element.32), channel_id=1, source_target_pairs={{0,192},{64,128},{1,193},{65,129},{2,194},{66,130},{3,195},{67,131... | collective-permute-start | bytes 1966088 | tf_op jit(solution)/shard_map/ppermute | solution.py:549
  68.5 21.9 %all-to-all-start.2 = ((bf16[128,3,4,128]{3,2,1,0:T(4,128)(2,1)}), bf16[128,3,4,128]{3,2,1,0:T(4,128)(2,1)S(1)}, u32[]{:S(2)}, u32[]{:S(2)}) async-start(bf16[128,3,4,128]{3,2,1,0:T(4,128)(2,1)} %bitcast.6), calls=%async_computation.2 | async-start | bytes 786432 | tf_op jit(solution)/shard_map/all_to_all | solution.py:533
  92.3 19.9 %all-to-all-start.3 = ((bf16[128,8,128]{2,1,0:T(8,128)(2,1)}), bf16[128,8,128]{2,1,0:T(8,128)(2,1)S(1)}, u32[]{:S(2)}, u32[]{:S(2)}) async-start(bf16[128,8,128]{2,1,0:T(8,128)(2,1)} %bitcast.8), calls=%async_computation.3 | async-start | bytes 524288 | tf_op jit(solution)/shard_map/all_to_all | solution.py:533

commit v5 on v4

--- a/solution.py
+++ b/solution.py
@@ -84,7 +84,9 @@
     return pltpu.VMEM((rows, HD), jnp.float32)
 
 
-def pack_kernel(query_ref, grad_ref, key_ref, value_ref, out_ref, first_ref, second_ref, keys, values, wide, sems):
+def pack_kernel(
+    query_ref, grad_ref, key_ref, value_ref, out_ref, first_ref, second_ref, keys, values, packed, wide, sems
+):
     half = HALF * GROUP
     copies = [
         pltpu.make_async_copy(key_ref, keys, sems.at[0]),
@@ -96,21 +98,24 @@
         copy.start()
     for copy in copies[:2]:
         copy.wait()
-    first_ref[:, half:] = keys[:, HALF * HD :]
-    second_ref[:, half:] = values[:, HALF * HD :]
     for head in range(HEADS):
         lanes = slice(head * HD, (head + 1) * HD)
         wide[pl.ds(2 * head, ROWS, stride=TILE), :] = keys[:, lanes].astype(jnp.float32)
         wide[pl.ds(2 * head + 1, ROWS, stride=TILE), :] = values[:, lanes].astype(jnp.float32)
-    out_ref[...] = wide[...].astype(jnp.bfloat16)
-    for copy in copies[2:]:
+    packed[...] = wide[...].astype(jnp.bfloat16)
+    out = pltpu.make_async_copy(packed, out_ref, sems.at[0])
+    out.start()
+    first_ref[:, half:] = keys[:, HALF * HD :]
+    second_ref[:, half:] = values[:, HALF * HD :]
+    for copy in copies[2:] + [out]:
         copy.wait()
 
 
 def pack(queries, grad_output, keys, values):
-    shapes = (near(ROWS * TILE, HD), near(ROWS, LENT), near(ROWS, LENT))
-    scratch = [near(ROWS, WIDTH), near(ROWS, WIDTH), wide_scratch(ROWS * TILE), pltpu.SemaphoreType.DMA((4,))]
-    return call(pack_kernel, shapes, [ANY] * 4, (VMEM,) * 3, scratch)(*in_far(queries, grad_output, keys, values))
+    shapes = (far(ROWS * TILE, HD), near(ROWS, LENT), near(ROWS, LENT))
+    scratch = [near(ROWS, WIDTH), near(ROWS, WIDTH), near(ROWS * TILE, HD), wide_scratch(ROWS * TILE)]
+    scratch.append(pltpu.SemaphoreType.DMA((4,)))
+    return call(pack_kernel, shapes, [ANY] * 4, (ANY, VMEM, VMEM), scratch)(*in_far(queries, grad_output, keys, values))
 
 
 def chain(parents_ref, level, seg):
@@ -149,7 +154,7 @@
         picked[rows_of(1, seg, 0, 8), :] = wide[tile_at(0, only), :]
         return carry
 
-    lax.fori_loop(0, SEGS, step, 0, unroll=8)
+    lax.fori_loop(0, SEGS, step, 0, unroll=True)
     out_ref[...] = picked[...].astype(jnp.bfloat16)
 
 
@@ -180,7 +185,7 @@
         from_one[tile_at(0, only), :] += rows(1, seg, 0, 8)
         return carry
 
-    lax.fori_loop(0, SEGS, step, 0, unroll=8)
+    lax.fori_loop(0, SEGS, step, 0, unroll=True)
     size = SEGS * TILE
     out_ref[0:size] = (from_three[0][...] + from_two[0][...] + from_one[...]).astype(jnp.bfloat16)
     out_ref[size : 2 * size] = (from_three[1][...] + from_two[1][...]).astype(jnp.bfloat16)
@@ -325,7 +330,7 @@
 def attention_kernel(
     place_ref, parents_ref, lengths_ref, query_ref, grad_ref, query, grad, keys, values, held,
     gquery_ref, gkey_ref, gvalue_ref, back_ref, terms_ref,
-    late_query, late_grad, gquery, gkey, gvalue, back_own, wide, sums, in_sems, out_sems, own_sem,
+    late_query, late_grad, gquery, gkey, gvalue, back_own, wide, sums, terms_low, in_sems, out_sems, own_sems,
 ):
     level_here = place_ref[0]
     seg = place_ref[1]
@@ -427,34 +432,41 @@
         work_on(1, (1, 2, 3), own, own, own)
         send(1, (1, 2, 3))
 
+    terms_low[...] = sums[...].astype(jnp.bfloat16)
+    terms_out = pltpu.make_async_copy(terms_low, terms_ref, own_sems.at[0])
+    terms_out.start()
+
     def hand_out(level):
+        copies = []
         for index, (guest, head, _) in enumerate(TASKS[level]):
             if guest:
                 place = head - HALF
                 back_own[:, place * HD : (place + 1) * HD] = gkey[index].astype(jnp.bfloat16)
                 back_own[:, (HALF + place) * HD : (HALF + place + 1) * HD] = gvalue[index].astype(jnp.bfloat16)
             else:
-                gkey_ref[:, head * HD : (head + 1) * HD] = gkey[index]
-                gvalue_ref[:, head * HD : (head + 1) * HD] = gvalue[index]
-        own = pltpu.make_async_copy(back_own, lanes_at(back_ref, BACK_KEY, 2 * HALF * HD), own_sem)
+                for i, (source, target) in enumerate(((gkey, gkey_ref), (gvalue, gvalue_ref))):
+                    copies.append(
+                        pltpu.make_async_copy(source.at[index], lanes_at(target, head * HD), in_sems.at[index, i])
+                    )
         if level in HOST:
-            own.start()
-            own.wait()
-        for index in range(len(TASKS[level])):
-            result(level, index).wait()
-
-    terms_ref[...] = sums[...].astype(jnp.bfloat16)
+            copies.append(pltpu.make_async_copy(back_own, lanes_at(back_ref, BACK_KEY, 2 * HALF * HD), own_sems.at[1]))
+        for copy in copies:
+            copy.start()
+        for copy in copies + [result(level, index) for index in range(len(TASKS[level]))]:
+            copy.wait()
+
     for level in range(LEVELS):
         at_level(level, lambda level=level: hand_out(level))
+    terms_out.wait()
 
 
 def attention(place, parents, lengths, queries, grad_output, tasks, held):
     shapes = (
         far(ROWS, HEADS * GROUP), far(ROWS, WIDTH, dtype=jnp.float32), far(ROWS, WIDTH, dtype=jnp.float32),
-        far(ROWS, BACK_VALUE + HALF * HD), near(ROWS * PIECE, HD),
+        far(ROWS, BACK_VALUE + HALF * HD), far(ROWS * PIECE, HD),
     )
     specs = [SMEM] * 3 + [ANY] * 2 + [VMEM] * 5
-    outs = (ANY, VMEM, VMEM, ANY, VMEM)
+    outs = (ANY,) * 5
     scratch = [
         near(MOST, ROWS, GROUP),
         near(MOST, ROWS, GROUP),
@@ -464,9 +476,10 @@
         near(ROWS, 2 * HALF * HD),
         wide_scratch(ROWS * PIECE),
         wide_scratch(ROWS * PIECE),
+        near(ROWS * PIECE, HD),
         pltpu.SemaphoreType.DMA((MOST, 2)),
         pltpu.SemaphoreType.DMA((MOST,)),
-        pltpu.SemaphoreType.DMA(()),
+        pltpu.SemaphoreType.DMA((2,)),
     ]
     return call(attention_kernel, shapes, specs, outs, scratch, flops=3 * 10**9, moved=10 * 2**20)(
         place, parents, lengths, *in_far(queries, grad_output), *in_near(*tasks, held)
@@ -536,7 +549,7 @@
 
 def per_device(queries, key_states, value_states, grad_output, parents, lengths):
     place = jnp.stack([lax.axis_index("depth"), lax.axis_index("seg")]).astype(jnp.int32)
-    place, parents, lengths = in_far(place, parents, lengths)
+    place, parents, lengths = [pltpu.with_memory_space_constraint(x, pltpu.SMEM) for x in (place, parents, lengths)]
     packed, *lent = pack(queries, grad_output, key_states, value_states)
     first, second = [lax.ppermute(each, "depth", [(host, here) for here, host in HOST.items()]) for each in lent]
     picked = select(parents, exchange(packed, TILE))

time: 114 us -> 112 us (0.982)
  Pallas kernels: 23.9 us -> 22.2 us
  transfers between devices with their start and end apart: 7 -> 7, of which waited for: 5 -> 5; matrix products, arithmetic and copies ran while one was open for 1% -> 0% of each run, Pallas kernels for 11% -> 11%
where the time goes in v5:
time: 112 us
  waiting for transfers between devices  46.5 us (42%)
  starting transfers between devices  41.5 us (37%)
  Pallas kernels  22.2 us (20%)
    all_to_all x4, waiting for transfers between devices, exchange(): lax.all_to_all(pieces.reshape(DEVICES, *tile, HD), ('depth', 'seg'), 0, 0...  38 us
    all_to_all x4, starting transfers between devices, exchange(): lax.all_to_all(pieces.reshape(DEVICES, *tile, HD), ('depth', 'seg'), 0, 0...  36.2 us
    ppermute x1, waiting for transfers between devices, per_device(): back = lax.ppermute(back, 'depth', list(HOST.items()))  8.49 us
    pallas_call x1, Pallas kernels, root_grad(): call(root_kernel, shapes, specs, outs, scratch, flops=10 ** 9, moved=6 *...  6.57 us
    pallas_call x1, Pallas kernels, attention(): call(attention_kernel, shapes, specs, outs, scratch, flops=3 * 10 ** 9, m...  5.98 us
    pallas_call x1, Pallas kernels, join(): call(join_kernel, shapes, specs, outs, grid=(HEADS,), moved=6 * 2 ** 20)  3.74 us
    ppermute x1, starting transfers between devices, per_device(): back = lax.ppermute(back, 'depth', list(HOST.items()))  2.64 us
    ppermute x2, starting transfers between devices, per_device(): lax.ppermute(each, 'depth', [(host, here) for here, host in HOST.items()])  2.58 us
  transfers between devices with their start and end apart: 7, of which 5 were waited for; matrix products, arithmetic and copies ran while one was open for 0% of the time, Pallas kernels for 11%

profile of v5, /device:TPU:32, one launch (start us, length us, event | category | flops | bytes accessed | tf_op | source)
XLA Modules:
  0.0 111.7 jit_solution(7621781200630650888)
XLA Ops:
  0.6 1.9 %shard_map.85 = (bf16[1024,128]{1,0:T(8,128)(2,1)}, bf16[128,2304]{1,0:T(8,128)(2,1)S(1)}, bf16[128,2304]{1,0:T(8,128)(2,1)S(1)}) custom-call(bf16[128,4096]{1,0:T(8,128)(2,1)} %query_ref.5, bf16[128,4096]{1,0:T(8,128)(2,1)} %grad_ref.5, bf16[128,512]{1,0:T(8,128)(2,1)} %key_ref.3, bf16[128,512]{1,0:T(8,128)(2,1)} %value_ref.3), custom_call_target="tpu_custom_call" | custom-call | tf_op jit(solution)/shard_map/pallas_call | solution.py:118
  2.5 1.3 %collective-permute-start = (bf16[128,2304]{1,0:T(8,128)(2,1)S(1)}, bf16[128,2304]{1,0:T(8,128)(2,1)S(1)}, u32[]{:S(2)}, u32[]{:S(2)}) collective-permute-start(bf16[128,2304]{1,0:T(8,128)(2,1)S(1)} %get-tuple-element.23), channel_id=1, source_target_pairs={{192,0},{128,64},{193,1},{129,65},{194,2},{130,66},{195,3},{131,67... | collective-permute-start | bytes 1769480 | tf_op jit(solution)/shard_map/ppermute | solution.py:554
  3.8 16.1 %all-to-all-start = ((bf16[128,8,128]{2,1,0:T(8,128)(2,1)}), bf16[128,8,128]{2,1,0:T(8,128)(2,1)S(1)}, u32[]{:S(2)}, u32[]{:S(2)}) async-start(bf16[128,8,128]{2,1,0:T(8,128)(2,1)} %bitcast.15), calls=%async_computation | async-start | bytes 524288 | tf_op jit(solution)/shard_map/all_to_all | solution.py:546
  19.9 1.3 %collective-permute-start.1 = (bf16[128,2304]{1,0:T(8,128)(2,1)S(1)}, bf16[128,2304]{1,0:T(8,128)(2,1)S(1)}, u32[]{:S(2)}, u32[]{:S(2)}) collective-permute-start(bf16[128,2304]{1,0:T(8,128)(2,1)S(1)} %get-tuple-element.24), channel_id=1, source_target_pairs={{192,0},{128,64},{193,1},{129,65},{194,2},{130,66},{195,3},{131,67... | collective-permute-start | bytes 1769480 | tf_op jit(solution)/shard_map/ppermute | solution.py:554
  21.2 0.0 copy-start
  21.2 0.1 pad_add_fusion.place_ref
  21.3 12.8 %all-to-all-done = bf16[128,8,128]{2,1,0:T(8,128)(2,1)S(1)} async-done(((bf16[128,8,128]{2,1,0:T(8,128)(2,1)}), bf16[128,8,128]{2,1,0:T(8,128)(2,1)S(1)}, u32[]{:S(2)}, u32[]{:S(2)}) %all-to-all-start) | async-done | bytes 262176 | tf_op jit(solution)/shard_map/all_to_all | solution.py:546
  34.2 0.0 copy-done
  34.2 1.6 %shard_map.87.picked_ref = bf16[1536,128]{1,0:T(8,128)(2,1)} custom-call(s32[3,32]{1,0:T(4,128)S(1)} %copy-done, bf16[1024,128]{1,0:T(8,128)(2,1)S(1)} %bitcast.12), custom_call_target="tpu_custom_call" | custom-call | tf_op jit(solution)/shard_map/pallas_call | solution.py:163
  35.8 6.6 %all-to-all-start.1 = ((bf16[128,3,4,128]{3,2,1,0:T(4,128)(2,1)}), bf16[128,3,4,128]{3,2,1,0:T(4,128)(2,1)S(1)}, u32[]{:S(2)}, u32[]{:S(2)}) async-start(bf16[128,3,4,128]{3,2,1,0:T(4,128)(2,1)} %bitcast.4), calls=%async_computation.1 | async-start | bytes 786432 | tf_op jit(solution)/shard_map/all_to_all | solution.py:546
  42.4 0.0 copy-start.1
  42.4 0.0 collective-permute-done.after_ref.first_ref
  42.4 0.0 collective-permute-done.1.second_ref
  42.4 0.6 copy-done.1
  43.1 6.6 %shard_map.88 = (bf16[128,4096]{1,0:T(8,128)(2,1)}, f32[128,512]{1,0:T(8,128)}, f32[128,512]{1,0:T(8,128)}, bf16[2,128,1024]{2,1,0:T(8,128)(2,1)S(1)}, bf16[2,12...) custom-call(s32[2]{0:T(128)S(1)} %pad_add_fusion.place_ref, ...), custom_call_target="tpu_custom_call" | custom-call | flops 1000000000 | bytes 6291456 | tf_op jit(solution)/shard_map/pallas_call | solution.py:325
  49.7 9.1 %all-to-all-done.1 = bf16[128,3,4,128]{3,2,1,0:T(4,128)(2,1)S(1)} async-done(((bf16[128,3,4,128]{3,2,1,0:T(4,128)(2,1)}), bf16[128,3,4,128]{3,2,1,0:T(4,128)(2,1)S(1)}, u32[]{:S(2)}, u32[]{:S(2)}) %all-to-all-start.1) | async-done | bytes 393248 | tf_op jit(solution)/shard_map/all_to_all | solution.py:546
  58.7 6.0 %shard_map.89 = (bf16[128,4096]{1,0:T(8,128)(2,1)}, f32[128,512]{1,0:T(8,128)}, f32[128,512]{1,0:T(8,128)}, bf16[128,2560]{1,0:T(8,128)(2,1)}, bf16[1536,128]{1,0:T(8,128)(2,1)}) custom-call(s32[2]{0:T(128)S(1)} %pad_add_fusion.place_ref, s32[3,32]{1,0:T(4,128)S(1)} %copy-done, s32[4,32]{1,0:T(4,128)S(1)} %copy-done.1, bf16[128,4096]{1,0:T(8,128)(2,1)} %query_ref.5, ...), custom_call_target="tpu_custom_call" | custom-call | flops 3000000000 | bytes 10485760 | tf_op jit(solution)/shard_map/pallas_call | solution.py:484
  64.7 2.6 %collective-permute-start.2 = (bf16[128,2560]{1,0:T(8,128)(2,1)}, bf16[128,2560]{1,0:T(8,128)(2,1)S(1)}, u32[]{:S(2)}, u32[]{:S(2)}) collective-permute-start(bf16[128,2560]{1,0:T(8,128)(2,1)} %get-tuple-element.32), channel_id=1, source_target_pairs={{0,192},{64,128},{1,193},{65,129},{2,194},{66,130},{3,195},{67,131... | collective-permute-start | bytes 1966088 | tf_op jit(solution)/shard_map/ppermute | solution.py:562
  67.4 6.9 %all-to-all-start.2 = ((bf16[128,3,4,128]{3,2,1,0:T(4,128)(2,1)}), bf16[128,3,4,128]{3,2,1,0:T(4,128)(2,1)S(1)}, u32[]{:S(2)}, u32[]{:S(2)}) async-start(bf16[128,3,4,128]{3,2,1,0:T(4,128)(2,1)} %bitcast.14), calls=%async_computation.2 | async-start | bytes 786432 | tf_op jit(solution)/shard_map/all_to_all | solution.py:546
  74.2 8.5 %collective-permute-done.2.back_ref.back_key_ref.back_value_ref.after_ref = bf16[128,2560]{1,0:T(8,128)(2,1)S(1)} collective-permute-done((bf16[128,2560]{1,0:T(8,128)(2,1)}, bf16[128,2560]{1,0:T(8,128)(2,1)S(1)}, u32[]{:S(2)}, u32[]{:S(2)}) %collective-permute-start.2) | collective-permute-done | bytes 655392 | tf_op jit(solution)/shard_map/ppermute | solution.py:562
  82.7 6.6 %all-to-all-done.2 = bf16[128,3,4,128]{3,2,1,0:T(4,128)(2,1)S(1)} async-done(((bf16[128,3,4,128]{3,2,1,0:T(4,128)(2,1)}), bf16[128,3,4,128]{3,2,1,0:T(4,128)(2,1)S(1)}, u32[]{:S(2)}, u32[]{:S(2)}) %all-to-all-start.2) | async-done | bytes 393248 | tf_op jit(solution)/shard_map/all_to_all | solution.py:546
  89.3 1.6 %shard_map.92 = bf16[1024,128]{1,0:T(8,128)(2,1)} custom-call(s32[3,32]{1,0:T(4,128)S(1)} %copy-done, bf16[1536,128]{1,0:T(8,128)(2,1)S(1)} %bitcast.10, f32[8,128]{1,0:T(8,128)S(1)} %shard_map.91.after_ref), custom_call_target="tpu_custom_call" | custom-call | tf_op jit(solution)/shard_map/pallas_call | solution.py:198
  90.9 6.6 %all-to-all-start.3 = ((bf16[128,8,128]{2,1,0:T(8,128)(2,1)}), bf16[128,8,128]{2,1,0:T(8,128)(2,1)S(1)}, u32[]{:S(2)}, u32[]{:S(2)}) async-start(bf16[128,8,128]{2,1,0:T(8,128)(2,1)} %bitcast.8), calls=%async_computation.3 | async-start | bytes 524288 | tf_op jit(solution)/shard_map/all_to_all | solution.py:546
  97.6 3.7 %shard_map.90 = (bf16[128,4096]{1,0:T(8,128)(2,1)}, f32[128,512]{1,0:T(8,128)S(1)}, f32[128,512]{1,0:T(8,128)S(1)}) custom-call(s32[2]{0:T(128)S(1)} %pad_add_fusion.place_ref, bf16[128,4096]{1,0:T(8,128)(2,1)} %get-tuple-element.26.root_ref, bf16[128,4096]{1,0:T(8,128)(2,1)} %get-tuple-element.31.here_ref, ...), custom_call_target="tpu_custom_call" | custom-call | bytes 6291456 | tf_op jit(solution)/shard_map/pallas_call | solution.py:525
  101.3 9.5 %all-to-all-done.3 = bf16[128,8,128]{2,1,0:T(8,128)(2,1)S(1)} async-done(((bf16[128,8,128]{2,1,0:T(8,128)(2,1)}), bf16[128,8,128]{2,1,0:T(8,128)(2,1)S(1)}, u32[]{:S(2)}, u32[]{:S(2)}) %all-to-all-start.3) | async-done | bytes 262176 | tf_op jit(solution)/shard_map/all_to_all | solution.py:546
  110.8 0.9 shard_map.93
  (2 shorter events, 0.0 us)
Async XLA Ops:
  2.5 39.9 %collective-permute-start = (bf16[128,2304]{1,0:T(8,128)(2,1)S(1)}, bf16[128,2304]{1,0:T(8,128)(2,1)S(1)}, u32[]{:S(2)}, u32[]{:S(2)}) collective-permute-start(bf16[128,2304]{1,0:T(8,128)(2,1)S(1)} %get-tuple-element.23), channel_id=1, source_target_pairs={{192,0},{128,64},{193,1},{129,65},{194,2},{130,66},{195,3},{131,67... | collective-permute-start | bytes 1769480 | tf_op jit(solution)/shard_map/ppermute | solution.py:554
  3.8 30.3 %all-to-all-start = ((bf16[128,8,128]{2,1,0:T(8,128)(2,1)}), bf16[128,8,128]{2,1,0:T(8,128)(2,1)S(1)}, u32[]{:S(2)}, u32[]{:S(2)}) async-start(bf16[128,8,128]{2,1,0:T(8,128)(2,1)} %bitcast.15), calls=%async_computation | async-start | bytes 524288 | tf_op jit(solution)/shard_map/all_to_all | solution.py:546
  19.9 22.5 %collective-permute-start.1 = (bf16[128,2304]{1,0:T(8,128)(2,1)S(1)}, bf16[128,2304]{1,0:T(8,128)(2,1)S(1)}, u32[]{:S(2)}, u32[]{:S(2)}) collective-permute-start(bf16[128,2304]{1,0:T(8,128)(2,1)S(1)} %get-tuple-element.24), channel_id=1, source_target_pairs={{192,0},{128,64},{193,1},{129,65},{194,2},{130,66},{195,3},{131,67... | collective-permute-start | bytes 1769480 | tf_op jit(solution)/shard_map/ppermute | solution.py:554
  21.2 12.9 %copy-start = (s32[3,32]{1,0:T(4,128)S(1)}, s32[3,32]{1,0:T(4,128)}, u32[]{:S(2)}) copy-start(s32[3,32]{1,0:T(4,128)} %parents_ref.5) | copy-start | bytes 1156
  35.8 23.0 %all-to-all-start.1 = ((bf16[128,3,4,128]{3,2,1,0:T(4,128)(2,1)}), bf16[128,3,4,128]{3,2,1,0:T(4,128)(2,1)S(1)}, u32[]{:S(2)}, u32[]{:S(2)}) async-start(bf16[128,3,4,128]{3,2,1,0:T(4,128)(2,1)} %bitcast.4), calls=%async_computation.1 | async-start | bytes 786432 | tf_op jit(solution)/shard_map/all_to_all | solution.py:546
  42.4 0.7 copy-start.1
  64.7 18.0 %collective-permute-start.2 = (bf16[128,2560]{1,0:T(8,128)(2,1)}, bf16[128,2560]{1,0:T(8,128)(2,1)S(1)}, u32[]{:S(2)}, u32[]{:S(2)}) collective-permute-start(bf16[128,2560]{1,0:T(8,128)(2,1)} %get-tuple-element.32), channel_id=1, source_target_pairs={{0,192},{64,128},{1,193},{65,129},{2,194},{66,130},{3,195},{67,131... | collective-permute-start | bytes 1966088 | tf_op jit(solution)/shard_map/ppermute | solution.py:562
  67.4 21.9 %all-to-all-start.2 = ((bf16[128,3,4,128]{3,2,1,0:T(4,128)(2,1)}), bf16[128,3,4,128]{3,2,1,0:T(4,128)(2,1)S(1)}, u32[]{:S(2)}, u32[]{:S(2)}) async-start(bf16[128,3,4,128]{3,2,1,0:T(4,128)(2,1)} %bitcast.14), calls=%async_computation.2 | async-start | bytes 786432 | tf_op jit(solution)/shard_map/all_to_all | solution.py:546
  90.9 19.9 %all-to-all-start.3 = ((bf16[128,8,128]{2,1,0:T(8,128)(2,1)}), bf16[128,8,128]{2,1,0:T(8,128)(2,1)S(1)}, u32[]{:S(2)}, u32[]{:S(2)}) async-start(bf16[128,8,128]{2,1,0:T(8,128)(2,1)} %bitcast.8), calls=%async_computation.3 | async-start | bytes 524288 | tf_op jit(solution)/shard_map/all_to_all | solution.py:546

commit v6 on v5

--- a/solution.py
+++ b/solution.py
@@ -81,7 +81,7 @@
 
 
 def wide_scratch(rows):
-    return pltpu.VMEM((rows, HD), jnp.float32)
+    return pltpu.VMEM((rows + 16, HD), jnp.float32)
 
 
 def pack_kernel(
@@ -102,7 +102,7 @@
         lanes = slice(head * HD, (head + 1) * HD)
         wide[pl.ds(2 * head, ROWS, stride=TILE), :] = keys[:, lanes].astype(jnp.float32)
         wide[pl.ds(2 * head + 1, ROWS, stride=TILE), :] = values[:, lanes].astype(jnp.float32)
-    packed[...] = wide[...].astype(jnp.bfloat16)
+    packed[...] = wide[0 : ROWS * TILE].astype(jnp.bfloat16)
     out = pltpu.make_async_copy(packed, out_ref, sems.at[0])
     out.start()
     first_ref[:, half:] = keys[:, HALF * HD :]
@@ -136,7 +136,7 @@
 
 
 def select_kernel(parents_ref, held_ref, out_ref, wide, picked):
-    wide[...] = held_ref[...].astype(jnp.float32)
+    wide[0 : DEVICES * TILE] = held_ref[...].astype(jnp.float32)
 
     def step(seg, carry):
         for upper, ancestor in enumerate(chain(parents_ref, 3, seg)):
@@ -155,7 +155,7 @@
         return carry
 
     lax.fori_loop(0, SEGS, step, 0, unroll=True)
-    out_ref[...] = picked[...].astype(jnp.bfloat16)
+    out_ref[...] = picked[0 : DEVICES * PIECE].astype(jnp.bfloat16)
 
 
 def select(parents, held):
@@ -164,7 +164,7 @@
 
 
 def sum_kernel(parents_ref, terms_ref, after_ref, out_ref, wide, *totals):
-    wide[...] = terms_ref[...].astype(jnp.float32)
+    wide[0 : DEVICES * PIECE] = terms_ref[...].astype(jnp.float32)
     for total in totals:
         total[...] = jnp.zeros_like(total)
     from_three, from_two, from_one = totals[:3], totals[3:5], totals[5]
@@ -194,7 +194,7 @@
 
 
 def sum_terms(parents, terms, after):
-    scratch = [wide_scratch(DEVICES * PIECE)] + [wide_scratch(SEGS * TILE)] * 6
+    scratch = [wide_scratch(DEVICES * PIECE)] + [near(SEGS * TILE, HD, dtype=jnp.float32)] * 6
     return call(sum_kernel, near(DEVICES * TILE, HD), [SMEM, VMEM, ANY], VMEM, scratch)(
         parents, *in_near(terms), after
     )
@@ -357,7 +357,7 @@
 
     for level in (1, 2):
         at_level(level, lambda level=level: fetch_late(level))
-    wide[...] = held[...].astype(jnp.float32)
+    wide[0 : ROWS * PIECE] = held[...].astype(jnp.float32)
 
     def slot_rows(slot, part):
         return pl.ds(2 * slot + part, ROWS, stride=PIECE)
@@ -432,7 +432,7 @@
         work_on(1, (1, 2, 3), own, own, own)
         send(1, (1, 2, 3))
 
-    terms_low[...] = sums[...].astype(jnp.bfloat16)
+    terms_low[...] = sums[0 : ROWS * PIECE].astype(jnp.bfloat16)
     terms_out = pltpu.make_async_copy(terms_low, terms_ref, own_sems.at[0])
     terms_out.start()
 
@@ -526,7 +526,7 @@
 
 
 def finish_kernel(extra_ref, own_key_ref, own_value_ref, key_ref, value_ref, wide):
-    wide[...] = extra_ref[...].astype(jnp.float32)
+    wide[0 : ROWS * TILE] = extra_ref[...].astype(jnp.float32)
     for head in range(HEADS):
         lanes = slice(head * HD, (head + 1) * HD)
         for part, (own_ref, out_ref) in enumerate(((own_key_ref, key_ref), (own_value_ref, value_ref))):

time: 112 us -> 112 us (level)
  no operation moved by 1% of the time
where the time goes in v6:
time: 112 us
  waiting for transfers between devices  46.5 us (42%)
  starting transfers between devices  41.5 us (37%)
  Pallas kernels  22.2 us (20%)
    all_to_all x4, waiting for transfers between devices, exchange(): lax.all_to_all(pieces.reshape(DEVICES, *tile, HD), ('depth', 'seg'), 0, 0...  38 us
    all_to_all x4, starting transfers between devices, exchange(): lax.all_to_all(pieces.reshape(DEVICES, *tile, HD), ('depth', 'seg'), 0, 0...  36.2 us
    ppermute x1, waiting for transfers between devices, per_device(): back = lax.ppermute(back, 'depth', list(HOST.items()))  8.52 us
    pallas_call x1, Pallas kernels, root_grad(): call(root_kernel, shapes, specs, outs, scratch, flops=10 ** 9, moved=6 *...  6.57 us
    pallas_call x1, Pallas kernels, attention(): call(attention_kernel, shapes, specs, outs, scratch, flops=3 * 10 ** 9, m...  5.97 us
    pallas_call x1, Pallas kernels, join(): call(join_kernel, shapes, specs, outs, grid=(HEADS,), moved=6 * 2 ** 20)  3.74 us
    ppermute x1, starting transfers between devices, per_device(): back = lax.ppermute(back, 'depth', list(HOST.items()))  2.65 us
    ppermute x2, starting transfers between devices, per_device(): lax.ppermute(each, 'depth', [(host, here) for here, host in HOST.items()])  2.58 us
  transfers between devices with their start and end apart: 7, of which 5 were waited for; matrix products, arithmetic and copies ran while one was open for 0% of the time, Pallas kernels for 11%

profile of v6, /device:TPU:32, one launch (start us, length us, event | category | flops | bytes accessed | tf_op | source)
XLA Modules:
  0.0 111.7 jit_solution(6602042395245099722)
XLA Ops:
  0.6 1.9 %shard_map.85 = (bf16[1024,128]{1,0:T(8,128)(2,1)}, bf16[128,2304]{1,0:T(8,128)(2,1)S(1)}, bf16[128,2304]{1,0:T(8,128)(2,1)S(1)}) custom-call(bf16[128,4096]{1,0:T(8,128)(2,1)} %query_ref.5, bf16[128,4096]{1,0:T(8,128)(2,1)} %grad_ref.5, bf16[128,512]{1,0:T(8,128)(2,1)} %key_ref.3, bf16[128,512]{1,0:T(8,128)(2,1)} %value_ref.3), custom_call_target="tpu_custom_call" | custom-call | tf_op jit(solution)/shard_map/pallas_call | solution.py:118
  2.5 1.3 %collective-permute-start = (bf16[128,2304]{1,0:T(8,128)(2,1)S(1)}, bf16[128,2304]{1,0:T(8,128)(2,1)S(1)}, u32[]{:S(2)}, u32[]{:S(2)}) collective-permute-start(bf16[128,2304]{1,0:T(8,128)(2,1)S(1)} %get-tuple-element.23), channel_id=1, source_target_pairs={{192,0},{128,64},{193,1},{129,65},{194,2},{130,66},{195,3},{131,67... | collective-permute-start | bytes 1769480 | tf_op jit(solution)/shard_map/ppermute | solution.py:554
  3.8 16.1 %all-to-all-start = ((bf16[128,8,128]{2,1,0:T(8,128)(2,1)}), bf16[128,8,128]{2,1,0:T(8,128)(2,1)S(1)}, u32[]{:S(2)}, u32[]{:S(2)}) async-start(bf16[128,8,128]{2,1,0:T(8,128)(2,1)} %bitcast.15), calls=%async_computation | async-start | bytes 524288 | tf_op jit(solution)/shard_map/all_to_all | solution.py:546
  19.9 1.3 %collective-permute-start.1 = (bf16[128,2304]{1,0:T(8,128)(2,1)S(1)}, bf16[128,2304]{1,0:T(8,128)(2,1)S(1)}, u32[]{:S(2)}, u32[]{:S(2)}) collective-permute-start(bf16[128,2304]{1,0:T(8,128)(2,1)S(1)} %get-tuple-element.24), channel_id=1, source_target_pairs={{192,0},{128,64},{193,1},{129,65},{194,2},{130,66},{195,3},{131,67... | collective-permute-start | bytes 1769480 | tf_op jit(solution)/shard_map/ppermute | solution.py:554
  21.2 0.0 copy-start
  21.2 0.1 pad_add_fusion.place_ref
  21.3 12.8 %all-to-all-done = bf16[128,8,128]{2,1,0:T(8,128)(2,1)S(1)} async-done(((bf16[128,8,128]{2,1,0:T(8,128)(2,1)}), bf16[128,8,128]{2,1,0:T(8,128)(2,1)S(1)}, u32[]{:S(2)}, u32[]{:S(2)}) %all-to-all-start) | async-done | bytes 262176 | tf_op jit(solution)/shard_map/all_to_all | solution.py:546
  34.2 0.0 copy-done
  34.2 1.6 %shard_map.87.picked_ref = bf16[1536,128]{1,0:T(8,128)(2,1)} custom-call(s32[3,32]{1,0:T(4,128)S(1)} %copy-done, bf16[1024,128]{1,0:T(8,128)(2,1)S(1)} %bitcast.12), custom_call_target="tpu_custom_call" | custom-call | tf_op jit(solution)/shard_map/pallas_call | solution.py:163
  35.8 6.6 %all-to-all-start.1 = ((bf16[128,3,4,128]{3,2,1,0:T(4,128)(2,1)}), bf16[128,3,4,128]{3,2,1,0:T(4,128)(2,1)S(1)}, u32[]{:S(2)}, u32[]{:S(2)}) async-start(bf16[128,3,4,128]{3,2,1,0:T(4,128)(2,1)} %bitcast.4), calls=%async_computation.1 | async-start | bytes 786432 | tf_op jit(solution)/shard_map/all_to_all | solution.py:546
  42.4 0.0 copy-start.1
  42.4 0.0 collective-permute-done.after_ref.first_ref
  42.4 0.0 collective-permute-done.1.second_ref
  42.4 0.6 copy-done.1
  43.1 6.6 %shard_map.88 = (bf16[128,4096]{1,0:T(8,128)(2,1)}, f32[128,512]{1,0:T(8,128)}, f32[128,512]{1,0:T(8,128)}, bf16[2,128,1024]{2,1,0:T(8,128)(2,1)S(1)}, bf16[2,12...) custom-call(s32[2]{0:T(128)S(1)} %pad_add_fusion.place_ref, ...), custom_call_target="tpu_custom_call" | custom-call | flops 1000000000 | bytes 6291456 | tf_op jit(solution)/shard_map/pallas_call | solution.py:325
  49.7 9.1 %all-to-all-done.1 = bf16[128,3,4,128]{3,2,1,0:T(4,128)(2,1)S(1)} async-done(((bf16[128,3,4,128]{3,2,1,0:T(4,128)(2,1)}), bf16[128,3,4,128]{3,2,1,0:T(4,128)(2,1)S(1)}, u32[]{:S(2)}, u32[]{:S(2)}) %all-to-all-start.1) | async-done | bytes 393248 | tf_op jit(solution)/shard_map/all_to_all | solution.py:546
  58.7 6.0 %shard_map.89 = (bf16[128,4096]{1,0:T(8,128)(2,1)}, f32[128,512]{1,0:T(8,128)}, f32[128,512]{1,0:T(8,128)}, bf16[128,2560]{1,0:T(8,128)(2,1)}, bf16[1536,128]{1,0:T(8,128)(2,1)}) custom-call(s32[2]{0:T(128)S(1)} %pad_add_fusion.place_ref, s32[3,32]{1,0:T(4,128)S(1)} %copy-done, s32[4,32]{1,0:T(4,128)S(1)} %copy-done.1, bf16[128,4096]{1,0:T(8,128)(2,1)} %query_ref.5, ...), custom_call_target="tpu_custom_call" | custom-call | flops 3000000000 | bytes 10485760 | tf_op jit(solution)/shard_map/pallas_call | solution.py:484
  64.7 2.7 %collective-permute-start.2 = (bf16[128,2560]{1,0:T(8,128)(2,1)}, bf16[128,2560]{1,0:T(8,128)(2,1)S(1)}, u32[]{:S(2)}, u32[]{:S(2)}) collective-permute-start(bf16[128,2560]{1,0:T(8,128)(2,1)} %get-tuple-element.32), channel_id=1, source_target_pairs={{0,192},{64,128},{1,193},{65,129},{2,194},{66,130},{3,195},{67,131... | collective-permute-start | bytes 1966088 | tf_op jit(solution)/shard_map/ppermute | solution.py:562
  67.4 6.9 %all-to-all-start.2 = ((bf16[128,3,4,128]{3,2,1,0:T(4,128)(2,1)}), bf16[128,3,4,128]{3,2,1,0:T(4,128)(2,1)S(1)}, u32[]{:S(2)}, u32[]{:S(2)}) async-start(bf16[128,3,4,128]{3,2,1,0:T(4,128)(2,1)} %bitcast.14), calls=%async_computation.2 | async-start | bytes 786432 | tf_op jit(solution)/shard_map/all_to_all | solution.py:546
  74.2 8.5 %collective-permute-done.2.back_ref.back_key_ref.back_value_ref.after_ref = bf16[128,2560]{1,0:T(8,128)(2,1)S(1)} collective-permute-done((bf16[128,2560]{1,0:T(8,128)(2,1)}, bf16[128,2560]{1,0:T(8,128)(2,1)S(1)}, u32[]{:S(2)}, u32[]{:S(2)}) %collective-permute-start.2) | collective-permute-done | bytes 655392 | tf_op jit(solution)/shard_map/ppermute | solution.py:562
  82.7 6.6 %all-to-all-done.2 = bf16[128,3,4,128]{3,2,1,0:T(4,128)(2,1)S(1)} async-done(((bf16[128,3,4,128]{3,2,1,0:T(4,128)(2,1)}), bf16[128,3,4,128]{3,2,1,0:T(4,128)(2,1)S(1)}, u32[]{:S(2)}, u32[]{:S(2)}) %all-to-all-start.2) | async-done | bytes 393248 | tf_op jit(solution)/shard_map/all_to_all | solution.py:546
  89.3 1.6 %shard_map.92 = bf16[1024,128]{1,0:T(8,128)(2,1)} custom-call(s32[3,32]{1,0:T(4,128)S(1)} %copy-done, bf16[1536,128]{1,0:T(8,128)(2,1)S(1)} %bitcast.10, f32[8,128]{1,0:T(8,128)S(1)} %shard_map.91.after_ref), custom_call_target="tpu_custom_call" | custom-call | tf_op jit(solution)/shard_map/pallas_call | solution.py:198
  91.0 6.6 %all-to-all-start.3 = ((bf16[128,8,128]{2,1,0:T(8,128)(2,1)}), bf16[128,8,128]{2,1,0:T(8,128)(2,1)S(1)}, u32[]{:S(2)}, u32[]{:S(2)}) async-start(bf16[128,8,128]{2,1,0:T(8,128)(2,1)} %bitcast.8), calls=%async_computation.3 | async-start | bytes 524288 | tf_op jit(solution)/shard_map/all_to_all | solution.py:546
  97.6 3.7 %shard_map.90 = (bf16[128,4096]{1,0:T(8,128)(2,1)}, f32[128,512]{1,0:T(8,128)S(1)}, f32[128,512]{1,0:T(8,128)S(1)}) custom-call(s32[2]{0:T(128)S(1)} %pad_add_fusion.place_ref, bf16[128,4096]{1,0:T(8,128)(2,1)} %get-tuple-element.26.root_ref, bf16[128,4096]{1,0:T(8,128)(2,1)} %get-tuple-element.31.here_ref, ...), custom_call_target="tpu_custom_call" | custom-call | bytes 6291456 | tf_op jit(solution)/shard_map/pallas_call | solution.py:525
  101.3 9.5 %all-to-all-done.3 = bf16[128,8,128]{2,1,0:T(8,128)(2,1)S(1)} async-done(((bf16[128,8,128]{2,1,0:T(8,128)(2,1)}), bf16[128,8,128]{2,1,0:T(8,128)(2,1)S(1)}, u32[]{:S(2)}, u32[]{:S(2)}) %all-to-all-start.3) | async-done | bytes 262176 | tf_op jit(solution)/shard_map/all_to_all | solution.py:546
  110.8 0.9 shard_map.93
  (2 shorter events, 0.0 us)
Async XLA Ops:
  2.5 39.9 %collective-permute-start = (bf16[128,2304]{1,0:T(8,128)(2,1)S(1)}, bf16[128,2304]{1,0:T(8,128)(2,1)S(1)}, u32[]{:S(2)}, u32[]{:S(2)}) collective-permute-start(bf16[128,2304]{1,0:T(8,128)(2,1)S(1)} %get-tuple-element.23), channel_id=1, source_target_pairs={{192,0},{128,64},{193,1},{129,65},{194,2},{130,66},{195,3},{131,67... | collective-permute-start | bytes 1769480 | tf_op jit(solution)/shard_map/ppermute | solution.py:554
  3.8 30.3 %all-to-all-start = ((bf16[128,8,128]{2,1,0:T(8,128)(2,1)}), bf16[128,8,128]{2,1,0:T(8,128)(2,1)S(1)}, u32[]{:S(2)}, u32[]{:S(2)}) async-start(bf16[128,8,128]{2,1,0:T(8,128)(2,1)} %bitcast.15), calls=%async_computation | async-start | bytes 524288 | tf_op jit(solution)/shard_map/all_to_all | solution.py:546
  19.9 22.5 %collective-permute-start.1 = (bf16[128,2304]{1,0:T(8,128)(2,1)S(1)}, bf16[128,2304]{1,0:T(8,128)(2,1)S(1)}, u32[]{:S(2)}, u32[]{:S(2)}) collective-permute-start(bf16[128,2304]{1,0:T(8,128)(2,1)S(1)} %get-tuple-element.24), channel_id=1, source_target_pairs={{192,0},{128,64},{193,1},{129,65},{194,2},{130,66},{195,3},{131,67... | collective-permute-start | bytes 1769480 | tf_op jit(solution)/shard_map/ppermute | solution.py:554
  21.2 12.9 %copy-start = (s32[3,32]{1,0:T(4,128)S(1)}, s32[3,32]{1,0:T(4,128)}, u32[]{:S(2)}) copy-start(s32[3,32]{1,0:T(4,128)} %parents_ref.5) | copy-start | bytes 1156
  35.8 23.0 %all-to-all-start.1 = ((bf16[128,3,4,128]{3,2,1,0:T(4,128)(2,1)}), bf16[128,3,4,128]{3,2,1,0:T(4,128)(2,1)S(1)}, u32[]{:S(2)}, u32[]{:S(2)}) async-start(bf16[128,3,4,128]{3,2,1,0:T(4,128)(2,1)} %bitcast.4), calls=%async_computation.1 | async-start | bytes 786432 | tf_op jit(solution)/shard_map/all_to_all | solution.py:546
  42.4 0.7 copy-start.1
  64.7 18.0 %collective-permute-start.2 = (bf16[128,2560]{1,0:T(8,128)(2,1)}, bf16[128,2560]{1,0:T(8,128)(2,1)S(1)}, u32[]{:S(2)}, u32[]{:S(2)}) collective-permute-start(bf16[128,2560]{1,0:T(8,128)(2,1)} %get-tuple-element.32), channel_id=1, source_target_pairs={{0,192},{64,128},{1,193},{65,129},{2,194},{66,130},{3,195},{67,131... | collective-permute-start | bytes 1966088 | tf_op jit(solution)/shard_map/ppermute | solution.py:562
  67.4 22.0 %all-to-all-start.2 = ((bf16[128,3,4,128]{3,2,1,0:T(4,128)(2,1)}), bf16[128,3,4,128]{3,2,1,0:T(4,128)(2,1)S(1)}, u32[]{:S(2)}, u32[]{:S(2)}) async-start(bf16[128,3,4,128]{3,2,1,0:T(4,128)(2,1)} %bitcast.14), calls=%async_computation.2 | async-start | bytes 786432 | tf_op jit(solution)/shard_map/all_to_all | solution.py:546
  91.0 19.9 %all-to-all-start.3 = ((bf16[128,8,128]{2,1,0:T(8,128)(2,1)}), bf16[128,8,128]{2,1,0:T(8,128)(2,1)S(1)}, u32[]{:S(2)}, u32[]{:S(2)}) async-start(bf16[128,8,128]{2,1,0:T(8,128)(2,1)} %bitcast.8), calls=%async_computation.3 | async-start | bytes 524288 | tf_op jit(solution)/shard_map/all_to_all | solution.py:546

commit v7 on v6

--- a/solution.py
+++ b/solution.py
@@ -226,10 +226,10 @@
     probs = weights * (1.0 / jnp.sum(weights, axis=0, keepdims=True))
     grad_probs = dot_last(values, grad)
     correction = jnp.sum(probs * grad_probs, axis=0, keepdims=True)
-    grad_scores = (probs * ((grad_probs - correction) * FACTOR)).astype(jnp.bfloat16)
+    grad_scores = (probs * (grad_probs - correction)).astype(jnp.bfloat16)
     value_sum = dot(probs.astype(jnp.bfloat16), grad)
-    key_sum = dot(grad_scores, query)
-    turned = dot(keys.T, grad_scores).astype(jnp.bfloat16)
+    key_sum = dot(grad_scores, query) * FACTOR
+    turned = (dot(keys.T, grad_scores) * FACTOR).astype(jnp.bfloat16)
     for i in range(REPEAT):
         store(i, turned[:, i * ROWS : (i + 1) * ROWS].T)
     return key_sum, value_sum
@@ -429,8 +429,10 @@
         own, other = setting(1), setting(2)
         work_on(1, (4, 0), other, own)
         send(1, (4, 0))
-        work_on(1, (1, 2, 3), own, own, own)
-        send(1, (1, 2, 3))
+        work_on(1, (1, 2), own, own)
+        send(1, (1, 2))
+        work_on(1, (3,), own)
+        send(1, (3,))
 
     terms_low[...] = sums[0 : ROWS * PIECE].astype(jnp.bfloat16)
     terms_out = pltpu.make_async_copy(terms_low, terms_ref, own_sems.at[0])

time: 112 us -> 112 us (level)
  no operation moved by 1% of the time
where the time goes in v7:
time: 112 us; the launch traced here: 111 us
  waiting for transfers between devices  46.7 us (42%)
  starting transfers between devices  41.2 us (37%)
  Pallas kernels  22.1 us (20%)
    all_to_all x4, waiting for transfers between devices, exchange(): lax.all_to_all(pieces.reshape(DEVICES, *tile, HD), ('depth', 'seg'), 0, 0...  37.8 us
    all_to_all x4, starting transfers between devices, exchange(): lax.all_to_all(pieces.reshape(DEVICES, *tile, HD), ('depth', 'seg'), 0, 0...  36 us
    ppermute x1, waiting for transfers between devices, per_device(): back = lax.ppermute(back, 'depth', list(HOST.items()))  8.81 us
    pallas_call x1, Pallas kernels, root_grad(): call(root_kernel, shapes, specs, outs, scratch, flops=10 ** 9, moved=6 *...  6.58 us
    pallas_call x1, Pallas kernels, attention(): call(attention_kernel, shapes, specs, outs, scratch, flops=3 * 10 ** 9, m...  5.8 us
    pallas_call x1, Pallas kernels, join(): call(join_kernel, shapes, specs, outs, grid=(HEADS,), moved=6 * 2 ** 20)  3.74 us
    ppermute x1, starting transfers between devices, per_device(): back = lax.ppermute(back, 'depth', list(HOST.items()))  2.65 us
    ppermute x2, starting transfers between devices, per_device(): lax.ppermute(each, 'depth', [(host, here) for here, host in HOST.items()])  2.58 us
  transfers between devices with their start and end apart: 7, of which 5 were waited for; matrix products, arithmetic and copies ran while one was open for 0% of the time, Pallas kernels for 11%

profile of v7, /device:TPU:32, one launch (start us, length us, event | category | flops | bytes accessed | tf_op | source)
XLA Modules:
  0.0 111.5 jit_solution(14794536679080270059)
XLA Ops:
  0.6 1.9 %shard_map.85 = (bf16[1024,128]{1,0:T(8,128)(2,1)}, bf16[128,2304]{1,0:T(8,128)(2,1)S(1)}, bf16[128,2304]{1,0:T(8,128)(2,1)S(1)}) custom-call(bf16[128,4096]{1,0:T(8,128)(2,1)} %query_ref.5, bf16[128,4096]{1,0:T(8,128)(2,1)} %grad_ref.5, bf16[128,512]{1,0:T(8,128)(2,1)} %key_ref.3, bf16[128,512]{1,0:T(8,128)(2,1)} %value_ref.3), custom_call_target="tpu_custom_call" | custom-call | tf_op jit(solution)/shard_map/pallas_call | solution.py:118
  2.5 1.3 %collective-permute-start = (bf16[128,2304]{1,0:T(8,128)(2,1)S(1)}, bf16[128,2304]{1,0:T(8,128)(2,1)S(1)}, u32[]{:S(2)}, u32[]{:S(2)}) collective-permute-start(bf16[128,2304]{1,0:T(8,128)(2,1)S(1)} %get-tuple-element.23), channel_id=1, source_target_pairs={{192,0},{128,64},{193,1},{129,65},{194,2},{130,66},{195,3},{131,67... | collective-permute-start | bytes 1769480 | tf_op jit(solution)/shard_map/ppermute | solution.py:556
  3.8 16.1 %all-to-all-start = ((bf16[128,8,128]{2,1,0:T(8,128)(2,1)}), bf16[128,8,128]{2,1,0:T(8,128)(2,1)S(1)}, u32[]{:S(2)}, u32[]{:S(2)}) async-start(bf16[128,8,128]{2,1,0:T(8,128)(2,1)} %bitcast.15), calls=%async_computation | async-start | bytes 524288 | tf_op jit(solution)/shard_map/all_to_all | solution.py:548
  19.9 1.3 %collective-permute-start.1 = (bf16[128,2304]{1,0:T(8,128)(2,1)S(1)}, bf16[128,2304]{1,0:T(8,128)(2,1)S(1)}, u32[]{:S(2)}, u32[]{:S(2)}) collective-permute-start(bf16[128,2304]{1,0:T(8,128)(2,1)S(1)} %get-tuple-element.24), channel_id=1, source_target_pairs={{192,0},{128,64},{193,1},{129,65},{194,2},{130,66},{195,3},{131,67... | collective-permute-start | bytes 1769480 | tf_op jit(solution)/shard_map/ppermute | solution.py:556
  21.2 0.0 copy-start
  21.2 0.1 pad_add_fusion.place_ref
  21.3 12.8 %all-to-all-done = bf16[128,8,128]{2,1,0:T(8,128)(2,1)S(1)} async-done(((bf16[128,8,128]{2,1,0:T(8,128)(2,1)}), bf16[128,8,128]{2,1,0:T(8,128)(2,1)S(1)}, u32[]{:S(2)}, u32[]{:S(2)}) %all-to-all-start) | async-done | bytes 262176 | tf_op jit(solution)/shard_map/all_to_all | solution.py:548
  34.2 0.0 copy-done
  34.2 1.6 %shard_map.87.picked_ref = bf16[1536,128]{1,0:T(8,128)(2,1)} custom-call(s32[3,32]{1,0:T(4,128)S(1)} %copy-done, bf16[1024,128]{1,0:T(8,128)(2,1)S(1)} %bitcast.12), custom_call_target="tpu_custom_call" | custom-call | tf_op jit(solution)/shard_map/pallas_call | solution.py:163
  35.8 6.6 %all-to-all-start.1 = ((bf16[128,3,4,128]{3,2,1,0:T(4,128)(2,1)}), bf16[128,3,4,128]{3,2,1,0:T(4,128)(2,1)S(1)}, u32[]{:S(2)}, u32[]{:S(2)}) async-start(bf16[128,3,4,128]{3,2,1,0:T(4,128)(2,1)} %bitcast.4), calls=%async_computation.1 | async-start | bytes 786432 | tf_op jit(solution)/shard_map/all_to_all | solution.py:548
  42.4 0.0 copy-start.1
  42.4 0.0 collective-permute-done.after_ref.first_ref
  42.4 0.0 collective-permute-done.1.second_ref
  42.4 0.6 copy-done.1
  43.1 6.6 %shard_map.88 = (bf16[128,4096]{1,0:T(8,128)(2,1)}, f32[128,512]{1,0:T(8,128)}, f32[128,512]{1,0:T(8,128)}, bf16[2,128,1024]{2,1,0:T(8,128)(2,1)S(1)}, bf16[2,12...) custom-call(s32[2]{0:T(128)S(1)} %pad_add_fusion.place_ref, ...), custom_call_target="tpu_custom_call" | custom-call | flops 1000000000 | bytes 6291456 | tf_op jit(solution)/shard_map/pallas_call | solution.py:325
  49.7 9.1 %all-to-all-done.1 = bf16[128,3,4,128]{3,2,1,0:T(4,128)(2,1)S(1)} async-done(((bf16[128,3,4,128]{3,2,1,0:T(4,128)(2,1)}), bf16[128,3,4,128]{3,2,1,0:T(4,128)(2,1)S(1)}, u32[]{:S(2)}, u32[]{:S(2)}) %all-to-all-start.1) | async-done | bytes 393248 | tf_op jit(solution)/shard_map/all_to_all | solution.py:548
  58.7 5.8 %shard_map.89 = (bf16[128,4096]{1,0:T(8,128)(2,1)}, f32[128,512]{1,0:T(8,128)}, f32[128,512]{1,0:T(8,128)}, bf16[128,2560]{1,0:T(8,128)(2,1)}, bf16[1536,128]{1,0:T(8,128)(2,1)}) custom-call(s32[2]{0:T(128)S(1)} %pad_add_fusion.place_ref, s32[3,32]{1,0:T(4,128)S(1)} %copy-done, s32[4,32]{1,0:T(4,128)S(1)} %copy-done.1, bf16[128,4096]{1,0:T(8,128)(2,1)} %query_ref.5, ...), custom_call_target="tpu_custom_call" | custom-call | flops 3000000000 | bytes 10485760 | tf_op jit(solution)/shard_map/pallas_call | solution.py:486
  64.5 2.7 %collective-permute-start.2 = (bf16[128,2560]{1,0:T(8,128)(2,1)}, bf16[128,2560]{1,0:T(8,128)(2,1)S(1)}, u32[]{:S(2)}, u32[]{:S(2)}) collective-permute-start(bf16[128,2560]{1,0:T(8,128)(2,1)} %get-tuple-element.32), channel_id=1, source_target_pairs={{0,192},{64,128},{1,193},{65,129},{2,194},{66,130},{3,195},{67,131... | collective-permute-start | bytes 1966088 | tf_op jit(solution)/shard_map/ppermute | solution.py:564
  67.2 6.6 %all-to-all-start.2 = ((bf16[128,3,4,128]{3,2,1,0:T(4,128)(2,1)}), bf16[128,3,4,128]{3,2,1,0:T(4,128)(2,1)S(1)}, u32[]{:S(2)}, u32[]{:S(2)}) async-start(bf16[128,3,4,128]{3,2,1,0:T(4,128)(2,1)} %bitcast.14), calls=%async_computation.2 | async-start | bytes 786432 | tf_op jit(solution)/shard_map/all_to_all | solution.py:548
  73.8 8.8 %collective-permute-done.2.back_ref.back_key_ref.back_value_ref.after_ref = bf16[128,2560]{1,0:T(8,128)(2,1)S(1)} collective-permute-done((bf16[128,2560]{1,0:T(8,128)(2,1)}, bf16[128,2560]{1,0:T(8,128)(2,1)S(1)}, u32[]{:S(2)}, u32[]{:S(2)}) %collective-permute-start.2) | collective-permute-done | bytes 655392 | tf_op jit(solution)/shard_map/ppermute | solution.py:564
  82.7 6.5 %all-to-all-done.2 = bf16[128,3,4,128]{3,2,1,0:T(4,128)(2,1)S(1)} async-done(((bf16[128,3,4,128]{3,2,1,0:T(4,128)(2,1)}), bf16[128,3,4,128]{3,2,1,0:T(4,128)(2,1)S(1)}, u32[]{:S(2)}, u32[]{:S(2)}) %all-to-all-start.2) | async-done | bytes 393248 | tf_op jit(solution)/shard_map/all_to_all | solution.py:548
  89.1 1.6 %shard_map.92 = bf16[1024,128]{1,0:T(8,128)(2,1)} custom-call(s32[3,32]{1,0:T(4,128)S(1)} %copy-done, bf16[1536,128]{1,0:T(8,128)(2,1)S(1)} %bitcast.10, f32[8,128]{1,0:T(8,128)S(1)} %shard_map.91.after_ref), custom_call_target="tpu_custom_call" | custom-call | tf_op jit(solution)/shard_map/pallas_call | solution.py:198
  90.8 6.6 %all-to-all-start.3 = ((bf16[128,8,128]{2,1,0:T(8,128)(2,1)}), bf16[128,8,128]{2,1,0:T(8,128)(2,1)S(1)}, u32[]{:S(2)}, u32[]{:S(2)}) async-start(bf16[128,8,128]{2,1,0:T(8,128)(2,1)} %bitcast.8), calls=%async_computation.3 | async-start | bytes 524288 | tf_op jit(solution)/shard_map/all_to_all | solution.py:548
  97.4 3.7 %shard_map.90 = (bf16[128,4096]{1,0:T(8,128)(2,1)}, f32[128,512]{1,0:T(8,128)S(1)}, f32[128,512]{1,0:T(8,128)S(1)}) custom-call(s32[2]{0:T(128)S(1)} %pad_add_fusion.place_ref, bf16[128,4096]{1,0:T(8,128)(2,1)} %get-tuple-element.26.root_ref, bf16[128,4096]{1,0:T(8,128)(2,1)} %get-tuple-element.31.here_ref, ...), custom_call_target="tpu_custom_call" | custom-call | bytes 6291456 | tf_op jit(solution)/shard_map/pallas_call | solution.py:527
  101.1 9.5 %all-to-all-done.3 = bf16[128,8,128]{2,1,0:T(8,128)(2,1)S(1)} async-done(((bf16[128,8,128]{2,1,0:T(8,128)(2,1)}), bf16[128,8,128]{2,1,0:T(8,128)(2,1)S(1)}, u32[]{:S(2)}, u32[]{:S(2)}) %all-to-all-start.3) | async-done | bytes 262176 | tf_op jit(solution)/shard_map/all_to_all | solution.py:548
  110.6 0.9 shard_map.93
  (2 shorter events, 0.0 us)
Async XLA Ops:
  2.5 39.9 %collective-permute-start = (bf16[128,2304]{1,0:T(8,128)(2,1)S(1)}, bf16[128,2304]{1,0:T(8,128)(2,1)S(1)}, u32[]{:S(2)}, u32[]{:S(2)}) collective-permute-start(bf16[128,2304]{1,0:T(8,128)(2,1)S(1)} %get-tuple-element.23), channel_id=1, source_target_pairs={{192,0},{128,64},{193,1},{129,65},{194,2},{130,66},{195,3},{131,67... | collective-permute-start | bytes 1769480 | tf_op jit(solution)/shard_map/ppermute | solution.py:556
  3.8 30.3 %all-to-all-start = ((bf16[128,8,128]{2,1,0:T(8,128)(2,1)}), bf16[128,8,128]{2,1,0:T(8,128)(2,1)S(1)}, u32[]{:S(2)}, u32[]{:S(2)}) async-start(bf16[128,8,128]{2,1,0:T(8,128)(2,1)} %bitcast.15), calls=%async_computation | async-start | bytes 524288 | tf_op jit(solution)/shard_map/all_to_all | solution.py:548
  19.9 22.5 %collective-permute-start.1 = (bf16[128,2304]{1,0:T(8,128)(2,1)S(1)}, bf16[128,2304]{1,0:T(8,128)(2,1)S(1)}, u32[]{:S(2)}, u32[]{:S(2)}) collective-permute-start(bf16[128,2304]{1,0:T(8,128)(2,1)S(1)} %get-tuple-element.24), channel_id=1, source_target_pairs={{192,0},{128,64},{193,1},{129,65},{194,2},{130,66},{195,3},{131,67... | collective-permute-start | bytes 1769480 | tf_op jit(solution)/shard_map/ppermute | solution.py:556
  21.2 12.9 %copy-start = (s32[3,32]{1,0:T(4,128)S(1)}, s32[3,32]{1,0:T(4,128)}, u32[]{:S(2)}) copy-start(s32[3,32]{1,0:T(4,128)} %parents_ref.5) | copy-start | bytes 1156
  35.8 23.0 %all-to-all-start.1 = ((bf16[128,3,4,128]{3,2,1,0:T(4,128)(2,1)}), bf16[128,3,4,128]{3,2,1,0:T(4,128)(2,1)S(1)}, u32[]{:S(2)}, u32[]{:S(2)}) async-start(bf16[128,3,4,128]{3,2,1,0:T(4,128)(2,1)} %bitcast.4), calls=%async_computation.1 | async-start | bytes 786432 | tf_op jit(solution)/shard_map/all_to_all | solution.py:548
  42.4 0.7 copy-start.1
  64.5 18.1 %collective-permute-start.2 = (bf16[128,2560]{1,0:T(8,128)(2,1)}, bf16[128,2560]{1,0:T(8,128)(2,1)S(1)}, u32[]{:S(2)}, u32[]{:S(2)}) collective-permute-start(bf16[128,2560]{1,0:T(8,128)(2,1)} %get-tuple-element.32), channel_id=1, source_target_pairs={{0,192},{64,128},{1,193},{65,129},{2,194},{66,130},{3,195},{67,131... | collective-permute-start | bytes 1966088 | tf_op jit(solution)/shard_map/ppermute | solution.py:564
  67.2 21.9 %all-to-all-start.2 = ((bf16[128,3,4,128]{3,2,1,0:T(4,128)(2,1)}), bf16[128,3,4,128]{3,2,1,0:T(4,128)(2,1)S(1)}, u32[]{:S(2)}, u32[]{:S(2)}) async-start(bf16[128,3,4,128]{3,2,1,0:T(4,128)(2,1)} %bitcast.14), calls=%async_computation.2 | async-start | bytes 786432 | tf_op jit(solution)/shard_map/all_to_all | solution.py:548
  90.8 19.9 %all-to-all-start.3 = ((bf16[128,8,128]{2,1,0:T(8,128)(2,1)}), bf16[128,8,128]{2,1,0:T(8,128)(2,1)S(1)}, u32[]{:S(2)}, u32[]{:S(2)}) async-start(bf16[128,8,128]{2,1,0:T(8,128)(2,1)} %bitcast.8), calls=%async_computation.3 | async-start | bytes 524288 | tf_op jit(solution)/shard_map/all_to_all | solution.py:548
